TPU v7x, 32 devices: a whole 2x2x4 slice. The times are simulated.
32 devices in a mesh: dp: 4 (over z), ctx: 8 (over y, x, core).
Axes of the slice: x: 2, y: 2, z: 4, core: 2. Of those that a mesh axis runs over, the one named last changes fastest.
Arguments:
- patches: bfloat16 [8192, 1280], P(('dp', 'ctx')), may hold values from -6 to 6
- unit_counts: int32 [8, 4], P('ctx'), may hold values from 1 to 8, 16 in all within a row
- segment_ids: int32 [4096], P(('dp', 'ctx')), may hold values from 0 to 7, as said below
- merged_position: int32 [1024], P(('dp', 'ctx')), may hold values from 0 to 511, as said below
- ln_gain: float32 [1280], replicated, may hold values from 0.5 to 1.5
- ln_bias: float32 [1280], replicated, may hold values from -3 to 3
- qkv_weight: bfloat16 [1280, 2880], replicated, may hold values from -1 to 1
- out_weight: bfloat16 [960, 1280], replicated, may hold values from -0.1875 to 0.1875
- merge_gain: float32 [1280], replicated, may hold values from 0.5 to 1.5
- merge_bias: float32 [1280], replicated, may hold values from -3 to 3
- merged_grad: bfloat16 [2048, 5120], P(('dp', 'ctx')), may hold values from -6 to 6
Outputs:
- merged: bfloat16 [2048, 5120], P(('dp', 'ctx'))
- patch_grad: bfloat16 [8192, 1280], P(('dp', 'ctx'))
- norm_grads: float32 [4, 1280], replicated
Inputs may be any that keep to these rules, and one draw needn't show every extreme that they name: Each row of unit_counts sums to 16; the largest entry of a row is exactly 8. `segment_ids`: constant over each aligned run of 4 rows; 0 at the first row of every block of 32 rows and never falling within a block. `merged_position`: the tokens of device (d, c) have positions in c * 64 to c * 64 + 63, strictly rising along the device's tokens and rising by one within an image.
All inputs are finite; a program needn't handle non-finite values.
Results may differ from a plain program's by a relative error of at most 0.0068.
Values may be sent and summed in bfloat16 or wider, within the bound.
No kernel may reach another device: no remote copies, remote signals or barrier semaphores. Data moves between devices by JAX's collectives and lax.ppermute only.
A program may use at most 64 MiB of HBM per device.

v0:
```python
import jax
import jax.numpy as jnp
from jax import lax
from jax.sharding import PartitionSpec as P

HEAD = 80
UNIT = 32


EPS = 1e-06
NEG = -1e30


def norm_parts(values, scale_gain, shift_bias):
    average = jnp.mean(values, axis=-1, keepdims=True)
    centred = values - average
    inverse = lax.rsqrt(jnp.mean(centred * centred, axis=-1, keepdims=True) + EPS)
    normed = centred * inverse
    return (normed, inverse, normed * scale_gain + shift_bias)


def norm_back(upstream, normed, inverse, scale_gain):
    scaled = upstream * scale_gain
    centre = jnp.mean(scaled, axis=-1, keepdims=True)
    slope = jnp.mean(scaled * normed, axis=-1, keepdims=True)
    return inverse * (scaled - centre - normed * slope)


def image_mask(labels):
    length = labels.shape[-1]
    block_of = jnp.arange(length, dtype=jnp.int32) // UNIT
    joined = labels + block_of * UNIT
    return joined[..., :, None] == joined[..., None, :]


def lookup(table, index):
    entries = jnp.arange(table.shape[0], dtype=jnp.int32)
    chosen = jnp.expand_dims(index, -1) == entries
    return jnp.sum(jnp.where(chosen, table, 0), axis=-1)


def block_forward(rows, labels, ln_gain, ln_bias, qkv_weight, out_weight, merge_gain, merge_bias):
    batch, length, width = rows.shape
    inner = out_weight.shape[0]
    heads = inner // HEAD
    scale = HEAD ** (-0.5)
    flat = rows.reshape(batch * length, width).astype(jnp.float32)
    normed_in, inverse_in, shifted = norm_parts(flat, ln_gain, ln_bias)
    qkv = jnp.dot(
        shifted.astype(jnp.bfloat16), qkv_weight, preferred_element_type=jnp.float32
    ).astype(jnp.bfloat16)
    split = qkv.reshape(batch, length, 3, heads, HEAD)
    queries = split[:, :, 0]
    key_heads = split[:, :, 1]
    value_heads = split[:, :, 2]
    scores = (
        jnp.einsum("nqhe,nkhe->nhqk", queries, key_heads, preferred_element_type=jnp.float32)
        * scale
    )
    scores = jnp.where(image_mask(labels)[:, None], scores, NEG)
    peak = jnp.max(scores, axis=-1, keepdims=True)
    raised = jnp.exp(scores - peak)
    attention = raised / jnp.sum(raised, axis=-1, keepdims=True)
    attention_half = attention.astype(jnp.bfloat16)
    attended = jnp.einsum(
        "nhqk,nkhe->nqhe", attention_half, value_heads, preferred_element_type=jnp.float32
    ).astype(jnp.bfloat16)
    hidden = flat + jnp.dot(
        attended.reshape(batch * length, inner), out_weight, preferred_element_type=jnp.float32
    )
    normed_out, inverse_out, result = norm_parts(hidden, merge_gain, merge_bias)
    saved = (
        normed_in,
        inverse_in,
        queries,
        key_heads,
        value_heads,
        attention,
        attention_half,
        normed_out,
        inverse_out,
    )
    return (result.astype(jnp.bfloat16), saved)


def block_backward(upstream, saved, ln_gain, qkv_weight, out_weight, merge_gain):
    (
        normed_in,
        inverse_in,
        queries,
        key_heads,
        value_heads,
        attention,
        attention_half,
        normed_out,
        inverse_out,
    ) = saved
    batch = queries.shape[0]
    length = queries.shape[1]
    heads = queries.shape[2]
    inner = out_weight.shape[0]
    scale = HEAD ** (-0.5)
    transposed = (((1,), (1,)), ((), ()))
    merge_scale = jnp.sum(upstream * normed_out, axis=0)
    merge_shift = jnp.sum(upstream, axis=0)
    hidden_grad = norm_back(upstream, normed_out, inverse_out, merge_gain)
    attended_grad = lax.dot_general(
        hidden_grad.astype(jnp.bfloat16), out_weight, transposed, preferred_element_type=jnp.float32
    ).astype(jnp.bfloat16)
    attended_grad = attended_grad.reshape(batch, length, heads, HEAD)
    softmax_grad = jnp.einsum(
        "nqhe,nkhe->nhqk", attended_grad, value_heads, preferred_element_type=jnp.float32
    )
    value_grad = jnp.einsum(
        "nhqk,nqhe->nkhe", attention_half, attended_grad, preferred_element_type=jnp.float32
    )
    centred = softmax_grad - jnp.sum(attention * softmax_grad, axis=-1, keepdims=True)
    score_grad = (attention * centred * scale).astype(jnp.bfloat16)
    query_grad = jnp.einsum(
        "nhqk,nkhe->nqhe", score_grad, key_heads, preferred_element_type=jnp.float32
    )
    key_grad = jnp.einsum(
        "nhqk,nqhe->nkhe", score_grad, queries, preferred_element_type=jnp.float32
    )
    qkv_grad = jnp.stack([query_grad, key_grad, value_grad], axis=2).astype(jnp.bfloat16)
    qkv_grad = qkv_grad.reshape(batch * length, 3 * inner)
    input_grad = lax.dot_general(
        qkv_grad, qkv_weight, transposed, preferred_element_type=jnp.float32
    )
    norm_terms = jnp.stack(
        [
            jnp.sum(input_grad * normed_in, axis=0),
            jnp.sum(input_grad, axis=0),
            merge_scale,
            merge_shift,
        ]
    )
    row_grad = (hidden_grad + norm_back(input_grad, normed_in, inverse_in, ln_gain)).astype(
        jnp.bfloat16
    )
    return (row_grad, norm_terms)


def per_device(
    patches,
    unit_counts,
    segment_ids,
    merged_position,
    ln_gain,
    ln_bias,
    qkv_weight,
    out_weight,
    merge_gain,
    merge_bias,
    merged_grad,
):
    data_ranks = lax.axis_size("dp")
    owner_count = lax.axis_size("ctx")
    data_rank = lax.axis_index("dp")
    column_index = lax.axis_index("ctx")
    model_width = patches.shape[1]
    source_units = patches.shape[0] // UNIT
    device_units = segment_ids.shape[0] // UNIT
    capacity = -(-source_units // data_ranks)
    owner_slots = merged_grad.shape[0]
    token_width = merged_grad.shape[1]
    pair_slots = owner_slots // owner_count
    zero_half = jnp.zeros((), jnp.bfloat16)
    block_counts = unit_counts[0]
    block_ends = jnp.cumsum(block_counts)
    block_starts = block_ends - block_counts
    first_block = lookup(block_starts, data_rank)
    live_blocks = lookup(block_counts, data_rank)
    returned_tokens = lax.all_to_all(
        merged_grad.reshape(owner_count, pair_slots, token_width),
        "ctx",
        split_axis=0,
        concat_axis=0,
        tiled=True,
    )
    target_rank = jnp.arange(data_ranks, dtype=jnp.int32)[:, None]
    slot_index = jnp.arange(capacity, dtype=jnp.int32)[None, :]
    picked_block = (target_rank - first_block) % data_ranks + slot_index * data_ranks
    picked_live = (picked_block < live_blocks).reshape(-1)
    source_blocks = patches.reshape(source_units, UNIT, model_width)
    outgoing = jnp.take(
        source_blocks, jnp.minimum(picked_block, source_units - 1).reshape(-1), axis=0
    )
    outgoing = jnp.where(picked_live[:, None, None], outgoing, zero_half)
    arrived = lax.all_to_all(
        outgoing.reshape(data_ranks, capacity, UNIT, model_width),
        "dp",
        split_axis=0,
        concat_axis=0,
        tiled=True,
    )
    wanted_block = jnp.arange(device_units, dtype=jnp.int32) * data_ranks + data_rank
    sender_rank = jnp.sum((block_ends[None, :] <= wanted_block[:, None]).astype(jnp.int32), axis=1)
    sender_block = wanted_block - lookup(block_starts, sender_rank)
    arrived_slot = sender_rank * capacity + sender_block // data_ranks
    balanced = jnp.take(
        arrived.reshape(data_ranks * capacity, UNIT, model_width), arrived_slot, axis=0
    )
    balanced = balanced.reshape(1, device_units * UNIT, model_width)
    labels = segment_ids.reshape(1, device_units * UNIT)
    result, saved = block_forward(
        balanced, labels, ln_gain, ln_bias, qkv_weight, out_weight, merge_gain, merge_bias
    )
    tokens = result.reshape(-1, token_width)
    window_place = merged_position - column_index * owner_slots
    placer = (jnp.arange(owner_slots, dtype=jnp.int32)[:, None] == window_place[None, :]).astype(
        jnp.bfloat16
    )
    window = jnp.dot(placer, tokens, preferred_element_type=jnp.float32).astype(jnp.bfloat16)
    window_out = window.reshape(pair_slots, owner_count, token_width).transpose(1, 0, 2)
    merged = lax.all_to_all(window_out, "ctx", split_axis=0, concat_axis=0, tiled=True)
    window_grad = returned_tokens.transpose(1, 0, 2).reshape(owner_slots, token_width)
    token_grad = lax.dot_general(
        placer, window_grad, (((0,), (0,)), ((), ())), preferred_element_type=jnp.float32
    )
    upstream = token_grad.reshape(-1, model_width)
    row_grad, norm_terms = block_backward(
        upstream, saved, ln_gain, qkv_weight, out_weight, merge_gain
    )
    row_units = row_grad.reshape(device_units, UNIT, model_width)
    slot_block = (data_rank - block_starts[:, None]) % data_ranks + slot_index * data_ranks
    slot_live = (slot_block < block_counts[:, None]).reshape(-1)
    slot_unit = jnp.minimum((block_starts[:, None] + slot_block) // data_ranks, device_units - 1)
    backward_rows = jnp.take(row_units, slot_unit.reshape(-1), axis=0)
    backward_rows = jnp.where(slot_live[:, None, None], backward_rows, zero_half)
    came_back = lax.all_to_all(
        backward_rows.reshape(data_ranks, capacity, UNIT, model_width),
        "dp",
        split_axis=0,
        concat_axis=0,
        tiled=True,
    )
    local_block = jnp.arange(source_units, dtype=jnp.int32)
    from_rank = (first_block + local_block) % data_ranks
    from_slot = jnp.minimum(
        from_rank * capacity + local_block // data_ranks, data_ranks * capacity - 1
    )
    patch_grad = jnp.take(
        came_back.reshape(data_ranks * capacity, UNIT, model_width), from_slot, axis=0
    )
    patch_grad = jnp.where((local_block < live_blocks)[:, None, None], patch_grad, zero_half)
    norm_grads = lax.psum(norm_terms, ("dp", "ctx"))
    return (
        merged.reshape(owner_slots, token_width),
        patch_grad.reshape(source_units * UNIT, model_width),
        norm_grads,
    )


def solution(mesh):
    return jax.shard_map(
        per_device,
        mesh=mesh,
        in_specs=(
            P(("dp", "ctx"), None),
            P("ctx", None),
            P(("dp", "ctx")),
            P(("dp", "ctx")),
            P(),
            P(),
            P(),
            P(),
            P(),
            P(),
            P(("dp", "ctx"), None),
        ),
        out_specs=(P(("dp", "ctx"), None), P(("dp", "ctx"), None), P()),
        check_vma=False,
    )
```

profile of v0, /device:TPU:0, one launch (start us, length us, event | category | flops | bytes accessed | tf_op | source)
XLA Modules:
  0.0 141.1 jit_solution(16169771677792506338)
XLA Ops:
  0.7 5.3 %all-to-all-start.2 = ((bf16[8,8,5120]{2,1,0:T(8,128)(2,1)}), bf16[8,8,5120]{2,1,0:T(8,128)(2,1)S(1)}, u32[]{:S(2)}, u32[]{:S(2)}) async-start(bf16[8,8,5120]{2,1,0:T(8,128)(2,1)} %bitcast.116), calls=%async_computation.2 | async-start | bytes 1310720 | tf_op jit(solution)/shard_map/all_to_all | solution.py:174
  6.0 0.8 reduce-window.7
  6.8 1.4 and_select_fusion.3
  8.2 0.6 fusion.56
  9.2 0.6 and_select_fusion.6
  10.0 0.7 fusion.53
  10.6 2.0 %add_compare_fusion = (pred[4,2]{1,0:T(4,128)(4,1)}, pred[4,2]{1,0:T(4,128)(4,1)}, pred[4,2]{1,0:T(4,128)(4,1)S(1)}) fusion(s32[4]{0:T(128)} %bitcast.120, s32[4]{0:T(128)S(1)} %get-tuple-element.12, s32[2]{0:T(128)S(1)} %iota_multiply_fusion, s32[4]{0:T(128)S(1)} %get-tuple-element.13, s32[]{:T(128)} %get-tuple-element.21, s32[4]{0:T(128)S(1)} %and_select_fusion.6), kind=kLoop, calls=%fused_computation.98 | loop fusion | flops 216 | bytes 100 | tf_op jit(solution)/shard_map/lt | solution.py:227
  12.7 2.5 %gather_fusion.2 = bf16[8,32,1280]{2,1,0:T(8,128)(2,1)} fusion(bf16[8,32,1280]{2,1,0:T(8,128)(2,1)} %bitcast.115, s32[1024]{0:T(1024)S(1)} %pad_clamp_fusion.3), kind=kCustom, calls=%fused_computation.clone | custom fusion | bytes 1310752 | tf_op jit(solution)/shard_map/jit(_take)/gather | solution.py:186
  15.2 2.1 %select_select_fusion.1 = bf16[8,32,1280]{2,1,0:T(8,128)(2,1)} fusion(bf16[8,32,1280]{2,1,0:T(8,128)(2,1)} %gather_fusion.2, pred[8]{0:T(512)(128)(4,1)S(1)} %compare_and_fusion.1, pred[8]{0:T(512)(128)(4,1)S(1)} %lt.89), kind=kLoop, calls=%fused_computation.52 | loop fusion | flops 655360 | bytes 1310736 | tf_op jit(solution)/shard_map/jit(_where)/select_n | solution.py:189
  17.3 4.9 %all-to-all-start = ((bf16[4,2,32,1280]{3,2,1,0:T(8,128)(2,1)}), bf16[4,2,32,1280]{3,2,1,0:T(8,128)(2,1)}, u32[]{:S(2)}, u32[]{:S(2)}) async-start(bf16[4,2,32,1280]{3,2,1,0:T(8,128)(2,1)} %bitcast.105), calls=%async_computation | async-start | bytes 1310720 | tf_op jit(solution)/shard_map/all_to_all | solution.py:190
  22.4 0.5 fusion.63
  23.0 1.4 fusion.33
  24.4 2.1 %reshape.595 = f32[128,1280]{1,0:T(8,128)} reshape(f32[32,5120]{1,0:T(8,128)} %fusion.33) | data formatting | bytes 1310720 | tf_op jit(solution)/shard_map/reshape | solution.py:221
  26.5 13.7 %all-to-all-done = bf16[4,2,32,1280]{3,2,1,0:T(8,128)(2,1)} async-done(((bf16[4,2,32,1280]{3,2,1,0:T(8,128)(2,1)}), bf16[4,2,32,1280]{3,2,1,0:T(8,128)(2,1)}, u32[]{:S(2)}, u32[]{:S(2)}) %all-to-all-start) | async-done | bytes 655392 | tf_op jit(solution)/shard_map/all_to_all | solution.py:190
  40.2 1.7 %gather_fusion = bf16[4,32,1280]{2,1,0:T(8,128)(2,1)S(1)} fusion(bf16[8,32,1280]{2,1,0:T(8,128)(2,1)} %bitcast.5, s32[1024]{0:T(1024)S(1)} %pad_clamp_fusion.2), kind=kCustom, calls=%fused_computation.2 | custom fusion | bytes 655376 | tf_op jit(solution)/shard_map/jit(_take)/gather | solution.py:201
  42.1 0.6 div.94
  42.7 0.2 fusion.32
  43.0 0.6 rsqrt.20
  43.7 5.4 %convolution_convert_fusion.1 = bf16[128,2880]{0,1:T(8,128)(2,1)S(1)} fusion(bf16[1280,2880]{0,1:T(8,128)(2,1)} %param.19, bf16[128,1280]{1,0:T(8,128)(2,1)S(1)} %bitcast_select_fusion, f32[1280]{0:T(1024)S(1)} %copy-done.9, f32[1280]{0:T(1024)S(1)} %copy-done.7, f32[128]{0:T(128)} %rsqrt.20, f32[128]{0:T(128)} %div.94), kind=kOutput, calls=%fused_computation.8 | convolution fusion | flops 945070080 | bytes 8449024 | tf_op jit(solution)/shard_map/dot_general | solution.py:49
  49.1 1.3 fusion.71
  50.4 0.6 copy-done.22
  51.0 1.4 %convolution_convert_fusion.5 = bf16[12,80,128]{2,1,0:T(8,128)(2,1)S(1)} fusion(bf16[1,128,3,12,80]{1,4,3,2,0:T(8,128)(2,1)S(1)} %bitcast.109, f32[12,128,128]{1,2,0:T(8,128)} %get-tuple-element.23, f32[12,128]{1,0:T(8,128)S(1)} %get-tuple-element.22), kind=kOutput, calls=%fused_computation.21 | convolution fusion | flops 31973376 | bytes 1286144 | tf_op jit(solution)/shard_map/nhqk,nkhe->nqhe/dot_general | solution.py:65
  52.5 0.6 fusion.72
  53.1 0.2 multiply_reduce_fusion.3
  53.6 0.3 multiply_reduce_fusion.1
  53.9 0.9 convolution_convert_fusion.6
  54.8 1.1 fusion.12
  55.9 2.2 %fusion.44 = f32[12,128,128]{1,2,0:T(8,128)} fusion(bf16[128,12,80]{0,2,1:T(8,128)(2,1)S(1)} %bitcast.114, bf16[1,128,3,12,80]{1,4,3,2,0:T(8,128)(2,1)} %bitcast.110), kind=kOutput, calls=%fused_computation.75 | convolution fusion | flops 31457280 | bytes 1277952 | tf_op jit(solution)/shard_map/nqhe,nkhe->nhqk/dot_general | solution.py:111
  58.1 3.0 %fusion.10 = bf16[1,128,1,12,80]{1,4,3,2,0:T(8,128)(2,1)} fusion(f32[12,128,128]{1,2,0:T(8,128)} %fusion.44, bf16[1,128,3,12,80]{1,4,3,2,0:T(8,128)(2,1)} %bitcast.111, f32[12,128,128]{1,2,0:T(8,128)} %get-tuple-element.23, f32[12,128]{1,0:T(8,128)S(1)} %copy-done.23), kind=kOutput, calls=%fused_computation.23 | convolution fusion | flops 32958080 | bytes 3653632 | tf_op jit(solution)/shard_map/nhqk,nkhe->nqhe/dot_general | solution.py:119
  61.1 3.1 %fusion.11 = bf16[1,128,1,12,80]{1,4,3,2,0:T(8,128)(2,1)} fusion(f32[12,128,128]{1,2,0:T(8,128)} %fusion.44, bf16[1,128,3,12,80]{1,4,3,2,0:T(8,128)(2,1)} %bitcast.112, f32[12,128,128]{1,2,0:T(8,128)} %get-tuple-element.23, f32[12,128]{1,0:T(8,128)S(1)} %copy-done.23), kind=kOutput, calls=%fused_computation.24 | convolution fusion | flops 32958080 | bytes 3653632 | tf_op jit(solution)/shard_map/nhqk,nqhe->nkhe/dot_general | solution.py:122
  64.3 1.3 pad_maximum_fusion
  65.6 4.6 %fusion.30 = (f32[1280]{0:T(1024)S(1)}, f32[128]{0:T(128)S(1)}, f32[128]{0:T(128)S(1)}, f32[1280]{0:T(1024)S(1)}, f32[128,1280]{1,0:T(8,128)S(1)}) fusion(bf16[128,1280]{1,0:T(8,128)(2,1)} %copy-done.3, f32[128]{0:T(128)S(1)} %copy-done.11, f32[128]{0:T(128)S(1)} %copy-done.10, f32[1280]{0:T(1024)S(1)} %copy-done.7, bf16[128,2880]{0,1:T(8,128)(2,1)S(1)} %bitcast.101, ...), kind=kOutput, calls=%fused_computation.44 | convolution fusion | flops 945353984 | bytes 9110528 | tf_op jit(solution)/shard_map/dot_general | solution.py:127
  70.3 1.4 fusion.29
  71.6 1.2 reshape.590
  72.9 0.3 fusion.2
  73.2 1.2 copy.51
  74.4 3.8 %all-to-all-start.1 = ((bf16[8,8,5120]{2,1,0:T(8,128)(2,1)}), bf16[8,8,5120]{2,1,0:T(8,128)(2,1)S(1)}, u32[]{:S(2)}, u32[]{:S(2)}) async-start(bf16[8,8,5120]{2,1,0:T(8,128)(2,1)} %bitcast.106), calls=%async_computation.1 | async-start | bytes 1310720 | tf_op jit(solution)/shard_map/all_to_all | solution.py:216
  78.3 1.4 %gather_fusion.1 = bf16[8,32,1280]{2,1,0:T(8,128)(2,1)} fusion(bf16[4,32,1280]{2,1,0:T(8,128)(2,1)S(1)} %bitcast.102, s32[1024]{0:T(1024)S(1)} %pad_clamp_fusion.1), kind=kCustom, calls=%fused_computation.3 | custom fusion | bytes 1310752 | tf_op jit(solution)/shard_map/jit(_take)/gather | solution.py:229
  79.7 2.1 %select_select_fusion.2 = bf16[4,2,32,1280]{3,2,1,0:T(8,128)(2,1)} fusion(bf16[4,2,32,1280]{3,2,1,0:T(8,128)(2,1)} %bitcast.107, pred[4,2]{1,0:T(4,128)(4,1)S(1)} %copy-done.16, pred[4,2]{1,0:T(4,128)(4,1)S(1)} %copy-done.15), kind=kLoop, calls=%fused_computation.54 | loop fusion | flops 655360 | bytes 1310736 | tf_op jit(solution)/shard_map/jit(_where)/select_n | solution.py:230
  81.8 7.6 %all-to-all-done.1 = bf16[8,8,5120]{2,1,0:T(8,128)(2,1)S(1)} async-done(((bf16[8,8,5120]{2,1,0:T(8,128)(2,1)}), bf16[8,8,5120]{2,1,0:T(8,128)(2,1)S(1)}, u32[]{:S(2)}, u32[]{:S(2)}) %all-to-all-start.1) | async-done | bytes 655392 | tf_op jit(solution)/shard_map/all_to_all | solution.py:216
  89.4 4.2 %all-to-all-start.3 = ((bf16[4,2,32,1280]{3,2,1,0:T(8,128)(2,1)}), bf16[4,2,32,1280]{3,2,1,0:T(8,128)(2,1)}, u32[]{:S(2)}, u32[]{:S(2)}) async-start(bf16[4,2,32,1280]{3,2,1,0:T(8,128)(2,1)} %select_select_fusion.2), calls=%async_computation.3 | async-start | bytes 1310720 | tf_op jit(solution)/shard_map/all_to_all | solution.py:231
  93.5 0.6 compare_and_fusion
  94.1 0.6 compare_select_fusion.1
  94.7 0.6 iota_compare_fusion.4
  95.4 40.3 %psum.7 = f32[4,1280]{1,0:T(4,128)} all-reduce(f32[4,1280]{1,0:T(4,128)S(1)} %pad_maximum_fusion.1), channel_id=1, replica_groups=mesh['dp'=4,'ctx'=8] {'dp','ctx'}, use_global_device_ids=true, to_apply=%region_20.22 | all-reduce | flops 5120 | bytes 40960 | tf_op jit(solution)/shard_map/psum | solution.py:247
  135.7 2.5 %gather_fusion.3 = bf16[8,32,1280]{2,1,0:T(8,128)(2,1)} fusion(bf16[8,32,1280]{2,1,0:T(8,128)(2,1)} %bitcast.37, s32[1024]{0:T(1024)S(1)} %pad_clamp_fusion), kind=kCustom, calls=%fused_computation.1.clone | custom fusion | bytes 1310752 | tf_op jit(solution)/shard_map/jit(_take)/gather | solution.py:243
  138.2 2.1 %select_select_fusion = bf16[8,32,1280]{2,1,0:T(8,128)(2,1)} fusion(bf16[8,32,1280]{2,1,0:T(8,128)(2,1)} %gather_fusion.3, pred[8]{0:T(512)(128)(4,1)S(1)} %compare_and_fusion, pred[8]{0:T(512)(128)(4,1)S(1)} %iota_compare_fusion.4), kind=kLoop, calls=%fused_computation.51 | loop fusion | flops 655360 | bytes 1310736 | tf_op jit(solution)/shard_map/jit(_where)/select_n | solution.py:246
  140.3 0.8 copy.53
  (83 shorter events, 1.7 us)
Async XLA Ops:
  0.6 51.9 %copy-start = (bf16[960,1280]{1,0:T(8,128)(2,1)S(1)}, bf16[960,1280]{1,0:T(8,128)(2,1)}, u32[]{:S(2)}) copy-start(bf16[960,1280]{1,0:T(8,128)(2,1)} %param.20) | copy-start | bytes 7372804
  0.6 22.3 %copy-start.20 = (s32[32]{0:T(128)S(1)}, s32[32]{0:T(128)}, u32[]{:S(2)}) copy-start(s32[32]{0:T(128)} %param.16) | copy-start | bytes 388
  0.7 16.6 %all-to-all-start.2 = ((bf16[8,8,5120]{2,1,0:T(8,128)(2,1)}), bf16[8,8,5120]{2,1,0:T(8,128)(2,1)S(1)}, u32[]{:S(2)}, u32[]{:S(2)}) async-start(bf16[8,8,5120]{2,1,0:T(8,128)(2,1)} %bitcast.116), calls=%async_computation.2 | async-start | bytes 1310720 | tf_op jit(solution)/shard_map/all_to_all | solution.py:174
  17.3 22.9 %all-to-all-start = ((bf16[4,2,32,1280]{3,2,1,0:T(8,128)(2,1)}), bf16[4,2,32,1280]{3,2,1,0:T(8,128)(2,1)}, u32[]{:S(2)}, u32[]{:S(2)}) async-start(bf16[4,2,32,1280]{3,2,1,0:T(8,128)(2,1)} %bitcast.105), calls=%async_computation | async-start | bytes 1310720 | tf_op jit(solution)/shard_map/all_to_all | solution.py:190
  22.1 21.5 %copy-start.7 = (f32[1280]{0:T(1024)S(1)}, f32[1280]{0:T(1024)}, u32[]{:S(2)}) copy-start(f32[1280]{0:T(1024)} %param.17) | copy-start | bytes 15364
  22.1 21.5 %copy-start.9 = (f32[1280]{0:T(1024)S(1)}, f32[1280]{0:T(1024)}, u32[]{:S(2)}) copy-start(f32[1280]{0:T(1024)} %param.18) | copy-start | bytes 15364
  22.3 21.2 %copy-start.17 = (pred[128]{0:T(512)(128)(4,1)}, pred[128]{0:T(512)(128)(4,1)S(1)}, u32[]{:S(2)}) copy-start(pred[128]{0:T(512)(128)(4,1)S(1)} %broadcast_in_dim.123) | copy-start | bytes 388
  22.9 20.6 %copy-start.13 = (s32[32]{0:T(128)}, s32[32]{0:T(128)S(1)}, u32[]{:S(2)}) copy-start(s32[32]{0:T(128)S(1)} %broadcast_subtract_fusion) | copy-start | bytes 388
  43.7 5.4 %copy-start.3 = (bf16[128,1280]{1,0:T(8,128)(2,1)}, bf16[128,1280]{1,0:T(8,128)(2,1)S(1)}, u32[]{:S(2)}) copy-start(bf16[128,1280]{1,0:T(8,128)(2,1)S(1)} %bitcast_select_fusion) | copy-start | bytes 983044
  49.1 3.4 %copy-start.6 = (bf16[128,2880]{0,1:T(8,128)(2,1)}, bf16[128,2880]{0,1:T(8,128)(2,1)S(1)}, u32[]{:S(2)}) copy-start(bf16[128,2880]{0,1:T(8,128)(2,1)S(1)} %convolution_convert_fusion.1) | copy-start | bytes 2211844
  50.4 0.6 copy-start.22
  50.4 2.1 %copy-start.4 = (bf16[128,1280]{1,0:T(8,128)(2,1)S(1)}, bf16[128,1280]{1,0:T(8,128)(2,1)}, u32[]{:S(2)}) copy-start(bf16[128,1280]{1,0:T(8,128)(2,1)} %copy-done.3) | copy-start | bytes 983044
  52.5 1.1 copy-start.1
  52.5 1.1 copy-start.8
  53.6 1.3 copy-start.21
  53.6 1.3 copy-start.23
  61.1 4.4 %copy-start.10 = (f32[128]{0:T(128)S(1)}, f32[128]{0:T(128)}, u32[]{:S(2)}) copy-start(f32[128]{0:T(128)} %div.94) | copy-start | bytes 1540
  61.1 4.4 %copy-start.11 = (f32[128]{0:T(128)S(1)}, f32[128]{0:T(128)}, u32[]{:S(2)}) copy-start(f32[128]{0:T(128)} %rsqrt.20) | copy-start | bytes 1540
  65.5 4.7 %copy-start.2 = (f32[128,1280]{1,0:T(8,128)S(1)}, f32[128,1280]{1,0:T(8,128)}, u32[]{:S(2)}) copy-start(f32[128,1280]{1,0:T(8,128)} %reshape.595) | copy-start | bytes 1966084
  65.5 4.7 %copy-start.12 = (f32[1280]{0:T(1024)S(1)}, f32[1280]{0:T(1024)}, u32[]{:S(2)}) copy-start(f32[1280]{0:T(1024)} %param.22) | copy-start | bytes 15364
  65.6 4.7 %copy-start.18 = (pred[128]{0:T(512)(128)(4,1)S(1)}, pred[128]{0:T(512)(128)(4,1)}, u32[]{:S(2)}) copy-start(pred[128]{0:T(512)(128)(4,1)} %copy-done.17) | copy-start | bytes 388
  70.2 2.7 %copy-start.14 = (s32[32]{0:T(128)S(1)}, s32[32]{0:T(128)}, u32[]{:S(2)}) copy-start(s32[32]{0:T(128)} %copy-done.13) | copy-start | bytes 388
  71.6 6.6 %copy-start.19 = (s32[8]{0:T(128)S(1)}, s32[8]{0:T(128)}, u32[]{:S(2)}) copy-start(s32[8]{0:T(128)} %fusion.63) | copy-start | bytes 100
  71.6 6.6 %copy-start.5 = (bf16[128,1280]{1,0:T(8,128)(2,1)S(1)}, bf16[128,1280]{1,0:T(8,128)(2,1)}, u32[]{:S(2)}) copy-start(bf16[128,1280]{1,0:T(8,128)(2,1)} %get-tuple-element.14) | copy-start | bytes 983044
  72.9 6.8 %copy-start.15 = (pred[4,2]{1,0:T(4,128)(4,1)S(1)}, pred[4,2]{1,0:T(4,128)(4,1)}, u32[]{:S(2)}) copy-start(pred[4,2]{1,0:T(4,128)(4,1)} %get-tuple-element.16) | copy-start | bytes 28
  72.9 6.8 %copy-start.16 = (pred[4,2]{1,0:T(4,128)(4,1)S(1)}, pred[4,2]{1,0:T(4,128)(4,1)}, u32[]{:S(2)}) copy-start(pred[4,2]{1,0:T(4,128)(4,1)} %get-tuple-element.17) | copy-start | bytes 28
  74.4 15.0 %all-to-all-start.1 = ((bf16[8,8,5120]{2,1,0:T(8,128)(2,1)}), bf16[8,8,5120]{2,1,0:T(8,128)(2,1)S(1)}, u32[]{:S(2)}, u32[]{:S(2)}) async-start(bf16[8,8,5120]{2,1,0:T(8,128)(2,1)} %bitcast.106), calls=%async_computation.1 | async-start | bytes 1310720 | tf_op jit(solution)/shard_map/all_to_all | solution.py:216
  89.4 46.3 %all-to-all-start.3 = ((bf16[4,2,32,1280]{3,2,1,0:T(8,128)(2,1)}), bf16[4,2,32,1280]{3,2,1,0:T(8,128)(2,1)}, u32[]{:S(2)}, u32[]{:S(2)}) async-start(bf16[4,2,32,1280]{3,2,1,0:T(8,128)(2,1)} %select_select_fusion.2), calls=%async_computation.3 | async-start | bytes 1310720 | tf_op jit(solution)/shard_map/all_to_all | solution.py:231
where the time goes:
time: 142 us; the launch traced here: 141 us
  blocking collectives  40.3 us (28%)
  matrix products  25.4 us (18%)
  waiting for transfers between devices  21.3 us (15%)
  other arithmetic  18.9 us (13%)
  starting transfers between devices  18.2 us (13%)
  local copies, waits for them, and re-layouts  16 us (11%)
    psum x1, blocking collectives, per_device(): norm_grads = lax.psum(norm_terms, ('dp', 'ctx'))  40.3 us
    all_to_all x1, waiting for transfers between devices, per_device(): lax.all_to_all(outgoing.reshape(data_ranks, capacity, UNIT, model_width),...  13.7 us
    all_to_all x1, waiting for transfers between devices, per_device(): lax.all_to_all(window_out, 'ctx', split_axis=0, concat_axis=0, tiled=True)  7.61 us
    dot_general x1, matrix products, block_forward(): jnp.dot(shifted.astype(jnp.bfloat16), qkv_weight, preferred_element_type=...  5.4 us
    all_to_all x1, starting transfers between devices, per_device(): lax.all_to_all(merged_grad.reshape(owner_count, pair_slots, token_width),...  5.31 us
    all_to_all x1, starting transfers between devices, per_device(): lax.all_to_all(outgoing.reshape(data_ranks, capacity, UNIT, model_width),...  4.87 us
    dot_general x1, matrix products, block_backward(): lax.dot_general(qkv_grad, qkv_weight, transposed, preferred_element_type=...  4.63 us
    all_to_all x1, starting transfers between devices, per_device(): lax.all_to_all(backward_rows.reshape(data_ranks, capacity, UNIT, model_wi...  4.16 us
  transfers between devices with their start and end apart: 4, of which 2 were waited for; matrix products, arithmetic and copies ran while one was open for 15% of the time, Pallas kernels for 0%

commit v1 on v0

v1 whole, which is shorter than its diff:
```python
import functools

import jax
import jax.numpy as jnp
from jax import lax
from jax.experimental import pallas as pl
from jax.experimental.pallas import tpu as pltpu
from jax.sharding import PartitionSpec as P

HEAD = 80
UNIT = 32
MERGE = 4
EPS = 1e-06
NEG = -1e30
LANES = 128
WIN = 256
F32 = jnp.float32
BF16 = jnp.bfloat16


def paired(size):
    return size <= 8 and size & (size - 1) == 0


def peer_of(index, slot, size):
    return index ^ slot if paired(size) else slot


def place(slot, size):
    return (slot, 0) if paired(size) else (0, slot)


def in_hbm(array):
    return pltpu.with_memory_space_constraint(array, pltpu.HBM)


def pieces(size, shape, dtype):
    if paired(size):
        return [jax.ShapeDtypeStruct((1, *shape), dtype)] * size
    return [jax.ShapeDtypeStruct((size, *shape), dtype)]


def exchange(arrays, axis, size):
    if paired(size):
        return [arrays[0]] + [
            lax.ppermute(arrays[slot], axis, [(i, i ^ slot) for i in range(size)])
            for slot in range(1, size)
        ]
    return [lax.all_to_all(arrays[0], axis, split_axis=0, concat_axis=0, tiled=True)]


def total(terms, sizes):
    dp, ctx = sizes
    if not (paired(dp) and paired(ctx)):
        return lax.psum(terms, ("dp", "ctx"))
    rounds = [("ctx", ctx, (1,)), ("ctx", ctx, range(2, ctx, 2)), ("dp", dp, range(1, dp))]
    for axis, size, slots in rounds:
        others = [
            lax.ppermute(terms, axis, [(i, i ^ slot) for i in range(size)]) for slot in slots
        ]
        for other in others:
            terms = terms + other
    return terms


def starts(counts, ranks):
    out = [jnp.int32(0)]
    for rank in range(ranks - 1):
        out.append(out[-1] + counts[rank])
    return out


def chosen(values, index):
    out = values[0]
    for i in range(1, len(values)):
        out = jnp.where(index == i, values[i], out)
    return out


def pack_blocks(sizes, capacity, where, counts, source, *rest):
    ranks = sizes[0]
    outs, sems = rest[:-1], rest[-1]
    me = where[0]
    first = chosen(starts(counts, ranks), me)
    copies = []
    for slot in range(ranks):
        array, entry = place(slot, ranks)
        lead = lax.rem(peer_of(me, slot, ranks) + 8 * ranks - first, ranks)
        for k in range(capacity):
            block = jnp.minimum(lead + k * ranks, source.shape[0] - 1)
            copies.append(
                pltpu.make_async_copy(
                    source.at[block], outs[array].at[entry, k], sems.at[slot * capacity + k]
                )
            )
            copies[-1].start()
    for copy in copies:
        copy.wait()


def moments(values):
    average = jnp.mean(values, axis=-1, keepdims=True)
    centred = values - average
    inverse = lax.rsqrt(jnp.mean(centred * centred, axis=-1, keepdims=True) + EPS)
    return centred * inverse, inverse


def norm_back(scaled, normed, inverse):
    centre = jnp.mean(scaled, axis=-1, keepdims=True)
    slope = jnp.mean(scaled * normed, axis=-1, keepdims=True)
    return inverse * (scaled - centre - normed * slope)


def dot(a, b, ca=1, cb=0):
    return lax.dot_general(a, b, (((ca,), (cb,)), ((), ())), preferred_element_type=F32)


def iota(shape, dim):
    return lax.broadcasted_iota(jnp.int32, shape, dim)


def block_kernel(sizes, capacity, *refs):
    ranks, owners = sizes
    n_in = ranks if paired(ranks) else 1
    where, counts, labels, positions, params, wq_far, wo_far = refs[:7]
    refs = refs[7:]
    arrived, refs = refs[:n_in], refs[n_in:]
    grads, refs = refs[0], refs[1:]
    back, refs = refs[:n_in], refs[n_in:]
    windows, terms, xs, qs, ks, vs, ats, ps, dqs, dks, dvs, gs, ws, rows_out, wq, wo, sems = refs
    ln_gain, ln_bias, merge_gain, merge_bias = (params[i : i + 1, :] for i in range(4))
    rows, width = xs.shape
    units = rows // UNIT
    inner = wo.shape[0]
    heads = inner // HEAD
    scale = HEAD ** (-0.5)
    tokens = rows // MERGE
    thirds = [slice(part * inner, (part + 1) * inner) for part in range(3)]
    loads = [
        pltpu.make_async_copy(wq_far.at[third], wq.at[third], sems.at[part])
        for part, third in enumerate(thirds)
    ]
    loads.append(pltpu.make_async_copy(wo_far, wo, sems.at[3]))
    for load in loads:
        load.start()
    pair = grads.shape[1]
    slots = owners * pair
    me, column = where[0], where[1]
    begin = starts(counts, ranks)

    for unit in range(units):
        wanted = unit * ranks + me
        sender = jnp.int32(0)
        for rank in range(1, ranks):
            sender = jnp.where(begin[rank] <= wanted, rank, sender)
        kth = (wanted - chosen(begin, sender)) // ranks
        span = slice(unit * UNIT, (unit + 1) * UNIT)
        if n_in == 1:
            xs[span, :] = arrived[0][sender, kth].astype(F32)
        else:
            slot = sender ^ me
            value = arrived[0][0, kth]
            for i in range(1, n_in):
                value = jnp.where(slot == i, arrived[i][0, kth], value)
            xs[span, :] = value.astype(F32)

    label = jnp.broadcast_to(labels[...].astype(F32), (rows, rows))
    joined = (label == label.T) & (
        iota((rows, rows), 0) // UNIT == iota((rows, rows), 1) // UNIT
    )
    own = iota((rows, tokens), 0) // MERGE == iota((rows, tokens), 1)
    place_of = positions[...] - column * slots
    spot = jnp.sum(jnp.where(own, place_of.astype(F32), 0.0), axis=1, keepdims=True)
    spot_row = jnp.broadcast_to(spot, (rows, LANES)).T[:1, :]
    spot = spot.astype(jnp.int32)
    spot_row = spot_row.astype(jnp.int32)

    def slot_place(index):
        local = index % slots
        return (local % pair) * owners + local // pair

    lane = iota((rows, MERGE * slots), 1)
    take = (
        (iota((rows, MERGE * slots), 0) % MERGE == lane // slots) & (slot_place(lane) == spot)
    ).astype(BF16)
    lead = iota((MERGE * slots, rows), 0)
    put = (
        (iota((MERGE * slots, rows), 1) % MERGE == lead // slots) & (slot_place(lead) == spot_row)
    ).astype(BF16)

    normed_in, inverse_in = moments(xs[...])
    shifted = (normed_in * ln_gain + ln_bias).astype(BF16)
    padded = qs.shape[1]
    zero = jnp.zeros((rows, padded - inner), BF16)
    for ref, part in ((qs, 0), (ks, 1), (vs, 2)):
        loads[part].wait()
        ref[:, :inner] = dot(shifted, wq[thirds[part], :], 1, 1).astype(BF16)
    qs[:, inner:] = zero
    ks[:, inner:] = zero
    vs[:, inner:] = zero
    ats[...] = jnp.zeros_like(ats)
    dqs[...] = jnp.zeros_like(dqs)
    dks[...] = jnp.zeros_like(dks)
    dvs[...] = jnp.zeros_like(dvs)

    win_lane = iota((rows, WIN), 1)

    def window(head):
        at = head * HEAD
        low = at // LANES * LANES
        mask = (win_lane >= at - low) & (win_lane < at - low + HEAD)
        return slice(low, low + WIN), mask

    none = jnp.zeros((), BF16)
    for head in range(heads):
        span, mask = window(head)
        scores = dot(jnp.where(mask, qs[:, span], none), ks[:, span], 1, 1) * scale
        scores = jnp.where(joined, scores, NEG)
        raised = jnp.exp(scores - jnp.max(scores, axis=-1, keepdims=True))
        prob = raised / jnp.sum(raised, axis=-1, keepdims=True)
        ps[head] = prob
        ats[:, span] += dot(prob.astype(BF16), jnp.where(mask, vs[:, span], none))
    loads[3].wait()
    hidden = xs[...] + dot(ats[:, :inner].astype(BF16), wo[...])
    normed_out, inverse_out = moments(hidden)
    result = (normed_out * merge_gain + merge_bias).astype(BF16)
    ws[...] = dot(put, result)
    for owner in range(owners):
        for part in range(MERGE):
            start = part * slots + owner * pair
            windows[owner, :, part * width : (part + 1) * width] = ws[
                start : start + pair, :
            ].astype(BF16)

    for owner in range(owners):
        for part in range(MERGE):
            start = part * slots + owner * pair
            ws[start : start + pair, :] = grads[
                owner, :, part * width : (part + 1) * width
            ].astype(F32)
    upstream = dot(take, ws[...].astype(BF16))
    terms[2:3, :] = jnp.sum(upstream * normed_out, axis=0, keepdims=True)
    terms[3:4, :] = jnp.sum(upstream, axis=0, keepdims=True)
    hidden_grad = norm_back(upstream * merge_gain, normed_out, inverse_out)
    gs[:, :inner] = dot(hidden_grad.astype(BF16), wo[...], 1, 1).astype(BF16)
    gs[:, inner:] = zero
    for head in range(heads):
        span, mask = window(head)
        prob = ps[head]
        grad = jnp.where(mask, gs[:, span], none)
        prob_grad = dot(grad, vs[:, span], 1, 1)
        dvs[:, span] += dot(prob.astype(BF16), grad, 0, 0)
        centred = prob_grad - jnp.sum(prob * prob_grad, axis=-1, keepdims=True)
        score_grad = (prob * centred * scale).astype(BF16)
        dqs[:, span] += dot(score_grad, jnp.where(mask, ks[:, span], none))
        dks[:, span] += dot(score_grad, jnp.where(mask, qs[:, span], none), 0, 0)
    input_grad = sum(
        dot(ref[:, :inner].astype(BF16), wq[thirds[part], :])
        for ref, part in ((dqs, 0), (dks, 1), (dvs, 2))
    )
    terms[0:1, :] = jnp.sum(input_grad * normed_in, axis=0, keepdims=True)
    terms[1:2, :] = jnp.sum(input_grad, axis=0, keepdims=True)
    row_grad = hidden_grad + norm_back(input_grad * ln_gain, normed_in, inverse_in)
    rows_out[...] = row_grad.astype(BF16).reshape(units, UNIT, width)

    for slot in range(ranks):
        array, entry = place(slot, ranks)
        peer = peer_of(me, slot, ranks)
        base_of = chosen(begin, peer)
        low = lax.rem(me + 8 * ranks - base_of, ranks)
        for k in range(capacity):
            unit = jnp.minimum((base_of + low + k * ranks) // ranks, units - 1)
            back[array][entry, k] = rows_out[unit]


def unpack_kernel(sizes, capacity, *refs):
    ranks = sizes[0]
    where, counts = refs[:2]
    came, patch_grad = refs[2:-1], refs[-1]
    me = where[0]
    first = chosen(starts(counts, ranks), me)
    live = chosen([counts[rank] for rank in range(ranks)], me)
    for slot in range(ranks):
        array, entry = place(slot, ranks)
        low = lax.rem(peer_of(me, slot, ranks) + 8 * ranks - first, ranks)
        for k in range(capacity):
            block = low + k * ranks

            @pl.when(block < live)
            def _(array=array, entry=entry, k=k, block=block):
                patch_grad[block] = came[array][entry, k]

            @pl.when((block >= live) & (block < patch_grad.shape[0]))
            def _(block=block):
                patch_grad[block] = jnp.zeros(patch_grad.shape[1:], BF16)


def per_device(
    sizes,
    patches,
    unit_counts,
    segment_ids,
    merged_position,
    ln_gain,
    ln_bias,
    qkv_weight,
    out_weight,
    merge_gain,
    merge_bias,
    merged_grad,
):
    ranks, owners = sizes
    width = patches.shape[1]
    source_units = patches.shape[0] // UNIT
    rows = segment_ids.shape[0]
    capacity = -(-source_units // ranks)
    owner_slots, token_width = merged_grad.shape
    pair = owner_slots // owners
    inner = out_weight.shape[0]
    heads = inner // HEAD
    padded = -(-inner // LANES) * LANES
    where = jnp.stack([lax.axis_index("dp"), lax.axis_index("ctx")]).astype(jnp.int32)
    counts = unit_counts.reshape(-1)
    smem = pl.BlockSpec(memory_space=pltpu.SMEM)
    vmem = pl.BlockSpec(memory_space=pltpu.VMEM)
    anywhere = pl.BlockSpec(memory_space=pl.ANY)

    block_shapes = pieces(ranks, (capacity, UNIT, width), BF16)
    window_shape = jax.ShapeDtypeStruct((owners, pair, token_width), BF16)
    n_in = len(block_shapes)
    swap = functools.partial(
        lax.all_to_all, axis_name="ctx", split_axis=0, concat_axis=0, tiled=True
    )

    outgoing = pl.pallas_call(
        functools.partial(pack_blocks, sizes, capacity),
        out_shape=block_shapes,
        in_specs=[smem, smem, anywhere],
        out_specs=[vmem] * n_in,
        scratch_shapes=[pltpu.SemaphoreType.DMA((ranks * capacity,))],
        compiler_params=pltpu.CompilerParams(vmem_limit_bytes=4 * 2**20),
        name="pack_blocks",
    )(
        in_hbm(where),
        in_hbm(counts),
        in_hbm(patches.reshape(source_units, UNIT, width)),
    )
    arrived = exchange(outgoing, "dp", ranks)

    grad_blocks = merged_grad.reshape(owners, pair, token_width)
    grads = swap(grad_blocks)

    results = pl.pallas_call(
        functools.partial(block_kernel, sizes, capacity),
        out_shape=[
            *block_shapes,
            window_shape,
            jax.ShapeDtypeStruct((4, width), F32),
        ],
        in_specs=[smem, smem] + [vmem] * 3 + [anywhere] * 2 + [vmem] * (n_in + 1),
        out_specs=[vmem] * (n_in + 2),
        scratch_shapes=[
            pltpu.VMEM((rows, width), F32),
            pltpu.VMEM((rows, padded), BF16),
            pltpu.VMEM((rows, padded), BF16),
            pltpu.VMEM((rows, padded), BF16),
            pltpu.VMEM((rows, padded), F32),
            pltpu.VMEM((heads, rows, rows), F32),
            pltpu.VMEM((rows, padded), F32),
            pltpu.VMEM((rows, padded), F32),
            pltpu.VMEM((rows, padded), F32),
            pltpu.VMEM((rows, padded), BF16),
            pltpu.VMEM((MERGE * owners * pair, width), F32),
            pltpu.VMEM((rows // UNIT, UNIT, width), BF16),
            pltpu.VMEM((3 * inner, width), BF16),
            pltpu.VMEM((inner, width), BF16),
            pltpu.SemaphoreType.DMA((4,)),
        ],
        compiler_params=pltpu.CompilerParams(vmem_limit_bytes=40 * 2**20),
        cost_estimate=pl.CostEstimate(
            flops=3 * 10**9, bytes_accessed=12 * 10**6, transcendentals=200_000
        ),
        name="block",
    )(
        in_hbm(where),
        in_hbm(counts),
        in_hbm(segment_ids.reshape(1, rows)),
        in_hbm(merged_position.reshape(1, rows // MERGE)),
        in_hbm(jnp.stack([ln_gain, ln_bias, merge_gain, merge_bias])),
        in_hbm(qkv_weight.T),
        in_hbm(out_weight),
        in_hbm(arrived[0]),
        *arrived[1:],
        grads,
    )
    came_back = exchange(results[:n_in], "dp", ranks)
    merged = swap(results[n_in])
    norm_grads = total(results[-1], sizes)
    patch_grad = pl.pallas_call(
        functools.partial(unpack_kernel, sizes, capacity),
        out_shape=jax.ShapeDtypeStruct((source_units, UNIT, width), BF16),
        in_specs=[smem, smem] + [vmem] * n_in,
        out_specs=vmem,
        compiler_params=pltpu.CompilerParams(vmem_limit_bytes=8 * 2**20),
        name="unpack",
    )(in_hbm(where), in_hbm(counts), in_hbm(came_back[0]), *came_back[1:])
    return (
        merged.reshape(owner_slots, token_width),
        patch_grad.reshape(source_units * UNIT, width),
        norm_grads,
    )


def solution(mesh):
    return jax.shard_map(
        functools.partial(per_device, (mesh.shape["dp"], mesh.shape["ctx"])),
        mesh=mesh,
        in_specs=(
            P(("dp", "ctx"), None),
            P("ctx", None),
            P(("dp", "ctx")),
            P(("dp", "ctx")),
            P(),
            P(),
            P(),
            P(),
            P(),
            P(),
            P(("dp", "ctx"), None),
        ),
        out_specs=(P(("dp", "ctx"), None), P(("dp", "ctx"), None), P()),
        check_vma=False,
    )
```

time: 142 us -> 74.4 us (0.52)
  blocking collectives: 40.3 us -> 0 us
  matrix products: 25.4 us -> 0 us
  Pallas kernels: 0 us -> 18 us
  other arithmetic: 18.9 us -> 1.89 us
  local copies, waits for them, and re-layouts: 16 us -> 4.95 us
  starting transfers between devices: 18.2 us -> 26.4 us
    psum x1 -> x0, blocking collectives: 40.3 us -> none  [per_device(): norm_grads = lax.psum(norm_terms, ('dp', 'ctx'))]
    dot_general x11 -> x0, matrix products: 24.1 us -> none  [the longest x1 5.4 us: block_forward(): jnp.dot(shifted.astype(jnp.bfloat16), qkv_weight, preferred_element_type=...]
    ppermute x0 -> x13, waiting for transfers between devices: none -> 21.9 us  [the longest x6 20.7 us: exchange(): lax.ppermute(arrays[slot], axis, [(i, i ^ slot) for i in range(size)])]
    all_to_all x4 -> x2, waiting for transfers between devices: 21.3 us -> 0.01 us  [the longest x1 0.01 us: per_device(): grads = swap(grad_blocks)]
    pallas_call x0 -> x3, Pallas kernels: none -> 18 us  [the longest x1 14.2 us: per_device(): pl.pallas_call(functools.partial(block_kernel, sizes, capacity), out_shap...]
    ppermute x0 -> x13, starting transfers between devices: none -> 17.1 us  [the longest x6 8.77 us: exchange(): lax.ppermute(arrays[slot], axis, [(i, i ^ slot) for i in range(size)])]
    select_n x10 -> x0, other arithmetic: 9.41 us -> none  [the longest x1 2.08 us: per_device(): outgoing = jnp.where(picked_live[:, None, None], outgoing, zero_half)]
    all_to_all x4 -> x2, starting transfers between devices: 18.2 us -> 9.3 us  [the longest x1 5.18 us: per_device(): grads = swap(grad_blocks)]
  transfers between devices with their start and end apart: 4 -> 15, of which waited for: 2 -> 5; matrix products, arithmetic and copies ran while one was open for 15% -> 6% of each run, Pallas kernels for 0% -> 5%
where the time goes in v1:
time: 74.4 us; the launch traced here: 73.8 us
  starting transfers between devices  26.4 us (35%)
  waiting for transfers between devices  21.9 us (29%)
  Pallas kernels  18 us (24%)
  local copies, waits for them, and re-layouts  4.95 us (7%)
  other arithmetic  1.89 us (3%)
    ppermute x6, waiting for transfers between devices, exchange(): lax.ppermute(arrays[slot], axis, [(i, i ^ slot) for i in range(size)])  20.7 us
    pallas_call x1, Pallas kernels, per_device(): pl.pallas_call(functools.partial(block_kernel, sizes, capacity), out_shap...  14.2 us
    ppermute x6, starting transfers between devices, exchange(): lax.ppermute(arrays[slot], axis, [(i, i ^ slot) for i in range(size)])  8.77 us
    ppermute x7, starting transfers between devices, total(): lax.ppermute(terms, axis, [(i, i ^ slot) for i in range(size)])  8.28 us
    all_to_all x1, starting transfers between devices, per_device(): grads = swap(grad_blocks)  5.18 us
    all_to_all x1, starting transfers between devices, per_device(): merged = swap(results[n_in])  4.12 us
    another operation x4, local copies, waits for them, and re-layouts, per_device(): jnp.stack([ln_gain, ln_bias, merge_gain, merge_bias])  2.8 us
    unnamed x5, local copies, waits for them, and re-layouts  2.15 us
  transfers between devices with their start and end apart: 15, of which 5 were waited for; matrix products, arithmetic and copies ran while one was open for 6% of the time, Pallas kernels for 5%

profile of v1, /device:TPU:0, one launch (start us, length us, event | category | flops | bytes accessed | tf_op | source)
XLA Modules:
  0.0 73.8 jit_solution(9025244275790533367)
XLA Ops:
  0.6 5.2 %all-to-all-start = ((bf16[8,8,5120]{2,1,0:T(8,128)(2,1)}), bf16[8,8,5120]{2,1,0:T(8,128)(2,1)S(1)}, u32[]{:S(2)}, u32[]{:S(2)}) async-start(bf16[8,8,5120]{2,1,0:T(8,128)(2,1)} %bitcast.13), calls=%async_computation | async-start | bytes 1310720 | tf_op jit(solution)/shard_map/all_to_all | solution.py:351
  5.8 0.6 pad_add_fusion.where.refs_0_
  6.4 1.9 %pack_blocks.1 = (bf16[1,2,32,1280]{3,2,1,0:T(8,128)(2,1)S(1)}, bf16[1,2,32,1280]{3,2,1,0:T(8,128)(2,1)S(1)}, bf16[1,2,32,1280]{3,2,1,0:T(8,128)(2,1)S(1)}, bf16[1,2,32,1280]{3,2,1,0:T(8,128)(2,1)S(1)}) custom-call(s32[2]{0:T(128)} %pad_add_fusion.where.refs_0_, s32[4]{0:T(128)} %bitcast.15, bf16[8,32,1280]{2,1,0:T(8,128)(2,1)} %bitcast.12), custom_call_target="tpu_custom_call" | custom-call | tf_op jit(solution)/shard_map/pack_blocks/pallas_call | solution.py:335
  8.4 0.0 copy-start.1
  8.4 0.7 copy-done.1
  9.0 1.6 %collective-permute-start = (bf16[1,2,32,1280]{3,2,1,0:T(8,128)(2,1)S(1)}, bf16[1,2,32,1280]{3,2,1,0:T(8,128)(2,1)S(1)}, u32[]{:S(2)}, u32[]{:S(2)}) collective-permute-start(bf16[1,2,32,1280]{3,2,1,0:T(8,128)(2,1)S(1)} %get-tuple-element.14), channel_id=1, source_target_pairs={{0,8},{8,0},{16,24},{24,16},{1,9},{9,1},{17,25},{25,17},{2,10},{10... | collective-permute-start | bytes 491528 | tf_op jit(solution)/shard_map/ppermute | solution.py:46
  10.6 2.6 %collective-permute-start.1 = (bf16[1,2,32,1280]{3,2,1,0:T(8,128)(2,1)S(1)}, bf16[1,2,32,1280]{3,2,1,0:T(8,128)(2,1)S(1)}, u32[]{:S(2)}, u32[]{:S(2)}) collective-permute-start(bf16[1,2,32,1280]{3,2,1,0:T(8,128)(2,1)S(1)} %get-tuple-element.15), channel_id=1, source_target_pairs={{0,16},{8,24},{16,0},{24,8},{1,17},{9,25},{17,1},{25,9},{2,18},{10... | collective-permute-start | bytes 491528 | tf_op jit(solution)/shard_map/ppermute | solution.py:46
  13.2 0.2 collective-permute-start.2
  13.4 0.7 stack.27
  14.1 0.7 stack.28
  14.8 0.7 stack.29
  15.5 0.7 stack.30
  16.2 0.6 pad_maximum_fusion.refs_4_
  16.9 1.9 %collective-permute-done.refs_8_ = bf16[1,2,32,1280]{3,2,1,0:T(8,128)(2,1)S(1)} collective-permute-done((bf16[1,2,32,1280]{3,2,1,0:T(8,128)(2,1)S(1)}, bf16[1,2,32,1280]{3,2,1,0:T(8,128)(2,1)S(1)}, u32[]{:S(2)}, u32[]{:S(2)}) %collective-permute-start) | collective-permute-done | bytes 163872 | tf_op jit(solution)/shard_map/ppermute | solution.py:46
  18.7 6.9 %collective-permute-done.1.refs_9_ = bf16[1,2,32,1280]{3,2,1,0:T(8,128)(2,1)S(1)} collective-permute-done((bf16[1,2,32,1280]{3,2,1,0:T(8,128)(2,1)S(1)}, bf16[1,2,32,1280]{3,2,1,0:T(8,128)(2,1)S(1)}, u32[]{:S(2)}, u32[]{:S(2)}) %collective-permute-start.1) | collective-permute-done | bytes 163872 | tf_op jit(solution)/shard_map/ppermute | solution.py:46
  25.6 0.0 collective-permute-done.2.refs_10_
  25.6 0.0 all-to-all-done.refs_11_
  25.6 14.2 %block.1 = (bf16[1,2,32,1280]{3,2,1,0:T(8,128)(2,1)S(1)}, bf16[1,2,32,1280]{3,2,1,0:T(8,128)(2,1)S(1)}, bf16[1,2,32,1280]{3,2,1,0:T(8,128)(2,1)S(1)}, bf16[1,2,3...) custom-call(s32[2]{0:T(128)} %pad_add_fusion.where.refs_0_, s32[4]{0:T(128)} %bitcast.16, ...), custom_call_target="tpu_custom_call" | custom-call | flops 3000000000 | bytes 12000000 | tf_op jit(solution)/shard_map/block/pallas_call | solution.py:353
  39.8 0.0 copy-start
  39.8 0.7 copy-done
  40.5 0.0 collective-permute-start.6
  40.5 1.2 %collective-permute-done.6 = f32[4,1280]{1,0:T(4,128)S(1)} collective-permute-done((f32[4,1280]{1,0:T(4,128)S(1)}, f32[4,1280]{1,0:T(4,128)S(1)}, u32[]{:S(2)}, u32[]{:S(2)}) %collective-permute-start.6) | collective-permute-done | bytes 20512 | tf_op jit(solution)/shard_map/ppermute | solution.py:59
  41.7 3.0 %collective-permute-start.9 = (f32[4,1280]{1,0:T(4,128)S(1)}, f32[4,1280]{1,0:T(4,128)S(1)}, u32[]{:S(2)}, u32[]{:S(2)}) collective-permute-start(f32[4,1280]{1,0:T(4,128)S(1)} %add.21), channel_id=1, source_target_pairs={{0,6},{1,7},{2,4},{3,5},{4,2},{5,3},{6,0},{7,1},{8,14},{9,15},{10,... | collective-permute-start | bytes 61448 | tf_op jit(solution)/shard_map/ppermute | solution.py:59
  44.7 0.6 collective-permute-start.8
  45.2 0.1 collective-permute-start.7
  45.3 4.1 %all-to-all-start.1 = ((bf16[8,8,5120]{2,1,0:T(8,128)(2,1)}), bf16[8,8,5120]{2,1,0:T(8,128)(2,1)S(1)}, u32[]{:S(2)}, u32[]{:S(2)}) async-start(bf16[8,8,5120]{2,1,0:T(8,128)(2,1)} %get-tuple-element.17), calls=%async_computation.1 | async-start | bytes 1310720 | tf_op jit(solution)/shard_map/all_to_all | solution.py:397
  49.4 0.0 collective-permute-done.9
  49.4 0.0 collective-permute-done.8
  49.5 0.0 collective-permute-done.7
  49.5 2.5 %collective-permute-start.12 = (f32[4,1280]{1,0:T(4,128)S(1)}, f32[4,1280]{1,0:T(4,128)S(1)}, u32[]{:S(2)}, u32[]{:S(2)}) collective-permute-start(f32[4,1280]{1,0:T(4,128)S(1)} %add_add_fusion.1), channel_id=1, source_target_pairs={{0,24},{8,16},{16,8},{24,0},{1,25},{9,17},{17,9},{25,1},{2,26},{10... | collective-permute-start | bytes 61448 | tf_op jit(solution)/shard_map/ppermute | solution.py:59
  52.0 2.0 %collective-permute-start.11 = (f32[4,1280]{1,0:T(4,128)S(1)}, f32[4,1280]{1,0:T(4,128)S(1)}, u32[]{:S(2)}, u32[]{:S(2)}) collective-permute-start(f32[4,1280]{1,0:T(4,128)S(1)} %add_add_fusion.1), channel_id=1, source_target_pairs={{0,16},{8,24},{16,0},{24,8},{1,17},{9,25},{17,1},{25,9},{2,18},{10... | collective-permute-start | bytes 61448 | tf_op jit(solution)/shard_map/ppermute | solution.py:59
  54.0 0.1 collective-permute-start.10
  54.1 1.9 %collective-permute-start.3 = (bf16[1,2,32,1280]{3,2,1,0:T(8,128)(2,1)S(1)}, bf16[1,2,32,1280]{3,2,1,0:T(8,128)(2,1)S(1)}, u32[]{:S(2)}, u32[]{:S(2)}) collective-permute-start(bf16[1,2,32,1280]{3,2,1,0:T(8,128)(2,1)S(1)} %get-tuple-element.19), channel_id=1, source_target_pairs={{0,8},{8,0},{16,24},{24,16},{1,9},{9,1},{17,25},{25,17},{2,10},{10... | collective-permute-start | bytes 491528 | tf_op jit(solution)/shard_map/ppermute | solution.py:46
  56.1 1.0 %collective-permute-start.4 = (bf16[1,2,32,1280]{3,2,1,0:T(8,128)(2,1)S(1)}, bf16[1,2,32,1280]{3,2,1,0:T(8,128)(2,1)S(1)}, u32[]{:S(2)}, u32[]{:S(2)}) collective-permute-start(bf16[1,2,32,1280]{3,2,1,0:T(8,128)(2,1)S(1)} %get-tuple-element.20), channel_id=1, source_target_pairs={{0,16},{8,24},{16,0},{24,8},{1,17},{9,25},{17,1},{25,9},{2,18},{10... | collective-permute-start | bytes 491528 | tf_op jit(solution)/shard_map/ppermute | solution.py:46
  57.1 0.0 collective-permute-done.12
  57.1 1.4 %collective-permute-start.5 = (bf16[1,2,32,1280]{3,2,1,0:T(8,128)(2,1)S(1)}, bf16[1,2,32,1280]{3,2,1,0:T(8,128)(2,1)S(1)}, u32[]{:S(2)}, u32[]{:S(2)}) collective-permute-start(bf16[1,2,32,1280]{3,2,1,0:T(8,128)(2,1)S(1)} %get-tuple-element.21), channel_id=1, source_target_pairs={{0,24},{8,16},{16,8},{24,0},{1,25},{9,17},{17,9},{25,1},{2,26},{10... | collective-permute-start | bytes 491528 | tf_op jit(solution)/shard_map/ppermute | solution.py:46
  58.5 0.0 collective-permute-done.11
  58.5 0.0 collective-permute-done.10
  58.5 0.6 add_add_fusion
  59.2 4.0 %collective-permute-done.3.refs_3_ = bf16[1,2,32,1280]{3,2,1,0:T(8,128)(2,1)S(1)} collective-permute-done((bf16[1,2,32,1280]{3,2,1,0:T(8,128)(2,1)S(1)}, bf16[1,2,32,1280]{3,2,1,0:T(8,128)(2,1)S(1)}, u32[]{:S(2)}, u32[]{:S(2)}) %collective-permute-start.3) | collective-permute-done | bytes 163872 | tf_op jit(solution)/shard_map/ppermute | solution.py:46
  63.1 8.0 %collective-permute-done.4.refs_4_ = bf16[1,2,32,1280]{3,2,1,0:T(8,128)(2,1)S(1)} collective-permute-done((bf16[1,2,32,1280]{3,2,1,0:T(8,128)(2,1)S(1)}, bf16[1,2,32,1280]{3,2,1,0:T(8,128)(2,1)S(1)}, u32[]{:S(2)}, u32[]{:S(2)}) %collective-permute-start.4) | collective-permute-done | bytes 163872 | tf_op jit(solution)/shard_map/ppermute | solution.py:46
  71.1 0.0 collective-permute-done.5.refs_5_
  71.1 1.9 %unpack.1 = bf16[8,32,1280]{2,1,0:T(8,128)(2,1)} custom-call(s32[2]{0:T(128)} %pad_add_fusion.where.refs_0_, s32[4]{0:T(128)} %bitcast.17, bf16[1,2,32,1280]{3,2,1,0:T(8,128)(2,1)} %copy-done, bf16[1,2,32,1280]{3,2,1,0:T(8,128)(2,1)S(1)} %collective-permute-done.3.refs_3_, bf16[1,2,32,1280]{3,2,1,0:T(8,128)(2,1)S(1)} %collective-permute-done.4.refs_4_, ...), custom_call_target="tpu_custom_call" | custom-call | tf_op jit(solution)/shard_map/unpack/pallas_call | solution.py:399
  73.0 0.0 all-to-all-done.1
  73.0 0.8 %copy.15 = bf16[64,5120]{1,0:T(8,128)(2,1)} copy(bf16[64,5120]{1,0:T(8,128)(2,1)S(1)} %bitcast.11) | data formatting | bytes 1310720
  (2 shorter events, 0.0 us)
Async XLA Ops:
  0.6 25.0 %all-to-all-start = ((bf16[8,8,5120]{2,1,0:T(8,128)(2,1)}), bf16[8,8,5120]{2,1,0:T(8,128)(2,1)S(1)}, u32[]{:S(2)}, u32[]{:S(2)}) async-start(bf16[8,8,5120]{2,1,0:T(8,128)(2,1)} %bitcast.13), calls=%async_computation | async-start | bytes 1310720 | tf_op jit(solution)/shard_map/all_to_all | solution.py:351
  8.4 0.7 copy-start.1
  9.0 9.7 %collective-permute-start = (bf16[1,2,32,1280]{3,2,1,0:T(8,128)(2,1)S(1)}, bf16[1,2,32,1280]{3,2,1,0:T(8,128)(2,1)S(1)}, u32[]{:S(2)}, u32[]{:S(2)}) collective-permute-start(bf16[1,2,32,1280]{3,2,1,0:T(8,128)(2,1)S(1)} %get-tuple-element.14), channel_id=1, source_target_pairs={{0,8},{8,0},{16,24},{24,16},{1,9},{9,1},{17,25},{25,17},{2,10},{10... | collective-permute-start | bytes 491528 | tf_op jit(solution)/shard_map/ppermute | solution.py:46
  10.6 15.0 %collective-permute-start.1 = (bf16[1,2,32,1280]{3,2,1,0:T(8,128)(2,1)S(1)}, bf16[1,2,32,1280]{3,2,1,0:T(8,128)(2,1)S(1)}, u32[]{:S(2)}, u32[]{:S(2)}) collective-permute-start(bf16[1,2,32,1280]{3,2,1,0:T(8,128)(2,1)S(1)} %get-tuple-element.15), channel_id=1, source_target_pairs={{0,16},{8,24},{16,0},{24,8},{1,17},{9,25},{17,1},{25,9},{2,18},{10... | collective-permute-start | bytes 491528 | tf_op jit(solution)/shard_map/ppermute | solution.py:46
  13.2 12.4 %collective-permute-start.2 = (bf16[1,2,32,1280]{3,2,1,0:T(8,128)(2,1)S(1)}, bf16[1,2,32,1280]{3,2,1,0:T(8,128)(2,1)S(1)}, u32[]{:S(2)}, u32[]{:S(2)}) collective-permute-start(bf16[1,2,32,1280]{3,2,1,0:T(8,128)(2,1)S(1)} %get-tuple-element.16), channel_id=1, source_target_pairs={{0,24},{8,16},{16,8},{24,0},{1,25},{9,17},{17,9},{25,1},{2,26},{10... | collective-permute-start | bytes 491528 | tf_op jit(solution)/shard_map/ppermute | solution.py:46
  39.8 0.7 copy-start
  40.5 1.2 %collective-permute-start.6 = (f32[4,1280]{1,0:T(4,128)S(1)}, f32[4,1280]{1,0:T(4,128)S(1)}, u32[]{:S(2)}, u32[]{:S(2)}) collective-permute-start(f32[4,1280]{1,0:T(4,128)S(1)} %get-tuple-element.22), channel_id=1, source_target_pairs={{0,1},{1,0},{2,3},{3,2},{4,5},{5,4},{6,7},{7,6},{8,9},{9,8},{10,11... | collective-permute-start | bytes 61448 | tf_op jit(solution)/shard_map/ppermute | solution.py:59
  41.7 7.8 %collective-permute-start.9 = (f32[4,1280]{1,0:T(4,128)S(1)}, f32[4,1280]{1,0:T(4,128)S(1)}, u32[]{:S(2)}, u32[]{:S(2)}) collective-permute-start(f32[4,1280]{1,0:T(4,128)S(1)} %add.21), channel_id=1, source_target_pairs={{0,6},{1,7},{2,4},{3,5},{4,2},{5,3},{6,0},{7,1},{8,14},{9,15},{10,... | collective-permute-start | bytes 61448 | tf_op jit(solution)/shard_map/ppermute | solution.py:59
  44.7 4.8 %collective-permute-start.8 = (f32[4,1280]{1,0:T(4,128)S(1)}, f32[4,1280]{1,0:T(4,128)S(1)}, u32[]{:S(2)}, u32[]{:S(2)}) collective-permute-start(f32[4,1280]{1,0:T(4,128)S(1)} %add.21), channel_id=1, source_target_pairs={{0,4},{1,5},{2,6},{3,7},{4,0},{5,1},{6,2},{7,3},{8,12},{9,13},{10,... | collective-permute-start | bytes 61448 | tf_op jit(solution)/shard_map/ppermute | solution.py:59
  45.2 4.2 %collective-permute-start.7 = (f32[4,1280]{1,0:T(4,128)S(1)}, f32[4,1280]{1,0:T(4,128)S(1)}, u32[]{:S(2)}, u32[]{:S(2)}) collective-permute-start(f32[4,1280]{1,0:T(4,128)S(1)} %add.21), channel_id=1, source_target_pairs={{0,2},{1,3},{2,0},{3,1},{4,6},{5,7},{6,4},{7,5},{8,10},{9,11},{10,... | collective-permute-start | bytes 61448 | tf_op jit(solution)/shard_map/ppermute | solution.py:59
  45.3 27.7 %all-to-all-start.1 = ((bf16[8,8,5120]{2,1,0:T(8,128)(2,1)}), bf16[8,8,5120]{2,1,0:T(8,128)(2,1)S(1)}, u32[]{:S(2)}, u32[]{:S(2)}) async-start(bf16[8,8,5120]{2,1,0:T(8,128)(2,1)} %get-tuple-element.17), calls=%async_computation.1 | async-start | bytes 1310720 | tf_op jit(solution)/shard_map/all_to_all | solution.py:397
  49.5 7.6 %collective-permute-start.12 = (f32[4,1280]{1,0:T(4,128)S(1)}, f32[4,1280]{1,0:T(4,128)S(1)}, u32[]{:S(2)}, u32[]{:S(2)}) collective-permute-start(f32[4,1280]{1,0:T(4,128)S(1)} %add_add_fusion.1), channel_id=1, source_target_pairs={{0,24},{8,16},{16,8},{24,0},{1,25},{9,17},{17,9},{25,1},{2,26},{10... | collective-permute-start | bytes 61448 | tf_op jit(solution)/shard_map/ppermute | solution.py:59
  52.0 6.5 %collective-permute-start.11 = (f32[4,1280]{1,0:T(4,128)S(1)}, f32[4,1280]{1,0:T(4,128)S(1)}, u32[]{:S(2)}, u32[]{:S(2)}) collective-permute-start(f32[4,1280]{1,0:T(4,128)S(1)} %add_add_fusion.1), channel_id=1, source_target_pairs={{0,16},{8,24},{16,0},{24,8},{1,17},{9,25},{17,1},{25,9},{2,18},{10... | collective-permute-start | bytes 61448 | tf_op jit(solution)/shard_map/ppermute | solution.py:59
  54.0 4.5 %collective-permute-start.10 = (f32[4,1280]{1,0:T(4,128)S(1)}, f32[4,1280]{1,0:T(4,128)S(1)}, u32[]{:S(2)}, u32[]{:S(2)}) collective-permute-start(f32[4,1280]{1,0:T(4,128)S(1)} %add_add_fusion.1), channel_id=1, source_target_pairs={{0,8},{8,0},{16,24},{24,16},{1,9},{9,1},{17,25},{25,17},{2,10},{10... | collective-permute-start | bytes 61448 | tf_op jit(solution)/shard_map/ppermute | solution.py:59
  54.1 9.0 %collective-permute-start.3 = (bf16[1,2,32,1280]{3,2,1,0:T(8,128)(2,1)S(1)}, bf16[1,2,32,1280]{3,2,1,0:T(8,128)(2,1)S(1)}, u32[]{:S(2)}, u32[]{:S(2)}) collective-permute-start(bf16[1,2,32,1280]{3,2,1,0:T(8,128)(2,1)S(1)} %get-tuple-element.19), channel_id=1, source_target_pairs={{0,8},{8,0},{16,24},{24,16},{1,9},{9,1},{17,25},{25,17},{2,10},{10... | collective-permute-start | bytes 491528 | tf_op jit(solution)/shard_map/ppermute | solution.py:46
  56.1 15.1 %collective-permute-start.4 = (bf16[1,2,32,1280]{3,2,1,0:T(8,128)(2,1)S(1)}, bf16[1,2,32,1280]{3,2,1,0:T(8,128)(2,1)S(1)}, u32[]{:S(2)}, u32[]{:S(2)}) collective-permute-start(bf16[1,2,32,1280]{3,2,1,0:T(8,128)(2,1)S(1)} %get-tuple-element.20), channel_id=1, source_target_pairs={{0,16},{8,24},{16,0},{24,8},{1,17},{9,25},{17,1},{25,9},{2,18},{10... | collective-permute-start | bytes 491528 | tf_op jit(solution)/shard_map/ppermute | solution.py:46
  57.1 14.0 %collective-permute-start.5 = (bf16[1,2,32,1280]{3,2,1,0:T(8,128)(2,1)S(1)}, bf16[1,2,32,1280]{3,2,1,0:T(8,128)(2,1)S(1)}, u32[]{:S(2)}, u32[]{:S(2)}) collective-permute-start(bf16[1,2,32,1280]{3,2,1,0:T(8,128)(2,1)S(1)} %get-tuple-element.21), channel_id=1, source_target_pairs={{0,24},{8,16},{16,8},{24,0},{1,25},{9,17},{17,9},{25,1},{2,26},{10... | collective-permute-start | bytes 491528 | tf_op jit(solution)/shard_map/ppermute | solution.py:46

commit v2 on v1

--- a/solution.py
+++ b/solution.py
@@ -16,6 +16,8 @@
 WIN = 256
 F32 = jnp.float32
 BF16 = jnp.bfloat16
+FRONT_FLOPS = 12 * 10**9
+UNPACK_FLOPS = 10**10
 
 
 def paired(size):
@@ -36,7 +38,9 @@
 
 def pieces(size, shape, dtype):
     if paired(size):
-        return [jax.ShapeDtypeStruct((1, *shape), dtype)] * size
+        return [pltpu.HBM((1, *shape), dtype)] + [
+            jax.ShapeDtypeStruct((1, *shape), dtype)
+        ] * (size - 1)
     return [jax.ShapeDtypeStruct((size, *shape), dtype)]
 
 
@@ -49,17 +53,12 @@
     return [lax.all_to_all(arrays[0], axis, split_axis=0, concat_axis=0, tiled=True)]
 
 
-def total(terms, sizes):
-    dp, ctx = sizes
-    if not (paired(dp) and paired(ctx)):
-        return lax.psum(terms, ("dp", "ctx"))
-    rounds = [("ctx", ctx, (1,)), ("ctx", ctx, range(2, ctx, 2)), ("dp", dp, range(1, dp))]
-    for axis, size, slots in rounds:
-        others = [
-            lax.ppermute(terms, axis, [(i, i ^ slot) for i in range(size)]) for slot in slots
-        ]
-        for other in others:
-            terms = terms + other
+def spread(terms, axis, size, slots):
+    others = [
+        lax.ppermute(terms, axis, [(i, i ^ slot) for i in range(size)]) for slot in slots
+    ]
+    for other in others:
+        terms = terms + other
     return terms
 
 
@@ -119,35 +118,24 @@
     return lax.broadcasted_iota(jnp.int32, shape, dim)
 
 
-def block_kernel(sizes, capacity, *refs):
-    ranks, owners = sizes
+def front_kernel(sizes, capacity, *refs):
+    ranks = sizes[0]
     n_in = ranks if paired(ranks) else 1
-    where, counts, labels, positions, params, wq_far, wo_far = refs[:7]
-    refs = refs[7:]
-    arrived, refs = refs[:n_in], refs[n_in:]
-    grads, refs = refs[0], refs[1:]
-    back, refs = refs[:n_in], refs[n_in:]
-    windows, terms, xs, qs, ks, vs, ats, ps, dqs, dks, dvs, gs, ws, rows_out, wq, wo, sems = refs
-    ln_gain, ln_bias, merge_gain, merge_bias = (params[i : i + 1, :] for i in range(4))
+    where, counts, ln_gain, ln_bias, wq_far = refs[:5]
+    arrived, refs = refs[5 : 5 + n_in], refs[5 + n_in :]
+    xs, normed_ref, inverse_ref, qs, ks, vs, wq, sems = refs
     rows, width = xs.shape
     units = rows // UNIT
-    inner = wo.shape[0]
-    heads = inner // HEAD
-    scale = HEAD ** (-0.5)
-    tokens = rows // MERGE
+    inner = wq.shape[0] // 3
     thirds = [slice(part * inner, (part + 1) * inner) for part in range(3)]
     loads = [
         pltpu.make_async_copy(wq_far.at[third], wq.at[third], sems.at[part])
         for part, third in enumerate(thirds)
     ]
-    loads.append(pltpu.make_async_copy(wo_far, wo, sems.at[3]))
     for load in loads:
         load.start()
-    pair = grads.shape[1]
-    slots = owners * pair
-    me, column = where[0], where[1]
+    me = where[0]
     begin = starts(counts, ranks)
-
     for unit in range(units):
         wanted = unit * ranks + me
         sender = jnp.int32(0)
@@ -156,13 +144,50 @@
         kth = (wanted - chosen(begin, sender)) // ranks
         span = slice(unit * UNIT, (unit + 1) * UNIT)
         if n_in == 1:
-            xs[span, :] = arrived[0][sender, kth].astype(F32)
+            xs[span, :] = arrived[0][sender, kth]
         else:
             slot = sender ^ me
             value = arrived[0][0, kth]
             for i in range(1, n_in):
                 value = jnp.where(slot == i, arrived[i][0, kth], value)
-            xs[span, :] = value.astype(F32)
+            xs[span, :] = value
+    normed, inverse = moments(xs[...].astype(F32))
+    normed_ref[...] = normed
+    inverse_ref[...] = jnp.broadcast_to(inverse, inverse_ref.shape)
+    gain, bias = ln_gain[...].reshape(1, width), ln_bias[...].reshape(1, width)
+    shifted = (normed * gain + bias).astype(BF16)
+    for ref, part in ((qs, 0), (ks, 1), (vs, 2)):
+        ref[:, inner:] = jnp.zeros((rows, ref.shape[1] - inner), BF16)
+        loads[part].wait()
+        ref[:, :inner] = dot(shifted, wq[thirds[part], :], 1, 1).astype(BF16)
+
+
+def block_kernel(sizes, capacity, *refs):
+    ranks, owners = sizes
+    n_in = ranks if paired(ranks) else 1
+    where, counts, labels, positions, *params, wq_far, wo_far = refs[:9]
+    xs, normed_ref, inverse_ref, qs, ks, vs, grads = refs[9:16]
+    refs = refs[16:]
+    back, refs = refs[:n_in], refs[n_in:]
+    windows, terms_out, ats, ps, dqs, dks, dvs, gs, ws, rows_out, terms, wq, wo, sems = refs
+    rows, width = xs.shape
+    ln_gain, merge_gain, merge_bias = (ref[...].reshape(1, width) for ref in params)
+    units = rows // UNIT
+    inner = wo.shape[0]
+    heads = inner // HEAD
+    scale = HEAD ** (-0.5)
+    tokens = rows // MERGE
+    loads = [
+        pltpu.make_async_copy(wo_far, wo, sems.at[0]),
+        pltpu.make_async_copy(wq_far, wq, sems.at[1]),
+    ]
+    for load in loads:
+        load.start()
+    pair = grads.shape[1]
+    slots = owners * pair
+    me, column = where[0], where[1]
+    begin = starts(counts, ranks)
+    normed_in, inverse_in = normed_ref[...], inverse_ref[:, :1]
 
     label = jnp.broadcast_to(labels[...].astype(F32), (rows, rows))
     joined = (label == label.T) & (
@@ -188,16 +213,7 @@
         (iota((MERGE * slots, rows), 1) % MERGE == lead // slots) & (slot_place(lead) == spot_row)
     ).astype(BF16)
 
-    normed_in, inverse_in = moments(xs[...])
-    shifted = (normed_in * ln_gain + ln_bias).astype(BF16)
-    padded = qs.shape[1]
-    zero = jnp.zeros((rows, padded - inner), BF16)
-    for ref, part in ((qs, 0), (ks, 1), (vs, 2)):
-        loads[part].wait()
-        ref[:, :inner] = dot(shifted, wq[thirds[part], :], 1, 1).astype(BF16)
-    qs[:, inner:] = zero
-    ks[:, inner:] = zero
-    vs[:, inner:] = zero
+    zero = jnp.zeros((rows, gs.shape[1] - inner), BF16)
     ats[...] = jnp.zeros_like(ats)
     dqs[...] = jnp.zeros_like(dqs)
     dks[...] = jnp.zeros_like(dks)
@@ -220,8 +236,8 @@
         prob = raised / jnp.sum(raised, axis=-1, keepdims=True)
         ps[head] = prob
         ats[:, span] += dot(prob.astype(BF16), jnp.where(mask, vs[:, span], none))
-    loads[3].wait()
-    hidden = xs[...] + dot(ats[:, :inner].astype(BF16), wo[...])
+    loads[0].wait()
+    hidden = xs[...].astype(F32) + dot(ats[:, :inner].astype(BF16), wo[...])
     normed_out, inverse_out = moments(hidden)
     result = (normed_out * merge_gain + merge_bias).astype(BF16)
     ws[...] = dot(put, result)
@@ -254,14 +270,23 @@
         score_grad = (prob * centred * scale).astype(BF16)
         dqs[:, span] += dot(score_grad, jnp.where(mask, ks[:, span], none))
         dks[:, span] += dot(score_grad, jnp.where(mask, qs[:, span], none), 0, 0)
+    loads[1].wait()
     input_grad = sum(
-        dot(ref[:, :inner].astype(BF16), wq[thirds[part], :])
+        dot(ref[:, :inner].astype(BF16), wq[part * inner : (part + 1) * inner, :])
         for ref, part in ((dqs, 0), (dks, 1), (dvs, 2))
     )
     terms[0:1, :] = jnp.sum(input_grad * normed_in, axis=0, keepdims=True)
     terms[1:2, :] = jnp.sum(input_grad, axis=0, keepdims=True)
     row_grad = hidden_grad + norm_back(input_grad * ln_gain, normed_in, inverse_in)
     rows_out[...] = row_grad.astype(BF16).reshape(units, UNIT, width)
+
+    terms_out[...] = terms[...]
+    spare = windows.shape[2] - MERGE * width
+    if spare:
+        high = terms[...].astype(BF16)
+        low = (terms[...] - high.astype(F32)).astype(BF16)
+        for owner in range(owners):
+            windows[owner, :, MERGE * width :] = jnp.concatenate([high, low], axis=0)
 
     for slot in range(ranks):
         array, entry = place(slot, ranks)
@@ -326,7 +351,10 @@
     anywhere = pl.BlockSpec(memory_space=pl.ANY)
 
     block_shapes = pieces(ranks, (capacity, UNIT, width), BF16)
-    window_shape = jax.ShapeDtypeStruct((owners, pair, token_width), BF16)
+    beside = paired(ranks) and paired(owners) and pair == 8
+    window_shape = jax.ShapeDtypeStruct(
+        (owners, pair, token_width + (width if beside else 0)), BF16
+    )
     n_in = len(block_shapes)
     swap = functools.partial(
         lax.all_to_all, axis_name="ctx", split_axis=0, concat_axis=0, tiled=True
@@ -350,6 +378,33 @@
     grad_blocks = merged_grad.reshape(owners, pair, token_width)
     grads = swap(grad_blocks)
 
+    wide = jax.ShapeDtypeStruct((rows, padded), BF16)
+    state = pl.pallas_call(
+        functools.partial(front_kernel, sizes, capacity),
+        out_shape=[
+            jax.ShapeDtypeStruct((rows, width), BF16),
+            jax.ShapeDtypeStruct((rows, width), F32),
+            jax.ShapeDtypeStruct((rows, LANES), F32),
+            wide,
+            wide,
+            wide,
+        ],
+        in_specs=[smem] * 2 + [vmem] * 2 + [anywhere] + [vmem] * n_in,
+        out_specs=[vmem] * 6,
+        scratch_shapes=[
+            pltpu.VMEM((3 * inner, width), BF16),
+            pltpu.SemaphoreType.DMA((3,)),
+        ],
+        compiler_params=pltpu.CompilerParams(vmem_limit_bytes=24 * 2**20),
+        cost_estimate=pl.CostEstimate(
+            flops=FRONT_FLOPS, bytes_accessed=8 * 10**6, transcendentals=0
+        ),
+        name="front",
+    )(
+        *map(in_hbm, (where, counts, ln_gain, ln_bias, qkv_weight.T, arrived[0])),
+        *arrived[1:],
+    )
+
     results = pl.pallas_call(
         functools.partial(block_kernel, sizes, capacity),
         out_shape=[
@@ -357,13 +412,9 @@
             window_shape,
             jax.ShapeDtypeStruct((4, width), F32),
         ],
-        in_specs=[smem, smem] + [vmem] * 3 + [anywhere] * 2 + [vmem] * (n_in + 1),
+        in_specs=[smem] * 2 + [vmem] * 5 + [anywhere] * 2 + [vmem] * 7,
         out_specs=[vmem] * (n_in + 2),
         scratch_shapes=[
-            pltpu.VMEM((rows, width), F32),
-            pltpu.VMEM((rows, padded), BF16),
-            pltpu.VMEM((rows, padded), BF16),
-            pltpu.VMEM((rows, padded), BF16),
             pltpu.VMEM((rows, padded), F32),
             pltpu.VMEM((heads, rows, rows), F32),
             pltpu.VMEM((rows, padded), F32),
@@ -372,38 +423,55 @@
             pltpu.VMEM((rows, padded), BF16),
             pltpu.VMEM((MERGE * owners * pair, width), F32),
             pltpu.VMEM((rows // UNIT, UNIT, width), BF16),
+            pltpu.VMEM((4, width), F32),
             pltpu.VMEM((3 * inner, width), BF16),
             pltpu.VMEM((inner, width), BF16),
-            pltpu.SemaphoreType.DMA((4,)),
+            pltpu.SemaphoreType.DMA((2,)),
         ],
         compiler_params=pltpu.CompilerParams(vmem_limit_bytes=40 * 2**20),
         cost_estimate=pl.CostEstimate(
-            flops=3 * 10**9, bytes_accessed=12 * 10**6, transcendentals=200_000
+            flops=2 * 10**9, bytes_accessed=12 * 10**6, transcendentals=200_000
         ),
         name="block",
     )(
-        in_hbm(where),
-        in_hbm(counts),
-        in_hbm(segment_ids.reshape(1, rows)),
-        in_hbm(merged_position.reshape(1, rows // MERGE)),
-        in_hbm(jnp.stack([ln_gain, ln_bias, merge_gain, merge_bias])),
-        in_hbm(qkv_weight.T),
-        in_hbm(out_weight),
-        in_hbm(arrived[0]),
-        *arrived[1:],
+        *map(
+            in_hbm,
+            (
+                where,
+                counts,
+                segment_ids.reshape(1, rows),
+                merged_position.reshape(1, rows // MERGE),
+                ln_gain,
+                merge_gain,
+                merge_bias,
+                qkv_weight.T,
+                out_weight,
+            ),
+        ),
+        *state,
         grads,
     )
     came_back = exchange(results[:n_in], "dp", ranks)
     merged = swap(results[n_in])
-    norm_grads = total(results[-1], sizes)
     patch_grad = pl.pallas_call(
         functools.partial(unpack_kernel, sizes, capacity),
         out_shape=jax.ShapeDtypeStruct((source_units, UNIT, width), BF16),
         in_specs=[smem, smem] + [vmem] * n_in,
         out_specs=vmem,
         compiler_params=pltpu.CompilerParams(vmem_limit_bytes=8 * 2**20),
+        cost_estimate=pl.CostEstimate(
+            flops=UNPACK_FLOPS, bytes_accessed=10**6, transcendentals=0
+        ),
         name="unpack",
     )(in_hbm(where), in_hbm(counts), in_hbm(came_back[0]), *came_back[1:])
+    if beside:
+        halves = merged[:, :, token_width:].astype(F32)
+        terms = jnp.sum(halves[:, :4] + halves[:, 4:], axis=0)
+        terms, patch_grad = lax.optimization_barrier((terms, patch_grad))
+        norm_grads = spread(terms, "dp", ranks, range(1, ranks))
+        merged = merged[:, :, :token_width]
+    else:
+        norm_grads = lax.psum(results[-1], ("dp", "ctx"))
     return (
         merged.reshape(owner_slots, token_width),
         patch_grad.reshape(source_units * UNIT, width),

time: 74.4 us -> 67.8 us (0.911)
  local copies, waits for them, and re-layouts: 4.95 us -> 0.88 us
  starting transfers between devices: 26.4 us -> 23 us
  Pallas kernels: 18 us -> 20.1 us
    pallas_call x0 -> x1, Pallas kernels: none -> 5.61 us  [per_device(): pl.pallas_call(functools.partial(front_kernel, sizes, capacity), out_shap...]
    pallas_call x1, Pallas kernels: 14.2 us -> 10 us  [per_device(): pl.pallas_call(functools.partial(block_kernel, sizes, capacity), out_shap...]
    ppermute x6, waiting for transfers between devices: 20.7 us -> 16.6 us  [exchange(): lax.ppermute(arrays[slot], axis, [(i, i ^ slot) for i in range(size)])]
    ppermute x7 -> x3, starting transfers between devices: 8.28 us -> 4.45 us  [spread(): lax.ppermute(terms, axis, [(i, i ^ slot) for i in range(size)])]
    all_to_all x1, waiting for transfers between devices: 0.01 us -> 3.02 us  [per_device(): merged = swap(results[n_in])]
    another operation x4 -> x0, local copies, waits for them, and re-layouts: 2.8 us -> none  [per_device(): jnp.stack([ln_gain, ln_bias, merge_gain, merge_bias])]
    unnamed x5 -> x0, local copies, waits for them, and re-layouts: 2.15 us -> none
    ppermute x6, starting transfers between devices: 8.77 us -> 10.9 us  [exchange(): lax.ppermute(arrays[slot], axis, [(i, i ^ slot) for i in range(size)])]
  transfers between devices with their start and end apart: 15 -> 11, of which waited for: 5 -> 6; matrix products, arithmetic and copies ran while one was open for 6% -> 1% of each run, Pallas kernels for 5% -> 11%
where the time goes in v2:
time: 67.8 us; the launch traced here: 67.4 us
  starting transfers between devices  23 us (34%)
  waiting for transfers between devices  21.4 us (32%)
  Pallas kernels  20.1 us (30%)
  other arithmetic  1.38 us (2%)
  local copies, waits for them, and re-layouts  0.88 us (1%)
  between operations  0.69 us (1%)
    ppermute x6, waiting for transfers between devices, exchange(): lax.ppermute(arrays[slot], axis, [(i, i ^ slot) for i in range(size)])  16.6 us
    ppermute x6, starting transfers between devices, exchange(): lax.ppermute(arrays[slot], axis, [(i, i ^ slot) for i in range(size)])  10.9 us
    pallas_call x1, Pallas kernels, per_device(): pl.pallas_call(functools.partial(block_kernel, sizes, capacity), out_shap...  10 us
    pallas_call x1, Pallas kernels, per_device(): pl.pallas_call(functools.partial(front_kernel, sizes, capacity), out_shap...  5.61 us
    ppermute x3, starting transfers between devices, spread(): lax.ppermute(terms, axis, [(i, i ^ slot) for i in range(size)])  4.45 us
    all_to_all x1, starting transfers between devices, per_device(): grads = swap(grad_blocks)  3.94 us
    all_to_all x1, starting transfers between devices, per_device(): merged = swap(results[n_in])  3.73 us
    all_to_all x1, waiting for transfers between devices, per_device(): merged = swap(results[n_in])  3.02 us
  transfers between devices with their start and end apart: 11, of which 6 were waited for; matrix products, arithmetic and copies ran while one was open for 1% of the time, Pallas kernels for 11%

profile of v2, /device:TPU:0, one launch (start us, length us, event | category | flops | bytes accessed | tf_op | source)
XLA Modules:
  0.0 67.4 jit_solution(4797066424529038912)
XLA Ops:
  0.6 0.7 pad_add_fusion.where.refs_0_
  1.3 2.6 %pack_blocks.1 = (bf16[1,2,32,1280]{3,2,1,0:T(8,128)(2,1)}, bf16[1,2,32,1280]{3,2,1,0:T(8,128)(2,1)S(1)}, bf16[1,2,32,1280]{3,2,1,0:T(8,128)(2,1)S(1)}, bf16[1,2,32,1280]{3,2,1,0:T(8,128)(2,1)S(1)}) custom-call(s32[2]{0:T(128)} %pad_add_fusion.where.refs_0_, s32[4]{0:T(128)} %bitcast.15, bf16[8,32,1280]{2,1,0:T(8,128)(2,1)} %bitcast.13), custom_call_target="tpu_custom_call" | custom-call | tf_op jit(solution)/shard_map/pack_blocks/pallas_call | solution.py:363
  3.9 3.1 %collective-permute-start = (bf16[1,2,32,1280]{3,2,1,0:T(8,128)(2,1)S(1)}, bf16[1,2,32,1280]{3,2,1,0:T(8,128)(2,1)S(1)}, u32[]{:S(2)}, u32[]{:S(2)}) collective-permute-start(bf16[1,2,32,1280]{3,2,1,0:T(8,128)(2,1)S(1)} %get-tuple-element.21), channel_id=1, source_target_pairs={{0,8},{8,0},{16,24},{24,16},{1,9},{9,1},{17,25},{25,17},{2,10},{10... | collective-permute-start | bytes 491528 | tf_op jit(solution)/shard_map/ppermute | solution.py:50
  7.0 2.6 %collective-permute-start.1 = (bf16[1,2,32,1280]{3,2,1,0:T(8,128)(2,1)S(1)}, bf16[1,2,32,1280]{3,2,1,0:T(8,128)(2,1)S(1)}, u32[]{:S(2)}, u32[]{:S(2)}) collective-permute-start(bf16[1,2,32,1280]{3,2,1,0:T(8,128)(2,1)S(1)} %get-tuple-element.22), channel_id=1, source_target_pairs={{0,16},{8,24},{16,0},{24,8},{1,17},{9,25},{17,1},{25,9},{2,18},{10... | collective-permute-start | bytes 491528 | tf_op jit(solution)/shard_map/ppermute | solution.py:50
  9.6 0.0 collective-permute-start.2
  9.6 3.9 %all-to-all-start = ((bf16[8,8,5120]{2,1,0:T(8,128)(2,1)}), bf16[8,8,5120]{2,1,0:T(8,128)(2,1)S(1)}, u32[]{:S(2)}, u32[]{:S(2)}) async-start(bf16[8,8,5120]{2,1,0:T(8,128)(2,1)} %bitcast.14), calls=%async_computation | async-start | bytes 1310720 | tf_op jit(solution)/shard_map/all_to_all | solution.py:379
  13.5 0.1 collective-permute-done.refs_6_
  13.7 8.4 %collective-permute-done.1.refs_7_ = bf16[1,2,32,1280]{3,2,1,0:T(8,128)(2,1)S(1)} collective-permute-done((bf16[1,2,32,1280]{3,2,1,0:T(8,128)(2,1)S(1)}, bf16[1,2,32,1280]{3,2,1,0:T(8,128)(2,1)S(1)}, u32[]{:S(2)}, u32[]{:S(2)}) %collective-permute-start.1) | collective-permute-done | bytes 163872 | tf_op jit(solution)/shard_map/ppermute | solution.py:50
  22.0 0.0 collective-permute-done.2.refs_8_
  22.0 5.6 %front.1 = (bf16[128,1280]{1,0:T(8,128)(2,1)S(1)}, f32[128,1280]{1,0:T(8,128)S(1)}, f32[128,128]{1,0:T(8,128)S(1)}, bf16[128,1024]{1,0:T(8,128)(2,1)S(1)}, bf16[...) custom-call(s32[2]{0:T(128)} %pad_add_fusion.where.refs_0_, s32[4]{0:T(128)} %bitcast.16, f32[1280]{0:T(1024)} %refs_4_.1, ...), custom_call_target="tpu_custom_call" | custom-call | flops 12000000000 | bytes 8000000 | tf_op jit(solution)/shard_map/front/pallas_call | solution.py:382
  27.7 0.0 all-to-all-done.refs_15_
  27.7 10.0 %block.1 = (bf16[1,2,32,1280]{3,2,1,0:T(8,128)(2,1)}, bf16[1,2,32,1280]{3,2,1,0:T(8,128)(2,1)S(1)}, bf16[1,2,32,1280]{3,2,1,0:T(8,128)(2,1)S(1)}, bf16[1,2,32,12...) custom-call(s32[2]{0:T(128)} %pad_add_fusion.where.refs_0_, s32[4]{0:T(128)} %bitcast.17, ...), custom_call_target="tpu_custom_call" | custom-call | flops 2000000000 | bytes 12000000 | tf_op jit(solution)/shard_map/block/pallas_call | solution.py:408
  37.7 2.7 %collective-permute-start.3 = (bf16[1,2,32,1280]{3,2,1,0:T(8,128)(2,1)S(1)}, bf16[1,2,32,1280]{3,2,1,0:T(8,128)(2,1)S(1)}, u32[]{:S(2)}, u32[]{:S(2)}) collective-permute-start(bf16[1,2,32,1280]{3,2,1,0:T(8,128)(2,1)S(1)} %get-tuple-element.32), channel_id=1, source_target_pairs={{0,8},{8,0},{16,24},{24,16},{1,9},{9,1},{17,25},{25,17},{2,10},{10... | collective-permute-start | bytes 491528 | tf_op jit(solution)/shard_map/ppermute | solution.py:50
  40.4 1.1 %collective-permute-start.4 = (bf16[1,2,32,1280]{3,2,1,0:T(8,128)(2,1)S(1)}, bf16[1,2,32,1280]{3,2,1,0:T(8,128)(2,1)S(1)}, u32[]{:S(2)}, u32[]{:S(2)}) collective-permute-start(bf16[1,2,32,1280]{3,2,1,0:T(8,128)(2,1)S(1)} %get-tuple-element.33), channel_id=1, source_target_pairs={{0,16},{8,24},{16,0},{24,8},{1,17},{9,25},{17,1},{25,9},{2,18},{10... | collective-permute-start | bytes 491528 | tf_op jit(solution)/shard_map/ppermute | solution.py:50
  41.5 1.4 %collective-permute-start.5 = (bf16[1,2,32,1280]{3,2,1,0:T(8,128)(2,1)S(1)}, bf16[1,2,32,1280]{3,2,1,0:T(8,128)(2,1)S(1)}, u32[]{:S(2)}, u32[]{:S(2)}) collective-permute-start(bf16[1,2,32,1280]{3,2,1,0:T(8,128)(2,1)S(1)} %get-tuple-element.34), channel_id=1, source_target_pairs={{0,24},{8,16},{16,8},{24,0},{1,25},{9,17},{17,9},{25,1},{2,26},{10... | collective-permute-start | bytes 491528 | tf_op jit(solution)/shard_map/ppermute | solution.py:50
  42.9 3.7 %all-to-all-start.1 = ((bf16[8,8,6400]{2,1,0:T(8,128)(2,1)}), bf16[8,8,6400]{2,1,0:T(8,128)(2,1)S(1)}, u32[]{:S(2)}, u32[]{:S(2)}) async-start(bf16[8,8,6400]{2,1,0:T(8,128)(2,1)} %get-tuple-element.30), calls=%async_computation.1 | async-start | bytes 1638400 | tf_op jit(solution)/shard_map/all_to_all | solution.py:455
  46.6 0.0 collective-permute-done.3.refs_3_
  46.6 8.0 %collective-permute-done.4.refs_4_ = bf16[1,2,32,1280]{3,2,1,0:T(8,128)(2,1)S(1)} collective-permute-done((bf16[1,2,32,1280]{3,2,1,0:T(8,128)(2,1)S(1)}, bf16[1,2,32,1280]{3,2,1,0:T(8,128)(2,1)S(1)}, u32[]{:S(2)}, u32[]{:S(2)}) %collective-permute-start.4) | collective-permute-done | bytes 163872 | tf_op jit(solution)/shard_map/ppermute | solution.py:50
  54.6 0.0 collective-permute-done.5.refs_5_
  54.6 1.9 %unpack.1 = bf16[8,32,1280]{2,1,0:T(8,128)(2,1)} custom-call(s32[2]{0:T(128)} %pad_add_fusion.where.refs_0_, s32[4]{0:T(128)} %bitcast.18, bf16[1,2,32,1280]{3,2,1,0:T(8,128)(2,1)} %get-tuple-element.31.refs_2_, bf16[1,2,32,1280]{3,2,1,0:T(8,128)(2,1)S(1)} %collective-permute-done.3.refs_3_, bf16[1,2,32,1280]{3,2,1,0:T(8,128)(2,1)S(1)} %collective-permute-done.4.refs_4_, ...), custom_call_target="tpu_custom_call" | custom-call | flops 10000000000 | bytes 1000000 | tf_op jit(solution)/shard_map/unpack/pallas_call | solution.py:456
  56.5 3.0 %all-to-all-done.1 = bf16[8,8,6400]{2,1,0:T(8,128)(2,1)S(1)} async-done(((bf16[8,8,6400]{2,1,0:T(8,128)(2,1)}), bf16[8,8,6400]{2,1,0:T(8,128)(2,1)S(1)}, u32[]{:S(2)}, u32[]{:S(2)}) %all-to-all-start.1) | async-done | bytes 819232 | tf_op jit(solution)/shard_map/all_to_all | solution.py:455
  59.6 0.1 fusion
  59.6 2.5 %collective-permute-start.8 = (f32[4,1280]{1,0:T(4,128)S(1)}, f32[4,1280]{1,0:T(4,128)S(1)}, u32[]{:S(2)}, u32[]{:S(2)}) collective-permute-start(f32[4,1280]{1,0:T(4,128)S(1)} %fusion), channel_id=1, source_target_pairs={{0,24},{8,16},{16,8},{24,0},{1,25},{9,17},{17,9},{25,1},{2,26},{10... | collective-permute-start | bytes 61448 | tf_op jit(solution)/shard_map/ppermute | solution.py:58
  62.1 0.0 collective-permute-start.7
  62.2 1.9 %collective-permute-start.6 = (f32[4,1280]{1,0:T(4,128)S(1)}, f32[4,1280]{1,0:T(4,128)S(1)}, u32[]{:S(2)}, u32[]{:S(2)}) collective-permute-start(f32[4,1280]{1,0:T(4,128)S(1)} %fusion), channel_id=1, source_target_pairs={{0,8},{8,0},{16,24},{24,16},{1,9},{9,1},{17,25},{25,17},{2,10},{10... | collective-permute-start | bytes 61448 | tf_op jit(solution)/shard_map/ppermute | solution.py:58
  64.1 0.9 %slice_bitcast_fusion = bf16[64,5120]{1,0:T(8,128)(2,1)} fusion(bf16[8,8,6400]{2,1,0:T(8,128)(2,1)S(1)} %all-to-all-done.1), kind=kLoop, calls=%fused_computation | loop fusion | bytes 1310720 | tf_op jit(solution)/shard_map/reshape | solution.py:476
  65.0 0.3 collective-permute-done.8
  65.3 1.5 %collective-permute-done.7 = f32[4,1280]{1,0:T(4,128)S(1)} collective-permute-done((f32[4,1280]{1,0:T(4,128)S(1)}, f32[4,1280]{1,0:T(4,128)S(1)}, u32[]{:S(2)}, u32[]{:S(2)}) %collective-permute-start.7) | collective-permute-done | bytes 20512 | tf_op jit(solution)/shard_map/ppermute | solution.py:58
  66.8 0.0 collective-permute-done.6
  66.8 0.6 add_add_fusion
  (1 shorter events, 0.0 us)
Async XLA Ops:
  3.9 9.8 %collective-permute-start = (bf16[1,2,32,1280]{3,2,1,0:T(8,128)(2,1)S(1)}, bf16[1,2,32,1280]{3,2,1,0:T(8,128)(2,1)S(1)}, u32[]{:S(2)}, u32[]{:S(2)}) collective-permute-start(bf16[1,2,32,1280]{3,2,1,0:T(8,128)(2,1)S(1)} %get-tuple-element.21), channel_id=1, source_target_pairs={{0,8},{8,0},{16,24},{24,16},{1,9},{9,1},{17,25},{25,17},{2,10},{10... | collective-permute-start | bytes 491528 | tf_op jit(solution)/shard_map/ppermute | solution.py:50
  7.0 15.0 %collective-permute-start.1 = (bf16[1,2,32,1280]{3,2,1,0:T(8,128)(2,1)S(1)}, bf16[1,2,32,1280]{3,2,1,0:T(8,128)(2,1)S(1)}, u32[]{:S(2)}, u32[]{:S(2)}) collective-permute-start(bf16[1,2,32,1280]{3,2,1,0:T(8,128)(2,1)S(1)} %get-tuple-element.22), channel_id=1, source_target_pairs={{0,16},{8,24},{16,0},{24,8},{1,17},{9,25},{17,1},{25,9},{2,18},{10... | collective-permute-start | bytes 491528 | tf_op jit(solution)/shard_map/ppermute | solution.py:50
  9.6 12.5 %collective-permute-start.2 = (bf16[1,2,32,1280]{3,2,1,0:T(8,128)(2,1)S(1)}, bf16[1,2,32,1280]{3,2,1,0:T(8,128)(2,1)S(1)}, u32[]{:S(2)}, u32[]{:S(2)}) collective-permute-start(bf16[1,2,32,1280]{3,2,1,0:T(8,128)(2,1)S(1)} %get-tuple-element.23), channel_id=1, source_target_pairs={{0,24},{8,16},{16,8},{24,0},{1,25},{9,17},{17,9},{25,1},{2,26},{10... | collective-permute-start | bytes 491528 | tf_op jit(solution)/shard_map/ppermute | solution.py:50
  9.6 18.1 %all-to-all-start = ((bf16[8,8,5120]{2,1,0:T(8,128)(2,1)}), bf16[8,8,5120]{2,1,0:T(8,128)(2,1)S(1)}, u32[]{:S(2)}, u32[]{:S(2)}) async-start(bf16[8,8,5120]{2,1,0:T(8,128)(2,1)} %bitcast.14), calls=%async_computation | async-start | bytes 1310720 | tf_op jit(solution)/shard_map/all_to_all | solution.py:379
  37.7 8.9 %collective-permute-start.3 = (bf16[1,2,32,1280]{3,2,1,0:T(8,128)(2,1)S(1)}, bf16[1,2,32,1280]{3,2,1,0:T(8,128)(2,1)S(1)}, u32[]{:S(2)}, u32[]{:S(2)}) collective-permute-start(bf16[1,2,32,1280]{3,2,1,0:T(8,128)(2,1)S(1)} %get-tuple-element.32), channel_id=1, source_target_pairs={{0,8},{8,0},{16,24},{24,16},{1,9},{9,1},{17,25},{25,17},{2,10},{10... | collective-permute-start | bytes 491528 | tf_op jit(solution)/shard_map/ppermute | solution.py:50
  40.4 14.2 %collective-permute-start.4 = (bf16[1,2,32,1280]{3,2,1,0:T(8,128)(2,1)S(1)}, bf16[1,2,32,1280]{3,2,1,0:T(8,128)(2,1)S(1)}, u32[]{:S(2)}, u32[]{:S(2)}) collective-permute-start(bf16[1,2,32,1280]{3,2,1,0:T(8,128)(2,1)S(1)} %get-tuple-element.33), channel_id=1, source_target_pairs={{0,16},{8,24},{16,0},{24,8},{1,17},{9,25},{17,1},{25,9},{2,18},{10... | collective-permute-start | bytes 491528 | tf_op jit(solution)/shard_map/ppermute | solution.py:50
  41.5 13.2 %collective-permute-start.5 = (bf16[1,2,32,1280]{3,2,1,0:T(8,128)(2,1)S(1)}, bf16[1,2,32,1280]{3,2,1,0:T(8,128)(2,1)S(1)}, u32[]{:S(2)}, u32[]{:S(2)}) collective-permute-start(bf16[1,2,32,1280]{3,2,1,0:T(8,128)(2,1)S(1)} %get-tuple-element.34), channel_id=1, source_target_pairs={{0,24},{8,16},{16,8},{24,0},{1,25},{9,17},{17,9},{25,1},{2,26},{10... | collective-permute-start | bytes 491528 | tf_op jit(solution)/shard_map/ppermute | solution.py:50
  42.9 16.7 %all-to-all-start.1 = ((bf16[8,8,6400]{2,1,0:T(8,128)(2,1)}), bf16[8,8,6400]{2,1,0:T(8,128)(2,1)S(1)}, u32[]{:S(2)}, u32[]{:S(2)}) async-start(bf16[8,8,6400]{2,1,0:T(8,128)(2,1)} %get-tuple-element.30), calls=%async_computation.1 | async-start | bytes 1638400 | tf_op jit(solution)/shard_map/all_to_all | solution.py:455
  59.6 5.6 %collective-permute-start.8 = (f32[4,1280]{1,0:T(4,128)S(1)}, f32[4,1280]{1,0:T(4,128)S(1)}, u32[]{:S(2)}, u32[]{:S(2)}) collective-permute-start(f32[4,1280]{1,0:T(4,128)S(1)} %fusion), channel_id=1, source_target_pairs={{0,24},{8,16},{16,8},{24,0},{1,25},{9,17},{17,9},{25,1},{2,26},{10... | collective-permute-start | bytes 61448 | tf_op jit(solution)/shard_map/ppermute | solution.py:58
  62.1 4.7 %collective-permute-start.7 = (f32[4,1280]{1,0:T(4,128)S(1)}, f32[4,1280]{1,0:T(4,128)S(1)}, u32[]{:S(2)}, u32[]{:S(2)}) collective-permute-start(f32[4,1280]{1,0:T(4,128)S(1)} %fusion), channel_id=1, source_target_pairs={{0,16},{8,24},{16,0},{24,8},{1,17},{9,25},{17,1},{25,9},{2,18},{10... | collective-permute-start | bytes 61448 | tf_op jit(solution)/shard_map/ppermute | solution.py:58
  62.2 4.6 %collective-permute-start.6 = (f32[4,1280]{1,0:T(4,128)S(1)}, f32[4,1280]{1,0:T(4,128)S(1)}, u32[]{:S(2)}, u32[]{:S(2)}) collective-permute-start(f32[4,1280]{1,0:T(4,128)S(1)} %fusion), channel_id=1, source_target_pairs={{0,8},{8,0},{16,24},{24,16},{1,9},{9,1},{17,25},{25,17},{2,10},{10... | collective-permute-start | bytes 61448 | tf_op jit(solution)/shard_map/ppermute | solution.py:58

commit v3 on v2

--- a/solution.py
+++ b/solution.py
@@ -17,6 +17,8 @@
 F32 = jnp.float32
 BF16 = jnp.bfloat16
 FRONT_FLOPS = 12 * 10**9
+HOLD_PARTS = 6
+HOLD_FLOPS = 10**8
 UNPACK_FLOPS = 10**10
 
 
@@ -76,10 +78,10 @@
     return out
 
 
-def pack_blocks(sizes, capacity, where, counts, source, *rest):
+def pack_blocks(sizes, capacity, counts, source, *rest):
     ranks = sizes[0]
     outs, sems = rest[:-1], rest[-1]
-    me = where[0]
+    me = lax.axis_index("dp")
     first = chosen(starts(counts, ranks), me)
     copies = []
     for slot in range(ranks):
@@ -97,6 +99,20 @@
         copy.wait()
 
 
+def hold(far, near, sems):
+    count = sems.shape[0]
+    step = far.shape[0] // count
+    spans = [slice(i * step, (i + 1) * step) for i in range(count)]
+    copies = [
+        pltpu.make_async_copy(far.at[span], near.at[span], sems.at[i])
+        for i, span in enumerate(spans)
+    ]
+    for copy in copies:
+        copy.start()
+    for copy in copies:
+        copy.wait()
+
+
 def moments(values):
     average = jnp.mean(values, axis=-1, keepdims=True)
     centred = values - average
@@ -121,20 +137,14 @@
 def front_kernel(sizes, capacity, *refs):
     ranks = sizes[0]
     n_in = ranks if paired(ranks) else 1
-    where, counts, ln_gain, ln_bias, wq_far = refs[:5]
-    arrived, refs = refs[5 : 5 + n_in], refs[5 + n_in :]
-    xs, normed_ref, inverse_ref, qs, ks, vs, wq, sems = refs
+    counts, ln_gain, ln_bias, wq = refs[:4]
+    arrived, refs = refs[4 : 4 + n_in], refs[4 + n_in :]
+    xs, normed_ref, inverse_ref, qs, ks, vs = refs
     rows, width = xs.shape
     units = rows // UNIT
     inner = wq.shape[0] // 3
     thirds = [slice(part * inner, (part + 1) * inner) for part in range(3)]
-    loads = [
-        pltpu.make_async_copy(wq_far.at[third], wq.at[third], sems.at[part])
-        for part, third in enumerate(thirds)
-    ]
-    for load in loads:
-        load.start()
-    me = where[0]
+    me = lax.axis_index("dp")
     begin = starts(counts, ranks)
     for unit in range(units):
         wanted = unit * ranks + me
@@ -158,16 +168,15 @@
     shifted = (normed * gain + bias).astype(BF16)
     for ref, part in ((qs, 0), (ks, 1), (vs, 2)):
         ref[:, inner:] = jnp.zeros((rows, ref.shape[1] - inner), BF16)
-        loads[part].wait()
         ref[:, :inner] = dot(shifted, wq[thirds[part], :], 1, 1).astype(BF16)
 
 
 def block_kernel(sizes, capacity, *refs):
     ranks, owners = sizes
     n_in = ranks if paired(ranks) else 1
-    where, counts, labels, positions, *params, wq_far, wo_far = refs[:9]
-    xs, normed_ref, inverse_ref, qs, ks, vs, grads = refs[9:16]
-    refs = refs[16:]
+    counts, labels, positions, *params, wq_far, wo_far = refs[:8]
+    xs, normed_ref, inverse_ref, qs, ks, vs, grads = refs[8:15]
+    refs = refs[15:]
     back, refs = refs[:n_in], refs[n_in:]
     windows, terms_out, ats, ps, dqs, dks, dvs, gs, ws, rows_out, terms, wq, wo, sems = refs
     rows, width = xs.shape
@@ -177,15 +186,13 @@
     heads = inner // HEAD
     scale = HEAD ** (-0.5)
     tokens = rows // MERGE
-    loads = [
-        pltpu.make_async_copy(wo_far, wo, sems.at[0]),
-        pltpu.make_async_copy(wq_far, wq, sems.at[1]),
-    ]
-    for load in loads:
-        load.start()
+    load_out = pltpu.make_async_copy(wo_far, wo, sems.at[0])
+    load_qkv = pltpu.make_async_copy(wq_far, wq, sems.at[1])
+    load_out.start()
+    load_qkv.start()
     pair = grads.shape[1]
     slots = owners * pair
-    me, column = where[0], where[1]
+    me, column = lax.axis_index("dp"), lax.axis_index("ctx")
     begin = starts(counts, ranks)
     normed_in, inverse_in = normed_ref[...], inverse_ref[:, :1]
 
@@ -220,23 +227,33 @@
     dvs[...] = jnp.zeros_like(dvs)
 
     win_lane = iota((rows, WIN), 1)
-
-    def window(head):
-        at = head * HEAD
+    none = jnp.zeros((), BF16)
+
+    def window(two):
+        at = 2 * two * HEAD
         low = at // LANES * LANES
-        mask = (win_lane >= at - low) & (win_lane < at - low + HEAD)
-        return slice(low, low + WIN), mask
-
-    none = jnp.zeros((), BF16)
-    for head in range(heads):
-        span, mask = window(head)
-        scores = dot(jnp.where(mask, qs[:, span], none), ks[:, span], 1, 1) * scale
-        scores = jnp.where(joined, scores, NEG)
-        raised = jnp.exp(scores - jnp.max(scores, axis=-1, keepdims=True))
-        prob = raised / jnp.sum(raised, axis=-1, keepdims=True)
-        ps[head] = prob
-        ats[:, span] += dot(prob.astype(BF16), jnp.where(mask, vs[:, span], none))
-    loads[0].wait()
+        first = (win_lane >= at - low) & (win_lane < at - low + HEAD)
+        second = (win_lane >= at - low + HEAD) & (win_lane < at - low + 2 * HEAD)
+        return slice(low, low + WIN), first, second
+
+    def stacked(value, first, second):
+        return jnp.concatenate(
+            [jnp.where(first, value, none), jnp.where(second, value, none)], axis=0
+        )
+
+    def own_part(value, first, second):
+        return jnp.where(first, value[:rows], jnp.where(second, value[rows:], 0.0))
+
+    for two in range(heads // 2):
+        span, first, second = window(two)
+        scores = dot(qs[:, span], stacked(ks[:, span], first, second), 1, 1) * scale
+        for side in range(2):
+            half = slice(side * rows, (side + 1) * rows)
+            score = jnp.where(joined, scores[:, half], NEG)
+            raised = jnp.exp(score - jnp.max(score, axis=-1, keepdims=True))
+            ps[two, :, half] = raised / jnp.sum(raised, axis=-1, keepdims=True)
+        ats[:, span] += dot(ps[two].astype(BF16), stacked(vs[:, span], first, second))
+    load_out.wait()
     hidden = xs[...].astype(F32) + dot(ats[:, :inner].astype(BF16), wo[...])
     normed_out, inverse_out = moments(hidden)
     result = (normed_out * merge_gain + merge_bias).astype(BF16)
@@ -260,17 +277,21 @@
     hidden_grad = norm_back(upstream * merge_gain, normed_out, inverse_out)
     gs[:, :inner] = dot(hidden_grad.astype(BF16), wo[...], 1, 1).astype(BF16)
     gs[:, inner:] = zero
-    for head in range(heads):
-        span, mask = window(head)
-        prob = ps[head]
-        grad = jnp.where(mask, gs[:, span], none)
-        prob_grad = dot(grad, vs[:, span], 1, 1)
-        dvs[:, span] += dot(prob.astype(BF16), grad, 0, 0)
-        centred = prob_grad - jnp.sum(prob * prob_grad, axis=-1, keepdims=True)
-        score_grad = (prob * centred * scale).astype(BF16)
-        dqs[:, span] += dot(score_grad, jnp.where(mask, ks[:, span], none))
-        dks[:, span] += dot(score_grad, jnp.where(mask, qs[:, span], none), 0, 0)
-    loads[1].wait()
+    for two in range(heads // 2):
+        span, first, second = window(two)
+        prob = ps[two]
+        grad = gs[:, span]
+        prob_grad = dot(grad, stacked(vs[:, span], first, second), 1, 1)
+        dvs[:, span] += own_part(dot(prob.astype(BF16), grad, 0, 0), first, second)
+        weighted = prob * prob_grad
+        centred = [
+            prob_grad[:, half] - jnp.sum(weighted[:, half], axis=-1, keepdims=True)
+            for half in (slice(0, rows), slice(rows, 2 * rows))
+        ]
+        score_grad = (prob * jnp.concatenate(centred, axis=1) * scale).astype(BF16)
+        dqs[:, span] += dot(score_grad, stacked(ks[:, span], first, second))
+        dks[:, span] += own_part(dot(score_grad, qs[:, span], 0, 0), first, second)
+    load_qkv.wait()
     input_grad = sum(
         dot(ref[:, :inner].astype(BF16), wq[part * inner : (part + 1) * inner, :])
         for ref, part in ((dqs, 0), (dks, 1), (dvs, 2))
@@ -300,9 +321,8 @@
 
 def unpack_kernel(sizes, capacity, *refs):
     ranks = sizes[0]
-    where, counts = refs[:2]
-    came, patch_grad = refs[2:-1], refs[-1]
-    me = where[0]
+    counts, *came, patch_grad = refs
+    me = lax.axis_index("dp")
     first = chosen(starts(counts, ranks), me)
     live = chosen([counts[rank] for rank in range(ranks)], me)
     for slot in range(ranks):
@@ -344,7 +364,6 @@
     inner = out_weight.shape[0]
     heads = inner // HEAD
     padded = -(-inner // LANES) * LANES
-    where = jnp.stack([lax.axis_index("dp"), lax.axis_index("ctx")]).astype(jnp.int32)
     counts = unit_counts.reshape(-1)
     smem = pl.BlockSpec(memory_space=pltpu.SMEM)
     vmem = pl.BlockSpec(memory_space=pltpu.VMEM)
@@ -363,13 +382,12 @@
     outgoing = pl.pallas_call(
         functools.partial(pack_blocks, sizes, capacity),
         out_shape=block_shapes,
-        in_specs=[smem, smem, anywhere],
+        in_specs=[smem, anywhere],
         out_specs=[vmem] * n_in,
         scratch_shapes=[pltpu.SemaphoreType.DMA((ranks * capacity,))],
         compiler_params=pltpu.CompilerParams(vmem_limit_bytes=4 * 2**20),
         name="pack_blocks",
     )(
-        in_hbm(where),
         in_hbm(counts),
         in_hbm(patches.reshape(source_units, UNIT, width)),
     )
@@ -377,6 +395,17 @@
 
     grad_blocks = merged_grad.reshape(owners, pair, token_width)
     grads = swap(grad_blocks)
+
+    near = pl.pallas_call(
+        hold,
+        out_shape=pltpu.VMEM(qkv_weight.T.shape, BF16),
+        in_specs=[anywhere],
+        out_specs=vmem,
+        scratch_shapes=[pltpu.SemaphoreType.DMA((HOLD_PARTS,))],
+        compiler_params=pltpu.CompilerParams(vmem_limit_bytes=2**20),
+        cost_estimate=pl.CostEstimate(flops=HOLD_FLOPS, bytes_accessed=10**6, transcendentals=0),
+        name="hold",
+    )(in_hbm(qkv_weight.T))
 
     wide = jax.ShapeDtypeStruct((rows, padded), BF16)
     state = pl.pallas_call(
@@ -389,19 +418,17 @@
             wide,
             wide,
         ],
-        in_specs=[smem] * 2 + [vmem] * 2 + [anywhere] + [vmem] * n_in,
+        in_specs=[smem] + [vmem] * (3 + n_in),
         out_specs=[vmem] * 6,
-        scratch_shapes=[
-            pltpu.VMEM((3 * inner, width), BF16),
-            pltpu.SemaphoreType.DMA((3,)),
-        ],
-        compiler_params=pltpu.CompilerParams(vmem_limit_bytes=24 * 2**20),
+        compiler_params=pltpu.CompilerParams(vmem_limit_bytes=16 * 2**20),
         cost_estimate=pl.CostEstimate(
             flops=FRONT_FLOPS, bytes_accessed=8 * 10**6, transcendentals=0
         ),
         name="front",
     )(
-        *map(in_hbm, (where, counts, ln_gain, ln_bias, qkv_weight.T, arrived[0])),
+        *map(in_hbm, (counts, ln_gain, ln_bias)),
+        near,
+        in_hbm(arrived[0]),
         *arrived[1:],
     )
 
@@ -412,11 +439,11 @@
             window_shape,
             jax.ShapeDtypeStruct((4, width), F32),
         ],
-        in_specs=[smem] * 2 + [vmem] * 5 + [anywhere] * 2 + [vmem] * 7,
+        in_specs=[smem] + [vmem] * 5 + [anywhere] * 2 + [vmem] * 7,
         out_specs=[vmem] * (n_in + 2),
         scratch_shapes=[
             pltpu.VMEM((rows, padded), F32),
-            pltpu.VMEM((heads, rows, rows), F32),
+            pltpu.VMEM((heads // 2, rows, 2 * rows), F32),
             pltpu.VMEM((rows, padded), F32),
             pltpu.VMEM((rows, padded), F32),
             pltpu.VMEM((rows, padded), F32),
@@ -437,7 +464,6 @@
         *map(
             in_hbm,
             (
-                where,
                 counts,
                 segment_ids.reshape(1, rows),
                 merged_position.reshape(1, rows // MERGE),
@@ -456,14 +482,14 @@
     patch_grad = pl.pallas_call(
         functools.partial(unpack_kernel, sizes, capacity),
         out_shape=jax.ShapeDtypeStruct((source_units, UNIT, width), BF16),
-        in_specs=[smem, smem] + [vmem] * n_in,
+        in_specs=[smem] + [vmem] * n_in,
         out_specs=vmem,
         compiler_params=pltpu.CompilerParams(vmem_limit_bytes=8 * 2**20),
         cost_estimate=pl.CostEstimate(
             flops=UNPACK_FLOPS, bytes_accessed=10**6, transcendentals=0
         ),
         name="unpack",
-    )(in_hbm(where), in_hbm(counts), in_hbm(came_back[0]), *came_back[1:])
+    )(in_hbm(counts), in_hbm(came_back[0]), *came_back[1:])
     if beside:
         halves = merged[:, :, token_width:].astype(F32)
         terms = jnp.sum(halves[:, :4] + halves[:, 4:], axis=0)

time: 67.8 us -> 64.8 us (0.956)
  waiting for transfers between devices: 21.4 us -> 19.7 us
  Pallas kernels: 20.1 us -> 19.4 us
    ppermute x6, waiting for transfers between devices: 16.6 us -> 13.4 us  [exchange(): lax.ppermute(arrays[slot], axis, [(i, i ^ slot) for i in range(size)])]
    pallas_call x0 -> x1, Pallas kernels: none -> 3.18 us  [per_device(): pl.pallas_call(hold, out_shape=pltpu.VMEM(qkv_weight.T.shape, BF16), in_s...]
    pallas_call x1, Pallas kernels: 5.61 us -> 3.45 us  [per_device(): pl.pallas_call(functools.partial(front_kernel, sizes, capacity), out_shap...]
    pallas_call x1, Pallas kernels: 10 us -> 8.3 us  [per_device(): pl.pallas_call(functools.partial(block_kernel, sizes, capacity), out_shap...]
    ppermute x3, waiting for transfers between devices: 1.85 us -> 3.31 us  [spread(): lax.ppermute(terms, axis, [(i, i ^ slot) for i in range(size)])]
  transfers between devices with their start and end apart: 11 -> 11, of which waited for: 6 -> 5; matrix products, arithmetic and copies ran while one was open for 1% -> 1% of each run, Pallas kernels for 11% -> 13%
where the time goes in v3:
time: 64.8 us; the launch traced here: 64.4 us
  starting transfers between devices  23 us (35%)
  waiting for transfers between devices  19.7 us (30%)
  Pallas kernels  19.4 us (30%)
  local copies, waits for them, and re-layouts  0.88 us (1%)
  other arithmetic  0.71 us (1%)
  between operations  0.69 us (1%)
    ppermute x6, waiting for transfers between devices, exchange(): lax.ppermute(arrays[slot], axis, [(i, i ^ slot) for i in range(size)])  13.4 us
    ppermute x6, starting transfers between devices, exchange(): lax.ppermute(arrays[slot], axis, [(i, i ^ slot) for i in range(size)])  10.9 us
    pallas_call x1, Pallas kernels, per_device(): pl.pallas_call(functools.partial(block_kernel, sizes, capacity), out_shap...  8.3 us
    ppermute x3, starting transfers between devices, spread(): lax.ppermute(terms, axis, [(i, i ^ slot) for i in range(size)])  4.45 us
    all_to_all x1, starting transfers between devices, per_device(): grads = swap(grad_blocks)  3.94 us
    all_to_all x1, starting transfers between devices, per_device(): merged = swap(results[n_in])  3.72 us
    pallas_call x1, Pallas kernels, per_device(): pl.pallas_call(functools.partial(front_kernel, sizes, capacity), out_shap...  3.45 us
    ppermute x3, waiting for transfers between devices, spread(): lax.ppermute(terms, axis, [(i, i ^ slot) for i in range(size)])  3.31 us
  transfers between devices with their start and end apart: 11, of which 5 were waited for; matrix products, arithmetic and copies ran while one was open for 1% of the time, Pallas kernels for 13%

profile of v3, /device:TPU:0, one launch (start us, length us, event | category | flops | bytes accessed | tf_op | source)
XLA Modules:
  0.0 64.4 jit_solution(3074558062262987093)
XLA Ops:
  0.6 2.6 %pack_blocks.1 = (bf16[1,2,32,1280]{3,2,1,0:T(8,128)(2,1)}, bf16[1,2,32,1280]{3,2,1,0:T(8,128)(2,1)S(1)}, bf16[1,2,32,1280]{3,2,1,0:T(8,128)(2,1)S(1)}, bf16[1,2,32,1280]{3,2,1,0:T(8,128)(2,1)S(1)}) custom-call(s32[4]{0:T(128)} %bitcast.13, bf16[8,32,1280]{2,1,0:T(8,128)(2,1)} %bitcast.11), custom_call_target="tpu_custom_call" | custom-call | tf_op jit(solution)/shard_map/pack_blocks/pallas_call | solution.py:382
  3.2 3.1 %collective-permute-start = (bf16[1,2,32,1280]{3,2,1,0:T(8,128)(2,1)S(1)}, bf16[1,2,32,1280]{3,2,1,0:T(8,128)(2,1)S(1)}, u32[]{:S(2)}, u32[]{:S(2)}) collective-permute-start(bf16[1,2,32,1280]{3,2,1,0:T(8,128)(2,1)S(1)} %get-tuple-element.21), channel_id=1, source_target_pairs={{0,8},{8,0},{16,24},{24,16},{1,9},{9,1},{17,25},{25,17},{2,10},{10... | collective-permute-start | bytes 491528 | tf_op jit(solution)/shard_map/ppermute | solution.py:52
  6.3 2.6 %collective-permute-start.1 = (bf16[1,2,32,1280]{3,2,1,0:T(8,128)(2,1)S(1)}, bf16[1,2,32,1280]{3,2,1,0:T(8,128)(2,1)S(1)}, u32[]{:S(2)}, u32[]{:S(2)}) collective-permute-start(bf16[1,2,32,1280]{3,2,1,0:T(8,128)(2,1)S(1)} %get-tuple-element.22), channel_id=1, source_target_pairs={{0,16},{8,24},{16,0},{24,8},{1,17},{9,25},{17,1},{25,9},{2,18},{10... | collective-permute-start | bytes 491528 | tf_op jit(solution)/shard_map/ppermute | solution.py:52
  8.9 0.0 collective-permute-start.2
  8.9 3.9 %all-to-all-start = ((bf16[8,8,5120]{2,1,0:T(8,128)(2,1)}), bf16[8,8,5120]{2,1,0:T(8,128)(2,1)S(1)}, u32[]{:S(2)}, u32[]{:S(2)}) async-start(bf16[8,8,5120]{2,1,0:T(8,128)(2,1)} %bitcast.12), calls=%async_computation | async-start | bytes 1310720 | tf_op jit(solution)/shard_map/all_to_all | solution.py:397
  12.8 3.2 %hold.1.refs_3_ = bf16[2880,1280]{1,0:T(8,128)(2,1)S(1)} custom-call(bf16[2880,1280]{1,0:T(8,128)(2,1)} %bitcast.9), custom_call_target="tpu_custom_call" | custom-call | flops 100000000 | bytes 1000000 | tf_op jit(solution)/shard_map/hold/pallas_call | solution.py:399
  16.0 0.0 collective-permute-done.refs_5_
  16.0 5.3 %collective-permute-done.1.refs_6_ = bf16[1,2,32,1280]{3,2,1,0:T(8,128)(2,1)S(1)} collective-permute-done((bf16[1,2,32,1280]{3,2,1,0:T(8,128)(2,1)S(1)}, bf16[1,2,32,1280]{3,2,1,0:T(8,128)(2,1)S(1)}, u32[]{:S(2)}, u32[]{:S(2)}) %collective-permute-start.1) | collective-permute-done | bytes 163872 | tf_op jit(solution)/shard_map/ppermute | solution.py:52
  21.4 0.0 collective-permute-done.2.refs_7_
  21.4 3.5 %front.1 = (bf16[128,1280]{1,0:T(8,128)(2,1)S(1)}, f32[128,1280]{1,0:T(8,128)S(1)}, f32[128,128]{1,0:T(8,128)S(1)}, bf16[128,1024]{1,0:T(8,128)(2,1)S(1)}, bf16[...) custom-call(s32[4]{0:T(128)} %bitcast.14, f32[1280]{0:T(1024)} %refs_3_.1, f32[1280]{0:T(1024)} %refs_2_.1, ...), custom_call_target="tpu_custom_call" | custom-call | flops 12000000000 | bytes 8000000 | tf_op jit(solution)/shard_map/front/pallas_call | solution.py:411
  24.8 0.0 all-to-all-done.refs_14_
  24.8 8.3 %block.1 = (bf16[1,2,32,1280]{3,2,1,0:T(8,128)(2,1)}, bf16[1,2,32,1280]{3,2,1,0:T(8,128)(2,1)S(1)}, bf16[1,2,32,1280]{3,2,1,0:T(8,128)(2,1)S(1)}, bf16[1,2,32,12...) custom-call(s32[4]{0:T(128)} %bitcast.15, s32[1,128]{1,0:T(1,128)} %bitcast.17, ...), custom_call_target="tpu_custom_call" | custom-call | flops 2000000000 | bytes 12000000 | tf_op jit(solution)/shard_map/block/pallas_call | solution.py:435
  33.1 2.7 %collective-permute-start.3 = (bf16[1,2,32,1280]{3,2,1,0:T(8,128)(2,1)S(1)}, bf16[1,2,32,1280]{3,2,1,0:T(8,128)(2,1)S(1)}, u32[]{:S(2)}, u32[]{:S(2)}) collective-permute-start(bf16[1,2,32,1280]{3,2,1,0:T(8,128)(2,1)S(1)} %get-tuple-element.32), channel_id=1, source_target_pairs={{0,8},{8,0},{16,24},{24,16},{1,9},{9,1},{17,25},{25,17},{2,10},{10... | collective-permute-start | bytes 491528 | tf_op jit(solution)/shard_map/ppermute | solution.py:52
  35.9 1.1 %collective-permute-start.4 = (bf16[1,2,32,1280]{3,2,1,0:T(8,128)(2,1)S(1)}, bf16[1,2,32,1280]{3,2,1,0:T(8,128)(2,1)S(1)}, u32[]{:S(2)}, u32[]{:S(2)}) collective-permute-start(bf16[1,2,32,1280]{3,2,1,0:T(8,128)(2,1)S(1)} %get-tuple-element.33), channel_id=1, source_target_pairs={{0,16},{8,24},{16,0},{24,8},{1,17},{9,25},{17,1},{25,9},{2,18},{10... | collective-permute-start | bytes 491528 | tf_op jit(solution)/shard_map/ppermute | solution.py:52
  36.9 1.4 %collective-permute-start.5 = (bf16[1,2,32,1280]{3,2,1,0:T(8,128)(2,1)S(1)}, bf16[1,2,32,1280]{3,2,1,0:T(8,128)(2,1)S(1)}, u32[]{:S(2)}, u32[]{:S(2)}) collective-permute-start(bf16[1,2,32,1280]{3,2,1,0:T(8,128)(2,1)S(1)} %get-tuple-element.34), channel_id=1, source_target_pairs={{0,24},{8,16},{16,8},{24,0},{1,25},{9,17},{17,9},{25,1},{2,26},{10... | collective-permute-start | bytes 491528 | tf_op jit(solution)/shard_map/ppermute | solution.py:52
  38.3 3.7 %all-to-all-start.1 = ((bf16[8,8,6400]{2,1,0:T(8,128)(2,1)}), bf16[8,8,6400]{2,1,0:T(8,128)(2,1)S(1)}, u32[]{:S(2)}, u32[]{:S(2)}) async-start(bf16[8,8,6400]{2,1,0:T(8,128)(2,1)} %get-tuple-element.30), calls=%async_computation.1 | async-start | bytes 1638400 | tf_op jit(solution)/shard_map/all_to_all | solution.py:481
  42.1 0.0 collective-permute-done.3.refs_2_
  42.1 8.0 %collective-permute-done.4.refs_3_ = bf16[1,2,32,1280]{3,2,1,0:T(8,128)(2,1)S(1)} collective-permute-done((bf16[1,2,32,1280]{3,2,1,0:T(8,128)(2,1)S(1)}, bf16[1,2,32,1280]{3,2,1,0:T(8,128)(2,1)S(1)}, u32[]{:S(2)}, u32[]{:S(2)}) %collective-permute-start.4) | collective-permute-done | bytes 163872 | tf_op jit(solution)/shard_map/ppermute | solution.py:52
  50.1 0.0 collective-permute-done.5.refs_4_
  50.1 1.9 %unpack.1 = bf16[8,32,1280]{2,1,0:T(8,128)(2,1)} custom-call(s32[4]{0:T(128)} %bitcast.16, bf16[1,2,32,1280]{3,2,1,0:T(8,128)(2,1)} %get-tuple-element.31.refs_1_, bf16[1,2,32,1280]{3,2,1,0:T(8,128)(2,1)S(1)} %collective-permute-done.3.refs_2_, bf16[1,2,32,1280]{3,2,1,0:T(8,128)(2,1)S(1)} %collective-permute-done.4.refs_3_, ...), custom_call_target="tpu_custom_call" | custom-call | flops 10000000000 | bytes 1000000 | tf_op jit(solution)/shard_map/unpack/pallas_call | solution.py:482
  52.0 3.0 %all-to-all-done.1 = bf16[8,8,6400]{2,1,0:T(8,128)(2,1)S(1)} async-done(((bf16[8,8,6400]{2,1,0:T(8,128)(2,1)}), bf16[8,8,6400]{2,1,0:T(8,128)(2,1)S(1)}, u32[]{:S(2)}, u32[]{:S(2)}) %all-to-all-start.1) | async-done | bytes 819232 | tf_op jit(solution)/shard_map/all_to_all | solution.py:481
  55.0 0.1 fusion
  55.1 1.1 %collective-permute-start.6 = (f32[4,1280]{1,0:T(4,128)S(1)}, f32[4,1280]{1,0:T(4,128)S(1)}, u32[]{:S(2)}, u32[]{:S(2)}) collective-permute-start(f32[4,1280]{1,0:T(4,128)S(1)} %fusion), channel_id=1, source_target_pairs={{0,8},{8,0},{16,24},{24,16},{1,9},{9,1},{17,25},{25,17},{2,10},{10... | collective-permute-start | bytes 61448 | tf_op jit(solution)/shard_map/ppermute | solution.py:60
  56.2 2.0 %collective-permute-start.7 = (f32[4,1280]{1,0:T(4,128)S(1)}, f32[4,1280]{1,0:T(4,128)S(1)}, u32[]{:S(2)}, u32[]{:S(2)}) collective-permute-start(f32[4,1280]{1,0:T(4,128)S(1)} %fusion), channel_id=1, source_target_pairs={{0,16},{8,24},{16,0},{24,8},{1,17},{9,25},{17,1},{25,9},{2,18},{10... | collective-permute-start | bytes 61448 | tf_op jit(solution)/shard_map/ppermute | solution.py:60
  58.2 1.4 %collective-permute-start.8 = (f32[4,1280]{1,0:T(4,128)S(1)}, f32[4,1280]{1,0:T(4,128)S(1)}, u32[]{:S(2)}, u32[]{:S(2)}) collective-permute-start(f32[4,1280]{1,0:T(4,128)S(1)} %fusion), channel_id=1, source_target_pairs={{0,24},{8,16},{16,8},{24,0},{1,25},{9,17},{17,9},{25,1},{2,26},{10... | collective-permute-start | bytes 61448 | tf_op jit(solution)/shard_map/ppermute | solution.py:60
  59.6 0.9 %slice_bitcast_fusion = bf16[64,5120]{1,0:T(8,128)(2,1)} fusion(bf16[8,8,6400]{2,1,0:T(8,128)(2,1)S(1)} %all-to-all-done.1), kind=kLoop, calls=%fused_computation | loop fusion | bytes 1310720 | tf_op jit(solution)/shard_map/reshape | solution.py:502
  60.4 0.0 collective-permute-done.6
  60.4 0.4 collective-permute-done.7
  60.9 2.9 %collective-permute-done.8 = f32[4,1280]{1,0:T(4,128)S(1)} collective-permute-done((f32[4,1280]{1,0:T(4,128)S(1)}, f32[4,1280]{1,0:T(4,128)S(1)}, u32[]{:S(2)}, u32[]{:S(2)}) %collective-permute-start.8) | collective-permute-done | bytes 20512 | tf_op jit(solution)/shard_map/ppermute | solution.py:60
  63.8 0.6 add_add_fusion
  (1 shorter events, 0.0 us)
Async XLA Ops:
  3.2 12.8 %collective-permute-start = (bf16[1,2,32,1280]{3,2,1,0:T(8,128)(2,1)S(1)}, bf16[1,2,32,1280]{3,2,1,0:T(8,128)(2,1)S(1)}, u32[]{:S(2)}, u32[]{:S(2)}) collective-permute-start(bf16[1,2,32,1280]{3,2,1,0:T(8,128)(2,1)S(1)} %get-tuple-element.21), channel_id=1, source_target_pairs={{0,8},{8,0},{16,24},{24,16},{1,9},{9,1},{17,25},{25,17},{2,10},{10... | collective-permute-start | bytes 491528 | tf_op jit(solution)/shard_map/ppermute | solution.py:52
  6.3 15.0 %collective-permute-start.1 = (bf16[1,2,32,1280]{3,2,1,0:T(8,128)(2,1)S(1)}, bf16[1,2,32,1280]{3,2,1,0:T(8,128)(2,1)S(1)}, u32[]{:S(2)}, u32[]{:S(2)}) collective-permute-start(bf16[1,2,32,1280]{3,2,1,0:T(8,128)(2,1)S(1)} %get-tuple-element.22), channel_id=1, source_target_pairs={{0,16},{8,24},{16,0},{24,8},{1,17},{9,25},{17,1},{25,9},{2,18},{10... | collective-permute-start | bytes 491528 | tf_op jit(solution)/shard_map/ppermute | solution.py:52
  8.9 12.5 %collective-permute-start.2 = (bf16[1,2,32,1280]{3,2,1,0:T(8,128)(2,1)S(1)}, bf16[1,2,32,1280]{3,2,1,0:T(8,128)(2,1)S(1)}, u32[]{:S(2)}, u32[]{:S(2)}) collective-permute-start(bf16[1,2,32,1280]{3,2,1,0:T(8,128)(2,1)S(1)} %get-tuple-element.23), channel_id=1, source_target_pairs={{0,24},{8,16},{16,8},{24,0},{1,25},{9,17},{17,9},{25,1},{2,26},{10... | collective-permute-start | bytes 491528 | tf_op jit(solution)/shard_map/ppermute | solution.py:52
  8.9 15.9 %all-to-all-start = ((bf16[8,8,5120]{2,1,0:T(8,128)(2,1)}), bf16[8,8,5120]{2,1,0:T(8,128)(2,1)S(1)}, u32[]{:S(2)}, u32[]{:S(2)}) async-start(bf16[8,8,5120]{2,1,0:T(8,128)(2,1)} %bitcast.12), calls=%async_computation | async-start | bytes 1310720 | tf_op jit(solution)/shard_map/all_to_all | solution.py:397
  33.1 8.9 %collective-permute-start.3 = (bf16[1,2,32,1280]{3,2,1,0:T(8,128)(2,1)S(1)}, bf16[1,2,32,1280]{3,2,1,0:T(8,128)(2,1)S(1)}, u32[]{:S(2)}, u32[]{:S(2)}) collective-permute-start(bf16[1,2,32,1280]{3,2,1,0:T(8,128)(2,1)S(1)} %get-tuple-element.32), channel_id=1, source_target_pairs={{0,8},{8,0},{16,24},{24,16},{1,9},{9,1},{17,25},{25,17},{2,10},{10... | collective-permute-start | bytes 491528 | tf_op jit(solution)/shard_map/ppermute | solution.py:52
  35.9 14.2 %collective-permute-start.4 = (bf16[1,2,32,1280]{3,2,1,0:T(8,128)(2,1)S(1)}, bf16[1,2,32,1280]{3,2,1,0:T(8,128)(2,1)S(1)}, u32[]{:S(2)}, u32[]{:S(2)}) collective-permute-start(bf16[1,2,32,1280]{3,2,1,0:T(8,128)(2,1)S(1)} %get-tuple-element.33), channel_id=1, source_target_pairs={{0,16},{8,24},{16,0},{24,8},{1,17},{9,25},{17,1},{25,9},{2,18},{10... | collective-permute-start | bytes 491528 | tf_op jit(solution)/shard_map/ppermute | solution.py:52
  36.9 13.2 %collective-permute-start.5 = (bf16[1,2,32,1280]{3,2,1,0:T(8,128)(2,1)S(1)}, bf16[1,2,32,1280]{3,2,1,0:T(8,128)(2,1)S(1)}, u32[]{:S(2)}, u32[]{:S(2)}) collective-permute-start(bf16[1,2,32,1280]{3,2,1,0:T(8,128)(2,1)S(1)} %get-tuple-element.34), channel_id=1, source_target_pairs={{0,24},{8,16},{16,8},{24,0},{1,25},{9,17},{17,9},{25,1},{2,26},{10... | collective-permute-start | bytes 491528 | tf_op jit(solution)/shard_map/ppermute | solution.py:52
  38.3 16.7 %all-to-all-start.1 = ((bf16[8,8,6400]{2,1,0:T(8,128)(2,1)}), bf16[8,8,6400]{2,1,0:T(8,128)(2,1)S(1)}, u32[]{:S(2)}, u32[]{:S(2)}) async-start(bf16[8,8,6400]{2,1,0:T(8,128)(2,1)} %get-tuple-element.30), calls=%async_computation.1 | async-start | bytes 1638400 | tf_op jit(solution)/shard_map/all_to_all | solution.py:481
  55.1 5.3 %collective-permute-start.6 = (f32[4,1280]{1,0:T(4,128)S(1)}, f32[4,1280]{1,0:T(4,128)S(1)}, u32[]{:S(2)}, u32[]{:S(2)}) collective-permute-start(f32[4,1280]{1,0:T(4,128)S(1)} %fusion), channel_id=1, source_target_pairs={{0,8},{8,0},{16,24},{24,16},{1,9},{9,1},{17,25},{25,17},{2,10},{10... | collective-permute-start | bytes 61448 | tf_op jit(solution)/shard_map/ppermute | solution.py:60
  56.2 4.7 %collective-permute-start.7 = (f32[4,1280]{1,0:T(4,128)S(1)}, f32[4,1280]{1,0:T(4,128)S(1)}, u32[]{:S(2)}, u32[]{:S(2)}) collective-permute-start(f32[4,1280]{1,0:T(4,128)S(1)} %fusion), channel_id=1, source_target_pairs={{0,16},{8,24},{16,0},{24,8},{1,17},{9,25},{17,1},{25,9},{2,18},{10... | collective-permute-start | bytes 61448 | tf_op jit(solution)/shard_map/ppermute | solution.py:60
  58.2 5.6 %collective-permute-start.8 = (f32[4,1280]{1,0:T(4,128)S(1)}, f32[4,1280]{1,0:T(4,128)S(1)}, u32[]{:S(2)}, u32[]{:S(2)}) collective-permute-start(f32[4,1280]{1,0:T(4,128)S(1)} %fusion), channel_id=1, source_target_pairs={{0,24},{8,16},{16,8},{24,0},{1,25},{9,17},{17,9},{25,1},{2,26},{10... | collective-permute-start | bytes 61448 | tf_op jit(solution)/shard_map/ppermute | solution.py:60

commit v4 on v3

--- a/solution.py
+++ b/solution.py
@@ -78,20 +78,20 @@
     return out
 
 
-def pack_blocks(sizes, capacity, counts, source, *rest):
+def pack_blocks(sizes, capacity, slots, counts, source, *rest):
     ranks = sizes[0]
     outs, sems = rest[:-1], rest[-1]
     me = lax.axis_index("dp")
     first = chosen(starts(counts, ranks), me)
     copies = []
-    for slot in range(ranks):
-        array, entry = place(slot, ranks)
+    for i, slot in enumerate(slots):
+        array, entry = (i, 0) if paired(ranks) else (0, slot)
         lead = lax.rem(peer_of(me, slot, ranks) + 8 * ranks - first, ranks)
         for k in range(capacity):
             block = jnp.minimum(lead + k * ranks, source.shape[0] - 1)
             copies.append(
                 pltpu.make_async_copy(
-                    source.at[block], outs[array].at[entry, k], sems.at[slot * capacity + k]
+                    source.at[block], outs[array].at[entry, k], sems.at[i * capacity + k]
                 )
             )
             copies[-1].start()
@@ -379,18 +379,24 @@
         lax.all_to_all, axis_name="ctx", split_axis=0, concat_axis=0, tiled=True
     )
 
-    outgoing = pl.pallas_call(
-        functools.partial(pack_blocks, sizes, capacity),
-        out_shape=block_shapes,
-        in_specs=[smem, anywhere],
-        out_specs=[vmem] * n_in,
-        scratch_shapes=[pltpu.SemaphoreType.DMA((ranks * capacity,))],
-        compiler_params=pltpu.CompilerParams(vmem_limit_bytes=4 * 2**20),
-        name="pack_blocks",
-    )(
-        in_hbm(counts),
-        in_hbm(patches.reshape(source_units, UNIT, width)),
-    )
+    def packed(slots, shapes, name):
+        return pl.pallas_call(
+            functools.partial(pack_blocks, sizes, capacity, slots),
+            out_shape=shapes,
+            in_specs=[smem, anywhere],
+            out_specs=[vmem] * len(shapes),
+            scratch_shapes=[pltpu.SemaphoreType.DMA((len(slots) * capacity,))],
+            compiler_params=pltpu.CompilerParams(vmem_limit_bytes=4 * 2**20),
+            name=name,
+        )(in_hbm(counts), in_hbm(patches.reshape(source_units, UNIT, width)))
+
+    if paired(ranks):
+        outgoing = [
+            *packed([0], block_shapes[:1], "pack_own"),
+            *packed(range(1, ranks), block_shapes[1:], "pack_blocks"),
+        ]
+    else:
+        outgoing = packed(range(ranks), block_shapes, "pack_blocks")
     arrived = exchange(outgoing, "dp", ranks)
 
     grad_blocks = merged_grad.reshape(owners, pair, token_width)

time: 64.8 us -> 64.1 us (0.989)
  waiting for transfers between devices: 19.7 us -> 17.4 us
  Pallas kernels: 19.4 us -> 20.9 us
    ppermute x6, waiting for transfers between devices: 13.4 us -> 11.1 us  [exchange(): lax.ppermute(arrays[slot], axis, [(i, i ^ slot) for i in range(size)])]
    pallas_call x1 -> x2, Pallas kernels: 2.58 us -> 4.11 us  [packed(): pl.pallas_call(functools.partial(pack_blocks, sizes, capacity, slots), ou...]
  transfers between devices with their start and end apart: 11 -> 11, of which waited for: 5 -> 5; matrix products, arithmetic and copies ran while one was open for 1% -> 1% of each run, Pallas kernels for 13% -> 17%
where the time goes in v4:
time: 64.1 us; the launch traced here: 63.6 us
  starting transfers between devices  23 us (36%)
  Pallas kernels  20.9 us (33%)
  waiting for transfers between devices  17.4 us (27%)
  local copies, waits for them, and re-layouts  0.88 us (1%)
  other arithmetic  0.71 us (1%)
  between operations  0.7 us (1%)
    ppermute x6, waiting for transfers between devices, exchange(): lax.ppermute(arrays[slot], axis, [(i, i ^ slot) for i in range(size)])  11.1 us
    ppermute x6, starting transfers between devices, exchange(): lax.ppermute(arrays[slot], axis, [(i, i ^ slot) for i in range(size)])  10.9 us
    pallas_call x1, Pallas kernels, per_device(): pl.pallas_call(functools.partial(block_kernel, sizes, capacity), out_shap...  8.3 us
    ppermute x3, starting transfers between devices, spread(): lax.ppermute(terms, axis, [(i, i ^ slot) for i in range(size)])  4.45 us
    pallas_call x2, Pallas kernels, packed(): pl.pallas_call(functools.partial(pack_blocks, sizes, capacity, slots), ou...  4.11 us
    all_to_all x1, starting transfers between devices, per_device(): grads = swap(grad_blocks)  3.94 us
    all_to_all x1, starting transfers between devices, per_device(): merged = swap(results[n_in])  3.73 us
    pallas_call x1, Pallas kernels, per_device(): pl.pallas_call(functools.partial(front_kernel, sizes, capacity), out_shap...  3.46 us
  transfers between devices with their start and end apart: 11, of which 5 were waited for; matrix products, arithmetic and copies ran while one was open for 1% of the time, Pallas kernels for 17%

profile of v4, /device:TPU:0, one launch (start us, length us, event | category | flops | bytes accessed | tf_op | source)
XLA Modules:
  0.0 63.6 jit_solution(15702087500494123550)
XLA Ops:
  0.6 1.8 %pack_blocks.1 = (bf16[1,2,32,1280]{3,2,1,0:T(8,128)(2,1)S(1)}, bf16[1,2,32,1280]{3,2,1,0:T(8,128)(2,1)S(1)}, bf16[1,2,32,1280]{3,2,1,0:T(8,128)(2,1)S(1)}) custom-call(s32[4]{0:T(128)} %bitcast.14, bf16[8,32,1280]{2,1,0:T(8,128)(2,1)} %bitcast.11), custom_call_target="tpu_custom_call" | custom-call | tf_op jit(solution)/shard_map/pack_blocks/pallas_call | solution.py:383
  2.5 3.1 %collective-permute-start = (bf16[1,2,32,1280]{3,2,1,0:T(8,128)(2,1)S(1)}, bf16[1,2,32,1280]{3,2,1,0:T(8,128)(2,1)S(1)}, u32[]{:S(2)}, u32[]{:S(2)}) collective-permute-start(bf16[1,2,32,1280]{3,2,1,0:T(8,128)(2,1)S(1)} %get-tuple-element.19), channel_id=1, source_target_pairs={{0,8},{8,0},{16,24},{24,16},{1,9},{9,1},{17,25},{25,17},{2,10},{10... | collective-permute-start | bytes 491528 | tf_op jit(solution)/shard_map/ppermute | solution.py:52
  5.5 2.6 %collective-permute-start.1 = (bf16[1,2,32,1280]{3,2,1,0:T(8,128)(2,1)S(1)}, bf16[1,2,32,1280]{3,2,1,0:T(8,128)(2,1)S(1)}, u32[]{:S(2)}, u32[]{:S(2)}) collective-permute-start(bf16[1,2,32,1280]{3,2,1,0:T(8,128)(2,1)S(1)} %get-tuple-element.20), channel_id=1, source_target_pairs={{0,16},{8,24},{16,0},{24,8},{1,17},{9,25},{17,1},{25,9},{2,18},{10... | collective-permute-start | bytes 491528 | tf_op jit(solution)/shard_map/ppermute | solution.py:52
  8.1 0.0 collective-permute-start.2
  8.1 3.9 %all-to-all-start = ((bf16[8,8,5120]{2,1,0:T(8,128)(2,1)}), bf16[8,8,5120]{2,1,0:T(8,128)(2,1)S(1)}, u32[]{:S(2)}, u32[]{:S(2)}) async-start(bf16[8,8,5120]{2,1,0:T(8,128)(2,1)} %bitcast.13), calls=%async_computation | async-start | bytes 1310720 | tf_op jit(solution)/shard_map/all_to_all | solution.py:403
  12.1 2.3 %pack_own.1.refs_4_ = bf16[1,2,32,1280]{3,2,1,0:T(8,128)(2,1)} custom-call(s32[4]{0:T(128)} %bitcast.15, bf16[8,32,1280]{2,1,0:T(8,128)(2,1)} %bitcast.12), custom_call_target="tpu_custom_call" | custom-call | tf_op jit(solution)/shard_map/pack_own/pallas_call | solution.py:383
  14.4 3.2 %hold.1.refs_3_ = bf16[2880,1280]{1,0:T(8,128)(2,1)S(1)} custom-call(bf16[2880,1280]{1,0:T(8,128)(2,1)} %bitcast.9), custom_call_target="tpu_custom_call" | custom-call | flops 100000000 | bytes 1000000 | tf_op jit(solution)/shard_map/hold/pallas_call | solution.py:405
  17.6 0.0 collective-permute-done.refs_5_
  17.6 3.0 %collective-permute-done.1.refs_6_ = bf16[1,2,32,1280]{3,2,1,0:T(8,128)(2,1)S(1)} collective-permute-done((bf16[1,2,32,1280]{3,2,1,0:T(8,128)(2,1)S(1)}, bf16[1,2,32,1280]{3,2,1,0:T(8,128)(2,1)S(1)}, u32[]{:S(2)}, u32[]{:S(2)}) %collective-permute-start.1) | collective-permute-done | bytes 163872 | tf_op jit(solution)/shard_map/ppermute | solution.py:52
  20.6 0.0 collective-permute-done.2.refs_7_
  20.6 3.5 %front.1 = (bf16[128,1280]{1,0:T(8,128)(2,1)S(1)}, f32[128,1280]{1,0:T(8,128)S(1)}, f32[128,128]{1,0:T(8,128)S(1)}, bf16[128,1024]{1,0:T(8,128)(2,1)S(1)}, bf16[...) custom-call(s32[4]{0:T(128)} %bitcast.16, f32[1280]{0:T(1024)} %refs_3_.1, f32[1280]{0:T(1024)} %refs_2_.1, ...), custom_call_target="tpu_custom_call" | custom-call | flops 12000000000 | bytes 8000000 | tf_op jit(solution)/shard_map/front/pallas_call | solution.py:417
  24.1 0.0 all-to-all-done.refs_14_
  24.1 8.3 %block.1 = (bf16[1,2,32,1280]{3,2,1,0:T(8,128)(2,1)}, bf16[1,2,32,1280]{3,2,1,0:T(8,128)(2,1)S(1)}, bf16[1,2,32,1280]{3,2,1,0:T(8,128)(2,1)S(1)}, bf16[1,2,32,12...) custom-call(s32[4]{0:T(128)} %bitcast.17, s32[1,128]{1,0:T(1,128)} %bitcast.19, ...), custom_call_target="tpu_custom_call" | custom-call | flops 2000000000 | bytes 12000000 | tf_op jit(solution)/shard_map/block/pallas_call | solution.py:441
  32.4 2.7 %collective-permute-start.3 = (bf16[1,2,32,1280]{3,2,1,0:T(8,128)(2,1)S(1)}, bf16[1,2,32,1280]{3,2,1,0:T(8,128)(2,1)S(1)}, u32[]{:S(2)}, u32[]{:S(2)}) collective-permute-start(bf16[1,2,32,1280]{3,2,1,0:T(8,128)(2,1)S(1)} %get-tuple-element.30), channel_id=1, source_target_pairs={{0,8},{8,0},{16,24},{24,16},{1,9},{9,1},{17,25},{25,17},{2,10},{10... | collective-permute-start | bytes 491528 | tf_op jit(solution)/shard_map/ppermute | solution.py:52
  35.1 1.1 %collective-permute-start.4 = (bf16[1,2,32,1280]{3,2,1,0:T(8,128)(2,1)S(1)}, bf16[1,2,32,1280]{3,2,1,0:T(8,128)(2,1)S(1)}, u32[]{:S(2)}, u32[]{:S(2)}) collective-permute-start(bf16[1,2,32,1280]{3,2,1,0:T(8,128)(2,1)S(1)} %get-tuple-element.31), channel_id=1, source_target_pairs={{0,16},{8,24},{16,0},{24,8},{1,17},{9,25},{17,1},{25,9},{2,18},{10... | collective-permute-start | bytes 491528 | tf_op jit(solution)/shard_map/ppermute | solution.py:52
  36.2 1.4 %collective-permute-start.5 = (bf16[1,2,32,1280]{3,2,1,0:T(8,128)(2,1)S(1)}, bf16[1,2,32,1280]{3,2,1,0:T(8,128)(2,1)S(1)}, u32[]{:S(2)}, u32[]{:S(2)}) collective-permute-start(bf16[1,2,32,1280]{3,2,1,0:T(8,128)(2,1)S(1)} %get-tuple-element.32), channel_id=1, source_target_pairs={{0,24},{8,16},{16,8},{24,0},{1,25},{9,17},{17,9},{25,1},{2,26},{10... | collective-permute-start | bytes 491528 | tf_op jit(solution)/shard_map/ppermute | solution.py:52
  37.6 3.7 %all-to-all-start.1 = ((bf16[8,8,6400]{2,1,0:T(8,128)(2,1)}), bf16[8,8,6400]{2,1,0:T(8,128)(2,1)S(1)}, u32[]{:S(2)}, u32[]{:S(2)}) async-start(bf16[8,8,6400]{2,1,0:T(8,128)(2,1)} %get-tuple-element.28), calls=%async_computation.1 | async-start | bytes 1638400 | tf_op jit(solution)/shard_map/all_to_all | solution.py:487
  41.3 0.0 collective-permute-done.3.refs_2_
  41.3 8.0 %collective-permute-done.4.refs_3_ = bf16[1,2,32,1280]{3,2,1,0:T(8,128)(2,1)S(1)} collective-permute-done((bf16[1,2,32,1280]{3,2,1,0:T(8,128)(2,1)S(1)}, bf16[1,2,32,1280]{3,2,1,0:T(8,128)(2,1)S(1)}, u32[]{:S(2)}, u32[]{:S(2)}) %collective-permute-start.4) | collective-permute-done | bytes 163872 | tf_op jit(solution)/shard_map/ppermute | solution.py:52
  49.3 0.0 collective-permute-done.5.refs_4_
  49.3 1.9 %unpack.1 = bf16[8,32,1280]{2,1,0:T(8,128)(2,1)} custom-call(s32[4]{0:T(128)} %bitcast.18, bf16[1,2,32,1280]{3,2,1,0:T(8,128)(2,1)} %get-tuple-element.29.refs_1_, bf16[1,2,32,1280]{3,2,1,0:T(8,128)(2,1)S(1)} %collective-permute-done.3.refs_2_, bf16[1,2,32,1280]{3,2,1,0:T(8,128)(2,1)S(1)} %collective-permute-done.4.refs_3_, ...), custom_call_target="tpu_custom_call" | custom-call | flops 10000000000 | bytes 1000000 | tf_op jit(solution)/shard_map/unpack/pallas_call | solution.py:488
  51.2 3.0 %all-to-all-done.1 = bf16[8,8,6400]{2,1,0:T(8,128)(2,1)S(1)} async-done(((bf16[8,8,6400]{2,1,0:T(8,128)(2,1)}), bf16[8,8,6400]{2,1,0:T(8,128)(2,1)S(1)}, u32[]{:S(2)}, u32[]{:S(2)}) %all-to-all-start.1) | async-done | bytes 819232 | tf_op jit(solution)/shard_map/all_to_all | solution.py:487
  54.3 0.1 fusion
  54.3 1.1 %collective-permute-start.6 = (f32[4,1280]{1,0:T(4,128)S(1)}, f32[4,1280]{1,0:T(4,128)S(1)}, u32[]{:S(2)}, u32[]{:S(2)}) collective-permute-start(f32[4,1280]{1,0:T(4,128)S(1)} %fusion), channel_id=1, source_target_pairs={{0,8},{8,0},{16,24},{24,16},{1,9},{9,1},{17,25},{25,17},{2,10},{10... | collective-permute-start | bytes 61448 | tf_op jit(solution)/shard_map/ppermute | solution.py:60
  55.4 2.0 %collective-permute-start.7 = (f32[4,1280]{1,0:T(4,128)S(1)}, f32[4,1280]{1,0:T(4,128)S(1)}, u32[]{:S(2)}, u32[]{:S(2)}) collective-permute-start(f32[4,1280]{1,0:T(4,128)S(1)} %fusion), channel_id=1, source_target_pairs={{0,16},{8,24},{16,0},{24,8},{1,17},{9,25},{17,1},{25,9},{2,18},{10... | collective-permute-start | bytes 61448 | tf_op jit(solution)/shard_map/ppermute | solution.py:60
  57.4 1.4 %collective-permute-start.8 = (f32[4,1280]{1,0:T(4,128)S(1)}, f32[4,1280]{1,0:T(4,128)S(1)}, u32[]{:S(2)}, u32[]{:S(2)}) collective-permute-start(f32[4,1280]{1,0:T(4,128)S(1)} %fusion), channel_id=1, source_target_pairs={{0,24},{8,16},{16,8},{24,0},{1,25},{9,17},{17,9},{25,1},{2,26},{10... | collective-permute-start | bytes 61448 | tf_op jit(solution)/shard_map/ppermute | solution.py:60
  58.8 0.9 %slice_bitcast_fusion = bf16[64,5120]{1,0:T(8,128)(2,1)} fusion(bf16[8,8,6400]{2,1,0:T(8,128)(2,1)S(1)} %all-to-all-done.1), kind=kLoop, calls=%fused_computation | loop fusion | bytes 1310720 | tf_op jit(solution)/shard_map/reshape | solution.py:508
  59.7 0.0 collective-permute-done.6
  59.7 0.4 collective-permute-done.7
  60.1 2.9 %collective-permute-done.8 = f32[4,1280]{1,0:T(4,128)S(1)} collective-permute-done((f32[4,1280]{1,0:T(4,128)S(1)}, f32[4,1280]{1,0:T(4,128)S(1)}, u32[]{:S(2)}, u32[]{:S(2)}) %collective-permute-start.8) | collective-permute-done | bytes 20512 | tf_op jit(solution)/shard_map/ppermute | solution.py:60
  63.0 0.6 add_add_fusion
  (1 shorter events, 0.0 us)
Async XLA Ops:
  2.5 15.1 %collective-permute-start = (bf16[1,2,32,1280]{3,2,1,0:T(8,128)(2,1)S(1)}, bf16[1,2,32,1280]{3,2,1,0:T(8,128)(2,1)S(1)}, u32[]{:S(2)}, u32[]{:S(2)}) collective-permute-start(bf16[1,2,32,1280]{3,2,1,0:T(8,128)(2,1)S(1)} %get-tuple-element.19), channel_id=1, source_target_pairs={{0,8},{8,0},{16,24},{24,16},{1,9},{9,1},{17,25},{25,17},{2,10},{10... | collective-permute-start | bytes 491528 | tf_op jit(solution)/shard_map/ppermute | solution.py:52
  5.5 15.0 %collective-permute-start.1 = (bf16[1,2,32,1280]{3,2,1,0:T(8,128)(2,1)S(1)}, bf16[1,2,32,1280]{3,2,1,0:T(8,128)(2,1)S(1)}, u32[]{:S(2)}, u32[]{:S(2)}) collective-permute-start(bf16[1,2,32,1280]{3,2,1,0:T(8,128)(2,1)S(1)} %get-tuple-element.20), channel_id=1, source_target_pairs={{0,16},{8,24},{16,0},{24,8},{1,17},{9,25},{17,1},{25,9},{2,18},{10... | collective-permute-start | bytes 491528 | tf_op jit(solution)/shard_map/ppermute | solution.py:52
  8.1 12.5 %collective-permute-start.2 = (bf16[1,2,32,1280]{3,2,1,0:T(8,128)(2,1)S(1)}, bf16[1,2,32,1280]{3,2,1,0:T(8,128)(2,1)S(1)}, u32[]{:S(2)}, u32[]{:S(2)}) collective-permute-start(bf16[1,2,32,1280]{3,2,1,0:T(8,128)(2,1)S(1)} %get-tuple-element.21), channel_id=1, source_target_pairs={{0,24},{8,16},{16,8},{24,0},{1,25},{9,17},{17,9},{25,1},{2,26},{10... | collective-permute-start | bytes 491528 | tf_op jit(solution)/shard_map/ppermute | solution.py:52
  8.1 15.9 %all-to-all-start = ((bf16[8,8,5120]{2,1,0:T(8,128)(2,1)}), bf16[8,8,5120]{2,1,0:T(8,128)(2,1)S(1)}, u32[]{:S(2)}, u32[]{:S(2)}) async-start(bf16[8,8,5120]{2,1,0:T(8,128)(2,1)} %bitcast.13), calls=%async_computation | async-start | bytes 1310720 | tf_op jit(solution)/shard_map/all_to_all | solution.py:403
  32.4 8.9 %collective-permute-start.3 = (bf16[1,2,32,1280]{3,2,1,0:T(8,128)(2,1)S(1)}, bf16[1,2,32,1280]{3,2,1,0:T(8,128)(2,1)S(1)}, u32[]{:S(2)}, u32[]{:S(2)}) collective-permute-start(bf16[1,2,32,1280]{3,2,1,0:T(8,128)(2,1)S(1)} %get-tuple-element.30), channel_id=1, source_target_pairs={{0,8},{8,0},{16,24},{24,16},{1,9},{9,1},{17,25},{25,17},{2,10},{10... | collective-permute-start | bytes 491528 | tf_op jit(solution)/shard_map/ppermute | solution.py:52
  35.1 14.2 %collective-permute-start.4 = (bf16[1,2,32,1280]{3,2,1,0:T(8,128)(2,1)S(1)}, bf16[1,2,32,1280]{3,2,1,0:T(8,128)(2,1)S(1)}, u32[]{:S(2)}, u32[]{:S(2)}) collective-permute-start(bf16[1,2,32,1280]{3,2,1,0:T(8,128)(2,1)S(1)} %get-tuple-element.31), channel_id=1, source_target_pairs={{0,16},{8,24},{16,0},{24,8},{1,17},{9,25},{17,1},{25,9},{2,18},{10... | collective-permute-start | bytes 491528 | tf_op jit(solution)/shard_map/ppermute | solution.py:52
  36.2 13.2 %collective-permute-start.5 = (bf16[1,2,32,1280]{3,2,1,0:T(8,128)(2,1)S(1)}, bf16[1,2,32,1280]{3,2,1,0:T(8,128)(2,1)S(1)}, u32[]{:S(2)}, u32[]{:S(2)}) collective-permute-start(bf16[1,2,32,1280]{3,2,1,0:T(8,128)(2,1)S(1)} %get-tuple-element.32), channel_id=1, source_target_pairs={{0,24},{8,16},{16,8},{24,0},{1,25},{9,17},{17,9},{25,1},{2,26},{10... | collective-permute-start | bytes 491528 | tf_op jit(solution)/shard_map/ppermute | solution.py:52
  37.6 16.7 %all-to-all-start.1 = ((bf16[8,8,6400]{2,1,0:T(8,128)(2,1)}), bf16[8,8,6400]{2,1,0:T(8,128)(2,1)S(1)}, u32[]{:S(2)}, u32[]{:S(2)}) async-start(bf16[8,8,6400]{2,1,0:T(8,128)(2,1)} %get-tuple-element.28), calls=%async_computation.1 | async-start | bytes 1638400 | tf_op jit(solution)/shard_map/all_to_all | solution.py:487
  54.3 5.3 %collective-permute-start.6 = (f32[4,1280]{1,0:T(4,128)S(1)}, f32[4,1280]{1,0:T(4,128)S(1)}, u32[]{:S(2)}, u32[]{:S(2)}) collective-permute-start(f32[4,1280]{1,0:T(4,128)S(1)} %fusion), channel_id=1, source_target_pairs={{0,8},{8,0},{16,24},{24,16},{1,9},{9,1},{17,25},{25,17},{2,10},{10... | collective-permute-start | bytes 61448 | tf_op jit(solution)/shard_map/ppermute | solution.py:60
  55.4 4.7 %collective-permute-start.7 = (f32[4,1280]{1,0:T(4,128)S(1)}, f32[4,1280]{1,0:T(4,128)S(1)}, u32[]{:S(2)}, u32[]{:S(2)}) collective-permute-start(f32[4,1280]{1,0:T(4,128)S(1)} %fusion), channel_id=1, source_target_pairs={{0,16},{8,24},{16,0},{24,8},{1,17},{9,25},{17,1},{25,9},{2,18},{10... | collective-permute-start | bytes 61448 | tf_op jit(solution)/shard_map/ppermute | solution.py:60
  57.4 5.6 %collective-permute-start.8 = (f32[4,1280]{1,0:T(4,128)S(1)}, f32[4,1280]{1,0:T(4,128)S(1)}, u32[]{:S(2)}, u32[]{:S(2)}) collective-permute-start(f32[4,1280]{1,0:T(4,128)S(1)} %fusion), channel_id=1, source_target_pairs={{0,24},{8,16},{16,8},{24,0},{1,25},{9,17},{17,9},{25,1},{2,26},{10... | collective-permute-start | bytes 61448 | tf_op jit(solution)/shard_map/ppermute | solution.py:60

commit v5 on v4

--- a/solution.py
+++ b/solution.py
@@ -485,6 +485,16 @@
     )
     came_back = exchange(results[:n_in], "dp", ranks)
     merged = swap(results[n_in])
+    if beside:
+        halves = merged[:, :, token_width:].astype(F32)
+        norm_grads = jnp.sum(halves[:, :4] + halves[:, 4:], axis=0)
+        for bit in range(ranks.bit_length() - 1):
+            norm_grads = spread(norm_grads, "dp", ranks, (1 << bit,))
+            if bit == 0:
+                norm_grads, came_back = lax.optimization_barrier((norm_grads, came_back))
+        merged = merged[:, :, :token_width]
+    else:
+        norm_grads = lax.psum(results[-1], ("dp", "ctx"))
     patch_grad = pl.pallas_call(
         functools.partial(unpack_kernel, sizes, capacity),
         out_shape=jax.ShapeDtypeStruct((source_units, UNIT, width), BF16),
@@ -496,14 +506,6 @@
         ),
         name="unpack",
     )(in_hbm(counts), in_hbm(came_back[0]), *came_back[1:])
-    if beside:
-        halves = merged[:, :, token_width:].astype(F32)
-        terms = jnp.sum(halves[:, :4] + halves[:, 4:], axis=0)
-        terms, patch_grad = lax.optimization_barrier((terms, patch_grad))
-        norm_grads = spread(terms, "dp", ranks, range(1, ranks))
-        merged = merged[:, :, :token_width]
-    else:
-        norm_grads = lax.psum(results[-1], ("dp", "ctx"))
     return (
         merged.reshape(owner_slots, token_width),
         patch_grad.reshape(source_units * UNIT, width),

time: 64.1 us -> 61.1 us (0.953)
  waiting for transfers between devices: 17.4 us -> 11.9 us
  starting transfers between devices: 23 us -> 25.5 us
    ppermute x6, waiting for transfers between devices: 11.1 us -> 3.03 us  [exchange(): lax.ppermute(arrays[slot], axis, [(i, i ^ slot) for i in range(size)])]
    all_to_all x1, waiting for transfers between devices: 3.02 us -> 7.83 us  [per_device(): merged = swap(results[n_in])]
    ppermute x3 -> x2, starting transfers between devices: 4.45 us -> 7.03 us  [spread(): lax.ppermute(terms, axis, [(i, i ^ slot) for i in range(size)])]
    ppermute x3 -> x2, waiting for transfers between devices: 3.31 us -> 1.08 us  [spread(): lax.ppermute(terms, axis, [(i, i ^ slot) for i in range(size)])]
  transfers between devices with their start and end apart: 11 -> 10, of which waited for: 5 -> 3; matrix products, arithmetic and copies ran while one was open for 1% -> 2% of each run, Pallas kernels for 17% -> 18%
where the time goes in v5:
time: 61.1 us; the launch traced here: 60.7 us
  starting transfers between devices  25.5 us (42%)
  Pallas kernels  20.9 us (34%)
  waiting for transfers between devices  11.9 us (19%)
  local copies, waits for them, and re-layouts  0.88 us (1%)
  between operations  0.72 us (1%)
  other arithmetic  0.71 us (1%)
    ppermute x6, starting transfers between devices, exchange(): lax.ppermute(arrays[slot], axis, [(i, i ^ slot) for i in range(size)])  10.8 us
    pallas_call x1, Pallas kernels, per_device(): pl.pallas_call(functools.partial(block_kernel, sizes, capacity), out_shap...  8.3 us
    all_to_all x1, waiting for transfers between devices, per_device(): merged = swap(results[n_in])  7.83 us
    ppermute x2, starting transfers between devices, spread(): lax.ppermute(terms, axis, [(i, i ^ slot) for i in range(size)])  7.03 us
    pallas_call x2, Pallas kernels, packed(): pl.pallas_call(functools.partial(pack_blocks, sizes, capacity, slots), ou...  4.11 us
    all_to_all x1, starting transfers between devices, per_device(): grads = swap(grad_blocks)  3.94 us
    all_to_all x1, starting transfers between devices, per_device(): merged = swap(results[n_in])  3.73 us
    pallas_call x1, Pallas kernels, per_device(): pl.pallas_call(functools.partial(front_kernel, sizes, capacity), out_shap...  3.46 us
  transfers between devices with their start and end apart: 10, of which 3 were waited for; matrix products, arithmetic and copies ran while one was open for 2% of the time, Pallas kernels for 18%

profile of v5, /device:TPU:0, one launch (start us, length us, event | category | flops | bytes accessed | tf_op | source)
XLA Modules:
  0.0 60.7 jit_solution(12787655089124499489)
XLA Ops:
  0.6 1.8 %pack_blocks.1 = (bf16[1,2,32,1280]{3,2,1,0:T(8,128)(2,1)S(1)}, bf16[1,2,32,1280]{3,2,1,0:T(8,128)(2,1)S(1)}, bf16[1,2,32,1280]{3,2,1,0:T(8,128)(2,1)S(1)}) custom-call(s32[4]{0:T(128)} %bitcast.14, bf16[8,32,1280]{2,1,0:T(8,128)(2,1)} %bitcast.11), custom_call_target="tpu_custom_call" | custom-call | tf_op jit(solution)/shard_map/pack_blocks/pallas_call | solution.py:383
  2.5 3.1 %collective-permute-start = (bf16[1,2,32,1280]{3,2,1,0:T(8,128)(2,1)S(1)}, bf16[1,2,32,1280]{3,2,1,0:T(8,128)(2,1)S(1)}, u32[]{:S(2)}, u32[]{:S(2)}) collective-permute-start(bf16[1,2,32,1280]{3,2,1,0:T(8,128)(2,1)S(1)} %get-tuple-element.22), channel_id=1, source_target_pairs={{0,8},{8,0},{16,24},{24,16},{1,9},{9,1},{17,25},{25,17},{2,10},{10... | collective-permute-start | bytes 491528 | tf_op jit(solution)/shard_map/ppermute | solution.py:52
  5.5 2.6 %collective-permute-start.1 = (bf16[1,2,32,1280]{3,2,1,0:T(8,128)(2,1)S(1)}, bf16[1,2,32,1280]{3,2,1,0:T(8,128)(2,1)S(1)}, u32[]{:S(2)}, u32[]{:S(2)}) collective-permute-start(bf16[1,2,32,1280]{3,2,1,0:T(8,128)(2,1)S(1)} %get-tuple-element.23), channel_id=1, source_target_pairs={{0,16},{8,24},{16,0},{24,8},{1,17},{9,25},{17,1},{25,9},{2,18},{10... | collective-permute-start | bytes 491528 | tf_op jit(solution)/shard_map/ppermute | solution.py:52
  8.1 0.0 collective-permute-start.2
  8.1 3.9 %all-to-all-start = ((bf16[8,8,5120]{2,1,0:T(8,128)(2,1)}), bf16[8,8,5120]{2,1,0:T(8,128)(2,1)S(1)}, u32[]{:S(2)}, u32[]{:S(2)}) async-start(bf16[8,8,5120]{2,1,0:T(8,128)(2,1)} %bitcast.13), calls=%async_computation | async-start | bytes 1310720 | tf_op jit(solution)/shard_map/all_to_all | solution.py:403
  12.1 2.3 %pack_own.1.refs_4_ = bf16[1,2,32,1280]{3,2,1,0:T(8,128)(2,1)} custom-call(s32[4]{0:T(128)} %bitcast.15, bf16[8,32,1280]{2,1,0:T(8,128)(2,1)} %bitcast.12), custom_call_target="tpu_custom_call" | custom-call | tf_op jit(solution)/shard_map/pack_own/pallas_call | solution.py:383
  14.4 3.2 %hold.1.refs_3_ = bf16[2880,1280]{1,0:T(8,128)(2,1)S(1)} custom-call(bf16[2880,1280]{1,0:T(8,128)(2,1)} %bitcast.9), custom_call_target="tpu_custom_call" | custom-call | flops 100000000 | bytes 1000000 | tf_op jit(solution)/shard_map/hold/pallas_call | solution.py:405
  17.6 0.0 collective-permute-done.refs_5_
  17.6 3.0 %collective-permute-done.1.refs_6_ = bf16[1,2,32,1280]{3,2,1,0:T(8,128)(2,1)S(1)} collective-permute-done((bf16[1,2,32,1280]{3,2,1,0:T(8,128)(2,1)S(1)}, bf16[1,2,32,1280]{3,2,1,0:T(8,128)(2,1)S(1)}, u32[]{:S(2)}, u32[]{:S(2)}) %collective-permute-start.1) | collective-permute-done | bytes 163872 | tf_op jit(solution)/shard_map/ppermute | solution.py:52
  20.6 0.0 collective-permute-done.2.refs_7_
  20.6 3.5 %front.1 = (bf16[128,1280]{1,0:T(8,128)(2,1)S(1)}, f32[128,1280]{1,0:T(8,128)S(1)}, f32[128,128]{1,0:T(8,128)S(1)}, bf16[128,1024]{1,0:T(8,128)(2,1)S(1)}, bf16[...) custom-call(s32[4]{0:T(128)} %bitcast.16, f32[1280]{0:T(1024)} %refs_3_.1, f32[1280]{0:T(1024)} %refs_2_.1, ...), custom_call_target="tpu_custom_call" | custom-call | flops 12000000000 | bytes 8000000 | tf_op jit(solution)/shard_map/front/pallas_call | solution.py:417
  24.1 0.0 all-to-all-done.refs_14_
  24.1 8.3 %block.1 = (bf16[1,2,32,1280]{3,2,1,0:T(8,128)(2,1)}, bf16[1,2,32,1280]{3,2,1,0:T(8,128)(2,1)S(1)}, bf16[1,2,32,1280]{3,2,1,0:T(8,128)(2,1)S(1)}, bf16[1,2,32,12...) custom-call(s32[4]{0:T(128)} %bitcast.17, s32[1,128]{1,0:T(1,128)} %bitcast.19, ...), custom_call_target="tpu_custom_call" | custom-call | flops 2000000000 | bytes 12000000 | tf_op jit(solution)/shard_map/block/pallas_call | solution.py:441
  32.4 3.7 %all-to-all-start.1 = ((bf16[8,8,6400]{2,1,0:T(8,128)(2,1)}), bf16[8,8,6400]{2,1,0:T(8,128)(2,1)S(1)}, u32[]{:S(2)}, u32[]{:S(2)}) async-start(bf16[8,8,6400]{2,1,0:T(8,128)(2,1)} %get-tuple-element.31), calls=%async_computation.1 | async-start | bytes 1638400 | tf_op jit(solution)/shard_map/all_to_all | solution.py:487
  36.1 2.6 %collective-permute-start.4 = (bf16[1,2,32,1280]{3,2,1,0:T(8,128)(2,1)S(1)}, bf16[1,2,32,1280]{3,2,1,0:T(8,128)(2,1)S(1)}, u32[]{:S(2)}, u32[]{:S(2)}) collective-permute-start(bf16[1,2,32,1280]{3,2,1,0:T(8,128)(2,1)S(1)} %get-tuple-element.33), channel_id=1, source_target_pairs={{0,8},{8,0},{16,24},{24,16},{1,9},{9,1},{17,25},{25,17},{2,10},{10... | collective-permute-start | bytes 491528 | tf_op jit(solution)/shard_map/ppermute | solution.py:52
  38.8 1.1 %collective-permute-start.5 = (bf16[1,2,32,1280]{3,2,1,0:T(8,128)(2,1)S(1)}, bf16[1,2,32,1280]{3,2,1,0:T(8,128)(2,1)S(1)}, u32[]{:S(2)}, u32[]{:S(2)}) collective-permute-start(bf16[1,2,32,1280]{3,2,1,0:T(8,128)(2,1)S(1)} %get-tuple-element.34), channel_id=1, source_target_pairs={{0,16},{8,24},{16,0},{24,8},{1,17},{9,25},{17,1},{25,9},{2,18},{10... | collective-permute-start | bytes 491528 | tf_op jit(solution)/shard_map/ppermute | solution.py:52
  39.9 1.4 %collective-permute-start.6 = (bf16[1,2,32,1280]{3,2,1,0:T(8,128)(2,1)S(1)}, bf16[1,2,32,1280]{3,2,1,0:T(8,128)(2,1)S(1)}, u32[]{:S(2)}, u32[]{:S(2)}) collective-permute-start(bf16[1,2,32,1280]{3,2,1,0:T(8,128)(2,1)S(1)} %get-tuple-element.35), channel_id=1, source_target_pairs={{0,24},{8,16},{16,8},{24,0},{1,25},{9,17},{17,9},{25,1},{2,26},{10... | collective-permute-start | bytes 491528 | tf_op jit(solution)/shard_map/ppermute | solution.py:52
  41.2 7.8 %all-to-all-done.1 = bf16[8,8,6400]{2,1,0:T(8,128)(2,1)S(1)} async-done(((bf16[8,8,6400]{2,1,0:T(8,128)(2,1)}), bf16[8,8,6400]{2,1,0:T(8,128)(2,1)S(1)}, u32[]{:S(2)}, u32[]{:S(2)}) %all-to-all-start.1) | async-done | bytes 819232 | tf_op jit(solution)/shard_map/all_to_all | solution.py:487
  49.1 0.1 fusion
  49.2 2.7 %collective-permute-start.3 = (f32[4,1280]{1,0:T(4,128)S(1)}, f32[4,1280]{1,0:T(4,128)S(1)}, u32[]{:S(2)}, u32[]{:S(2)}) collective-permute-start(f32[4,1280]{1,0:T(4,128)S(1)} %fusion), channel_id=1, source_target_pairs={{0,8},{8,0},{16,24},{24,16},{1,9},{9,1},{17,25},{25,17},{2,10},{10... | collective-permute-start | bytes 61448 | tf_op jit(solution)/shard_map/ppermute | solution.py:60
  51.9 0.9 %slice_bitcast_fusion = bf16[64,5120]{1,0:T(8,128)(2,1)} fusion(bf16[8,8,6400]{2,1,0:T(8,128)(2,1)S(1)} %all-to-all-done.1), kind=kLoop, calls=%fused_computation | loop fusion | bytes 1310720 | tf_op jit(solution)/shard_map/reshape | solution.py:510
  52.8 1.1 %collective-permute-done.3 = f32[4,1280]{1,0:T(4,128)S(1)} collective-permute-done((f32[4,1280]{1,0:T(4,128)S(1)}, f32[4,1280]{1,0:T(4,128)S(1)}, u32[]{:S(2)}, u32[]{:S(2)}) %collective-permute-start.3) | collective-permute-done | bytes 20512 | tf_op jit(solution)/shard_map/ppermute | solution.py:60
  53.8 0.0 collective-permute-done.4.refs_2_
  53.8 0.0 collective-permute-done.5.refs_3_
  53.9 0.0 collective-permute-done.6.refs_4_
  53.9 4.3 %collective-permute-start.7 = (f32[4,1280]{1,0:T(4,128)S(1)}, f32[4,1280]{1,0:T(4,128)S(1)}, u32[]{:S(2)}, u32[]{:S(2)}) collective-permute-start(f32[4,1280]{1,0:T(4,128)S(1)} %add.10), channel_id=1, source_target_pairs={{0,16},{8,24},{16,0},{24,8},{1,17},{9,25},{17,1},{25,9},{2,18},{10... | collective-permute-start | bytes 61448 | tf_op jit(solution)/shard_map/ppermute | solution.py:60
  58.2 1.9 %unpack.1 = bf16[8,32,1280]{2,1,0:T(8,128)(2,1)} custom-call(s32[4]{0:T(128)} %bitcast.18, bf16[1,2,32,1280]{3,2,1,0:T(8,128)(2,1)} %get-tuple-element.36.refs_1_, bf16[1,2,32,1280]{3,2,1,0:T(8,128)(2,1)S(1)} %collective-permute-done.4.refs_2_, bf16[1,2,32,1280]{3,2,1,0:T(8,128)(2,1)S(1)} %collective-permute-done.5.refs_3_, ...), custom_call_target="tpu_custom_call" | custom-call | flops 10000000000 | bytes 1000000 | tf_op jit(solution)/shard_map/unpack/pallas_call | solution.py:498
  60.1 0.0 collective-permute-done.7
  60.1 0.6 %add.11 = f32[4,1280]{1,0:T(4,128)} add(f32[4,1280]{1,0:T(4,128)S(1)} %add.10, f32[4,1280]{1,0:T(4,128)S(1)} %collective-permute-done.7) | non-fusion elementwise | flops 5120 | bytes 61440 | tf_op jit(solution)/shard_map/add | solution.py:63
  (2 shorter events, 0.0 us)
Async XLA Ops:
  2.5 15.1 %collective-permute-start = (bf16[1,2,32,1280]{3,2,1,0:T(8,128)(2,1)S(1)}, bf16[1,2,32,1280]{3,2,1,0:T(8,128)(2,1)S(1)}, u32[]{:S(2)}, u32[]{:S(2)}) collective-permute-start(bf16[1,2,32,1280]{3,2,1,0:T(8,128)(2,1)S(1)} %get-tuple-element.22), channel_id=1, source_target_pairs={{0,8},{8,0},{16,24},{24,16},{1,9},{9,1},{17,25},{25,17},{2,10},{10... | collective-permute-start | bytes 491528 | tf_op jit(solution)/shard_map/ppermute | solution.py:52
  5.5 15.0 %collective-permute-start.1 = (bf16[1,2,32,1280]{3,2,1,0:T(8,128)(2,1)S(1)}, bf16[1,2,32,1280]{3,2,1,0:T(8,128)(2,1)S(1)}, u32[]{:S(2)}, u32[]{:S(2)}) collective-permute-start(bf16[1,2,32,1280]{3,2,1,0:T(8,128)(2,1)S(1)} %get-tuple-element.23), channel_id=1, source_target_pairs={{0,16},{8,24},{16,0},{24,8},{1,17},{9,25},{17,1},{25,9},{2,18},{10... | collective-permute-start | bytes 491528 | tf_op jit(solution)/shard_map/ppermute | solution.py:52
  8.1 12.5 %collective-permute-start.2 = (bf16[1,2,32,1280]{3,2,1,0:T(8,128)(2,1)S(1)}, bf16[1,2,32,1280]{3,2,1,0:T(8,128)(2,1)S(1)}, u32[]{:S(2)}, u32[]{:S(2)}) collective-permute-start(bf16[1,2,32,1280]{3,2,1,0:T(8,128)(2,1)S(1)} %get-tuple-element.24), channel_id=1, source_target_pairs={{0,24},{8,16},{16,8},{24,0},{1,25},{9,17},{17,9},{25,1},{2,26},{10... | collective-permute-start | bytes 491528 | tf_op jit(solution)/shard_map/ppermute | solution.py:52
  8.1 15.9 %all-to-all-start = ((bf16[8,8,5120]{2,1,0:T(8,128)(2,1)}), bf16[8,8,5120]{2,1,0:T(8,128)(2,1)S(1)}, u32[]{:S(2)}, u32[]{:S(2)}) async-start(bf16[8,8,5120]{2,1,0:T(8,128)(2,1)} %bitcast.13), calls=%async_computation | async-start | bytes 1310720 | tf_op jit(solution)/shard_map/all_to_all | solution.py:403
  32.4 16.7 %all-to-all-start.1 = ((bf16[8,8,6400]{2,1,0:T(8,128)(2,1)}), bf16[8,8,6400]{2,1,0:T(8,128)(2,1)S(1)}, u32[]{:S(2)}, u32[]{:S(2)}) async-start(bf16[8,8,6400]{2,1,0:T(8,128)(2,1)} %get-tuple-element.31), calls=%async_computation.1 | async-start | bytes 1638400 | tf_op jit(solution)/shard_map/all_to_all | solution.py:487
  36.1 17.7 %collective-permute-start.4 = (bf16[1,2,32,1280]{3,2,1,0:T(8,128)(2,1)S(1)}, bf16[1,2,32,1280]{3,2,1,0:T(8,128)(2,1)S(1)}, u32[]{:S(2)}, u32[]{:S(2)}) collective-permute-start(bf16[1,2,32,1280]{3,2,1,0:T(8,128)(2,1)S(1)} %get-tuple-element.33), channel_id=1, source_target_pairs={{0,8},{8,0},{16,24},{24,16},{1,9},{9,1},{17,25},{25,17},{2,10},{10... | collective-permute-start | bytes 491528 | tf_op jit(solution)/shard_map/ppermute | solution.py:52
  38.8 15.1 %collective-permute-start.5 = (bf16[1,2,32,1280]{3,2,1,0:T(8,128)(2,1)S(1)}, bf16[1,2,32,1280]{3,2,1,0:T(8,128)(2,1)S(1)}, u32[]{:S(2)}, u32[]{:S(2)}) collective-permute-start(bf16[1,2,32,1280]{3,2,1,0:T(8,128)(2,1)S(1)} %get-tuple-element.34), channel_id=1, source_target_pairs={{0,16},{8,24},{16,0},{24,8},{1,17},{9,25},{17,1},{25,9},{2,18},{10... | collective-permute-start | bytes 491528 | tf_op jit(solution)/shard_map/ppermute | solution.py:52
  39.9 14.0 %collective-permute-start.6 = (bf16[1,2,32,1280]{3,2,1,0:T(8,128)(2,1)S(1)}, bf16[1,2,32,1280]{3,2,1,0:T(8,128)(2,1)S(1)}, u32[]{:S(2)}, u32[]{:S(2)}) collective-permute-start(bf16[1,2,32,1280]{3,2,1,0:T(8,128)(2,1)S(1)} %get-tuple-element.35), channel_id=1, source_target_pairs={{0,24},{8,16},{16,8},{24,0},{1,25},{9,17},{17,9},{25,1},{2,26},{10... | collective-permute-start | bytes 491528 | tf_op jit(solution)/shard_map/ppermute | solution.py:52
  49.2 4.7 %collective-permute-start.3 = (f32[4,1280]{1,0:T(4,128)S(1)}, f32[4,1280]{1,0:T(4,128)S(1)}, u32[]{:S(2)}, u32[]{:S(2)}) collective-permute-start(f32[4,1280]{1,0:T(4,128)S(1)} %fusion), channel_id=1, source_target_pairs={{0,8},{8,0},{16,24},{24,16},{1,9},{9,1},{17,25},{25,17},{2,10},{10... | collective-permute-start | bytes 61448 | tf_op jit(solution)/shard_map/ppermute | solution.py:60
  53.9 6.2 %collective-permute-start.7 = (f32[4,1280]{1,0:T(4,128)S(1)}, f32[4,1280]{1,0:T(4,128)S(1)}, u32[]{:S(2)}, u32[]{:S(2)}) collective-permute-start(f32[4,1280]{1,0:T(4,128)S(1)} %add.10), channel_id=1, source_target_pairs={{0,16},{8,24},{16,0},{24,8},{1,17},{9,25},{17,1},{25,9},{2,18},{10... | collective-permute-start | bytes 61448 | tf_op jit(solution)/shard_map/ppermute | solution.py:60

commit v6 on v5

--- a/solution.py
+++ b/solution.py
@@ -441,7 +441,7 @@
     results = pl.pallas_call(
         functools.partial(block_kernel, sizes, capacity),
         out_shape=[
-            *block_shapes,
+            *(jax.ShapeDtypeStruct(shape.shape, BF16) for shape in block_shapes),
             window_shape,
             jax.ShapeDtypeStruct((4, width), F32),
         ],
@@ -505,7 +505,7 @@
             flops=UNPACK_FLOPS, bytes_accessed=10**6, transcendentals=0
         ),
         name="unpack",
-    )(in_hbm(counts), in_hbm(came_back[0]), *came_back[1:])
+    )(in_hbm(counts), *came_back)
     return (
         merged.reshape(owner_slots, token_width),
         patch_grad.reshape(source_units * UNIT, width),

time: 61.1 us -> 61 us (level)
  transfers between devices with their start and end apart: 10 -> 10, of which waited for: 3 -> 4; matrix products, arithmetic and copies ran while one was open for 2% -> 2% of each run, Pallas kernels for 18% -> 17%
where the time goes in v6:
time: 61 us; the launch traced here: 60.5 us
  starting transfers between devices  25.5 us (42%)
  Pallas kernels  20.7 us (34%)
  waiting for transfers between devices  12.1 us (20%)
  local copies, waits for them, and re-layouts  0.88 us (1%)
  between operations  0.72 us (1%)
  other arithmetic  0.71 us (1%)
    ppermute x6, starting transfers between devices, exchange(): lax.ppermute(arrays[slot], axis, [(i, i ^ slot) for i in range(size)])  10.8 us
    pallas_call x1, Pallas kernels, per_device(): pl.pallas_call(functools.partial(block_kernel, sizes, capacity), out_shap...  8.28 us
    all_to_all x1, waiting for transfers between devices, per_device(): merged = swap(results[n_in])  7.83 us
    ppermute x2, starting transfers between devices, spread(): lax.ppermute(terms, axis, [(i, i ^ slot) for i in range(size)])  7.03 us
    pallas_call x2, Pallas kernels, packed(): pl.pallas_call(functools.partial(pack_blocks, sizes, capacity, slots), ou...  4.11 us
    all_to_all x1, starting transfers between devices, per_device(): grads = swap(grad_blocks)  3.94 us
    all_to_all x1, starting transfers between devices, per_device(): merged = swap(results[n_in])  3.73 us
    pallas_call x1, Pallas kernels, per_device(): pl.pallas_call(functools.partial(front_kernel, sizes, capacity), out_shap...  3.46 us
  transfers between devices with their start and end apart: 10, of which 4 were waited for; matrix products, arithmetic and copies ran while one was open for 2% of the time, Pallas kernels for 17%

profile of v6, /device:TPU:0, one launch (start us, length us, event | category | flops | bytes accessed | tf_op | source)
XLA Modules:
  0.0 60.5 jit_solution(2313063800179171745)
XLA Ops:
  0.6 1.8 %pack_blocks.1 = (bf16[1,2,32,1280]{3,2,1,0:T(8,128)(2,1)S(1)}, bf16[1,2,32,1280]{3,2,1,0:T(8,128)(2,1)S(1)}, bf16[1,2,32,1280]{3,2,1,0:T(8,128)(2,1)S(1)}) custom-call(s32[4]{0:T(128)} %bitcast.14, bf16[8,32,1280]{2,1,0:T(8,128)(2,1)} %bitcast.11), custom_call_target="tpu_custom_call" | custom-call | tf_op jit(solution)/shard_map/pack_blocks/pallas_call | solution.py:383
  2.5 3.1 %collective-permute-start = (bf16[1,2,32,1280]{3,2,1,0:T(8,128)(2,1)S(1)}, bf16[1,2,32,1280]{3,2,1,0:T(8,128)(2,1)S(1)}, u32[]{:S(2)}, u32[]{:S(2)}) collective-permute-start(bf16[1,2,32,1280]{3,2,1,0:T(8,128)(2,1)S(1)} %get-tuple-element.22), channel_id=1, source_target_pairs={{0,8},{8,0},{16,24},{24,16},{1,9},{9,1},{17,25},{25,17},{2,10},{10... | collective-permute-start | bytes 491528 | tf_op jit(solution)/shard_map/ppermute | solution.py:52
  5.5 2.6 %collective-permute-start.1 = (bf16[1,2,32,1280]{3,2,1,0:T(8,128)(2,1)S(1)}, bf16[1,2,32,1280]{3,2,1,0:T(8,128)(2,1)S(1)}, u32[]{:S(2)}, u32[]{:S(2)}) collective-permute-start(bf16[1,2,32,1280]{3,2,1,0:T(8,128)(2,1)S(1)} %get-tuple-element.23), channel_id=1, source_target_pairs={{0,16},{8,24},{16,0},{24,8},{1,17},{9,25},{17,1},{25,9},{2,18},{10... | collective-permute-start | bytes 491528 | tf_op jit(solution)/shard_map/ppermute | solution.py:52
  8.1 0.0 collective-permute-start.2
  8.1 3.9 %all-to-all-start = ((bf16[8,8,5120]{2,1,0:T(8,128)(2,1)}), bf16[8,8,5120]{2,1,0:T(8,128)(2,1)S(1)}, u32[]{:S(2)}, u32[]{:S(2)}) async-start(bf16[8,8,5120]{2,1,0:T(8,128)(2,1)} %bitcast.13), calls=%async_computation | async-start | bytes 1310720 | tf_op jit(solution)/shard_map/all_to_all | solution.py:403
  12.1 2.3 %pack_own.1.refs_4_ = bf16[1,2,32,1280]{3,2,1,0:T(8,128)(2,1)} custom-call(s32[4]{0:T(128)} %bitcast.15, bf16[8,32,1280]{2,1,0:T(8,128)(2,1)} %bitcast.12), custom_call_target="tpu_custom_call" | custom-call | tf_op jit(solution)/shard_map/pack_own/pallas_call | solution.py:383
  14.4 3.2 %hold.1.refs_3_ = bf16[2880,1280]{1,0:T(8,128)(2,1)S(1)} custom-call(bf16[2880,1280]{1,0:T(8,128)(2,1)} %bitcast.9), custom_call_target="tpu_custom_call" | custom-call | flops 100000000 | bytes 1000000 | tf_op jit(solution)/shard_map/hold/pallas_call | solution.py:405
  17.6 0.0 collective-permute-done.refs_5_
  17.6 3.0 %collective-permute-done.1.refs_6_ = bf16[1,2,32,1280]{3,2,1,0:T(8,128)(2,1)S(1)} collective-permute-done((bf16[1,2,32,1280]{3,2,1,0:T(8,128)(2,1)S(1)}, bf16[1,2,32,1280]{3,2,1,0:T(8,128)(2,1)S(1)}, u32[]{:S(2)}, u32[]{:S(2)}) %collective-permute-start.1) | collective-permute-done | bytes 163872 | tf_op jit(solution)/shard_map/ppermute | solution.py:52
  20.6 0.0 collective-permute-done.2.refs_7_
  20.6 3.5 %front.1 = (bf16[128,1280]{1,0:T(8,128)(2,1)S(1)}, f32[128,1280]{1,0:T(8,128)S(1)}, f32[128,128]{1,0:T(8,128)S(1)}, bf16[128,1024]{1,0:T(8,128)(2,1)S(1)}, bf16[...) custom-call(s32[4]{0:T(128)} %bitcast.16, f32[1280]{0:T(1024)} %refs_3_.1, f32[1280]{0:T(1024)} %refs_2_.1, ...), custom_call_target="tpu_custom_call" | custom-call | flops 12000000000 | bytes 8000000 | tf_op jit(solution)/shard_map/front/pallas_call | solution.py:417
  24.1 0.0 all-to-all-done.refs_14_
  24.1 8.3 %block.1 = (bf16[1,2,32,1280]{3,2,1,0:T(8,128)(2,1)S(1)}, bf16[1,2,32,1280]{3,2,1,0:T(8,128)(2,1)S(1)}, bf16[1,2,32,1280]{3,2,1,0:T(8,128)(2,1)S(1)}, bf16[1,2,3...) custom-call(s32[4]{0:T(128)} %bitcast.17, s32[1,128]{1,0:T(1,128)} %bitcast.19, ...), custom_call_target="tpu_custom_call" | custom-call | flops 2000000000 | bytes 12000000 | tf_op jit(solution)/shard_map/block/pallas_call | solution.py:441
  32.4 3.7 %all-to-all-start.1 = ((bf16[8,8,6400]{2,1,0:T(8,128)(2,1)}), bf16[8,8,6400]{2,1,0:T(8,128)(2,1)S(1)}, u32[]{:S(2)}, u32[]{:S(2)}) async-start(bf16[8,8,6400]{2,1,0:T(8,128)(2,1)} %get-tuple-element.31), calls=%async_computation.1 | async-start | bytes 1638400 | tf_op jit(solution)/shard_map/all_to_all | solution.py:487
  36.1 2.6 %collective-permute-start.4 = (bf16[1,2,32,1280]{3,2,1,0:T(8,128)(2,1)S(1)}, bf16[1,2,32,1280]{3,2,1,0:T(8,128)(2,1)S(1)}, u32[]{:S(2)}, u32[]{:S(2)}) collective-permute-start(bf16[1,2,32,1280]{3,2,1,0:T(8,128)(2,1)S(1)} %get-tuple-element.33), channel_id=1, source_target_pairs={{0,8},{8,0},{16,24},{24,16},{1,9},{9,1},{17,25},{25,17},{2,10},{10... | collective-permute-start | bytes 491528 | tf_op jit(solution)/shard_map/ppermute | solution.py:52
  38.7 1.1 %collective-permute-start.5 = (bf16[1,2,32,1280]{3,2,1,0:T(8,128)(2,1)S(1)}, bf16[1,2,32,1280]{3,2,1,0:T(8,128)(2,1)S(1)}, u32[]{:S(2)}, u32[]{:S(2)}) collective-permute-start(bf16[1,2,32,1280]{3,2,1,0:T(8,128)(2,1)S(1)} %get-tuple-element.34), channel_id=1, source_target_pairs={{0,16},{8,24},{16,0},{24,8},{1,17},{9,25},{17,1},{25,9},{2,18},{10... | collective-permute-start | bytes 491528 | tf_op jit(solution)/shard_map/ppermute | solution.py:52
  39.8 1.4 %collective-permute-start.6 = (bf16[1,2,32,1280]{3,2,1,0:T(8,128)(2,1)S(1)}, bf16[1,2,32,1280]{3,2,1,0:T(8,128)(2,1)S(1)}, u32[]{:S(2)}, u32[]{:S(2)}) collective-permute-start(bf16[1,2,32,1280]{3,2,1,0:T(8,128)(2,1)S(1)} %get-tuple-element.35), channel_id=1, source_target_pairs={{0,24},{8,16},{16,8},{24,0},{1,25},{9,17},{17,9},{25,1},{2,26},{10... | collective-permute-start | bytes 491528 | tf_op jit(solution)/shard_map/ppermute | solution.py:52
  41.2 7.8 %all-to-all-done.1 = bf16[8,8,6400]{2,1,0:T(8,128)(2,1)S(1)} async-done(((bf16[8,8,6400]{2,1,0:T(8,128)(2,1)}), bf16[8,8,6400]{2,1,0:T(8,128)(2,1)S(1)}, u32[]{:S(2)}, u32[]{:S(2)}) %all-to-all-start.1) | async-done | bytes 819232 | tf_op jit(solution)/shard_map/all_to_all | solution.py:487
  49.1 0.1 fusion
  49.1 2.7 %collective-permute-start.3 = (f32[4,1280]{1,0:T(4,128)S(1)}, f32[4,1280]{1,0:T(4,128)S(1)}, u32[]{:S(2)}, u32[]{:S(2)}) collective-permute-start(f32[4,1280]{1,0:T(4,128)S(1)} %fusion), channel_id=1, source_target_pairs={{0,8},{8,0},{16,24},{24,16},{1,9},{9,1},{17,25},{25,17},{2,10},{10... | collective-permute-start | bytes 61448 | tf_op jit(solution)/shard_map/ppermute | solution.py:60
  51.9 0.9 %slice_bitcast_fusion = bf16[64,5120]{1,0:T(8,128)(2,1)} fusion(bf16[8,8,6400]{2,1,0:T(8,128)(2,1)S(1)} %all-to-all-done.1), kind=kLoop, calls=%fused_computation | loop fusion | bytes 1310720 | tf_op jit(solution)/shard_map/reshape | solution.py:510
  52.7 1.1 %collective-permute-done.3 = f32[4,1280]{1,0:T(4,128)S(1)} collective-permute-done((f32[4,1280]{1,0:T(4,128)S(1)}, f32[4,1280]{1,0:T(4,128)S(1)}, u32[]{:S(2)}, u32[]{:S(2)}) %collective-permute-start.3) | collective-permute-done | bytes 20512 | tf_op jit(solution)/shard_map/ppermute | solution.py:60
  53.8 0.0 collective-permute-done.4.refs_2_
  53.8 0.0 collective-permute-done.5.refs_3_
  53.8 0.0 collective-permute-done.6.refs_4_
  53.8 4.3 %collective-permute-start.7 = (f32[4,1280]{1,0:T(4,128)S(1)}, f32[4,1280]{1,0:T(4,128)S(1)}, u32[]{:S(2)}, u32[]{:S(2)}) collective-permute-start(f32[4,1280]{1,0:T(4,128)S(1)} %add.10), channel_id=1, source_target_pairs={{0,16},{8,24},{16,0},{24,8},{1,17},{9,25},{17,1},{25,9},{2,18},{10... | collective-permute-start | bytes 61448 | tf_op jit(solution)/shard_map/ppermute | solution.py:60
  58.2 1.6 %unpack.1 = bf16[8,32,1280]{2,1,0:T(8,128)(2,1)} custom-call(s32[4]{0:T(128)} %bitcast.18, bf16[1,2,32,1280]{3,2,1,0:T(8,128)(2,1)S(1)} %get-tuple-element.36.refs_1_, bf16[1,2,32,1280]{3,2,1,0:T(8,128)(2,1)S(1)} %collective-permute-done.4.refs_2_, bf16[1,2,32,1280]{3,2,1,0:T(8,128)(2,1)S(1)} %collective-permute-done.5.refs_3_, ...), custom_call_target="tpu_custom_call" | custom-call | flops 10000000000 | bytes 1000000 | tf_op jit(solution)/shard_map/unpack/pallas_call | solution.py:498
  59.8 0.1 collective-permute-done.7
  59.9 0.6 %add.11 = f32[4,1280]{1,0:T(4,128)} add(f32[4,1280]{1,0:T(4,128)S(1)} %add.10, f32[4,1280]{1,0:T(4,128)S(1)} %collective-permute-done.7) | non-fusion elementwise | flops 5120 | bytes 61440 | tf_op jit(solution)/shard_map/add | solution.py:63
  (2 shorter events, 0.0 us)
Async XLA Ops:
  2.5 15.1 %collective-permute-start = (bf16[1,2,32,1280]{3,2,1,0:T(8,128)(2,1)S(1)}, bf16[1,2,32,1280]{3,2,1,0:T(8,128)(2,1)S(1)}, u32[]{:S(2)}, u32[]{:S(2)}) collective-permute-start(bf16[1,2,32,1280]{3,2,1,0:T(8,128)(2,1)S(1)} %get-tuple-element.22), channel_id=1, source_target_pairs={{0,8},{8,0},{16,24},{24,16},{1,9},{9,1},{17,25},{25,17},{2,10},{10... | collective-permute-start | bytes 491528 | tf_op jit(solution)/shard_map/ppermute | solution.py:52
  5.5 15.0 %collective-permute-start.1 = (bf16[1,2,32,1280]{3,2,1,0:T(8,128)(2,1)S(1)}, bf16[1,2,32,1280]{3,2,1,0:T(8,128)(2,1)S(1)}, u32[]{:S(2)}, u32[]{:S(2)}) collective-permute-start(bf16[1,2,32,1280]{3,2,1,0:T(8,128)(2,1)S(1)} %get-tuple-element.23), channel_id=1, source_target_pairs={{0,16},{8,24},{16,0},{24,8},{1,17},{9,25},{17,1},{25,9},{2,18},{10... | collective-permute-start | bytes 491528 | tf_op jit(solution)/shard_map/ppermute | solution.py:52
  8.1 12.5 %collective-permute-start.2 = (bf16[1,2,32,1280]{3,2,1,0:T(8,128)(2,1)S(1)}, bf16[1,2,32,1280]{3,2,1,0:T(8,128)(2,1)S(1)}, u32[]{:S(2)}, u32[]{:S(2)}) collective-permute-start(bf16[1,2,32,1280]{3,2,1,0:T(8,128)(2,1)S(1)} %get-tuple-element.24), channel_id=1, source_target_pairs={{0,24},{8,16},{16,8},{24,0},{1,25},{9,17},{17,9},{25,1},{2,26},{10... | collective-permute-start | bytes 491528 | tf_op jit(solution)/shard_map/ppermute | solution.py:52
  8.1 15.9 %all-to-all-start = ((bf16[8,8,5120]{2,1,0:T(8,128)(2,1)}), bf16[8,8,5120]{2,1,0:T(8,128)(2,1)S(1)}, u32[]{:S(2)}, u32[]{:S(2)}) async-start(bf16[8,8,5120]{2,1,0:T(8,128)(2,1)} %bitcast.13), calls=%async_computation | async-start | bytes 1310720 | tf_op jit(solution)/shard_map/all_to_all | solution.py:403
  32.4 16.7 %all-to-all-start.1 = ((bf16[8,8,6400]{2,1,0:T(8,128)(2,1)}), bf16[8,8,6400]{2,1,0:T(8,128)(2,1)S(1)}, u32[]{:S(2)}, u32[]{:S(2)}) async-start(bf16[8,8,6400]{2,1,0:T(8,128)(2,1)} %get-tuple-element.31), calls=%async_computation.1 | async-start | bytes 1638400 | tf_op jit(solution)/shard_map/all_to_all | solution.py:487
  36.1 17.7 %collective-permute-start.4 = (bf16[1,2,32,1280]{3,2,1,0:T(8,128)(2,1)S(1)}, bf16[1,2,32,1280]{3,2,1,0:T(8,128)(2,1)S(1)}, u32[]{:S(2)}, u32[]{:S(2)}) collective-permute-start(bf16[1,2,32,1280]{3,2,1,0:T(8,128)(2,1)S(1)} %get-tuple-element.33), channel_id=1, source_target_pairs={{0,8},{8,0},{16,24},{24,16},{1,9},{9,1},{17,25},{25,17},{2,10},{10... | collective-permute-start | bytes 491528 | tf_op jit(solution)/shard_map/ppermute | solution.py:52
  38.7 15.1 %collective-permute-start.5 = (bf16[1,2,32,1280]{3,2,1,0:T(8,128)(2,1)S(1)}, bf16[1,2,32,1280]{3,2,1,0:T(8,128)(2,1)S(1)}, u32[]{:S(2)}, u32[]{:S(2)}) collective-permute-start(bf16[1,2,32,1280]{3,2,1,0:T(8,128)(2,1)S(1)} %get-tuple-element.34), channel_id=1, source_target_pairs={{0,16},{8,24},{16,0},{24,8},{1,17},{9,25},{17,1},{25,9},{2,18},{10... | collective-permute-start | bytes 491528 | tf_op jit(solution)/shard_map/ppermute | solution.py:52
  39.8 14.0 %collective-permute-start.6 = (bf16[1,2,32,1280]{3,2,1,0:T(8,128)(2,1)S(1)}, bf16[1,2,32,1280]{3,2,1,0:T(8,128)(2,1)S(1)}, u32[]{:S(2)}, u32[]{:S(2)}) collective-permute-start(bf16[1,2,32,1280]{3,2,1,0:T(8,128)(2,1)S(1)} %get-tuple-element.35), channel_id=1, source_target_pairs={{0,24},{8,16},{16,8},{24,0},{1,25},{9,17},{17,9},{25,1},{2,26},{10... | collective-permute-start | bytes 491528 | tf_op jit(solution)/shard_map/ppermute | solution.py:52
  49.1 4.7 %collective-permute-start.3 = (f32[4,1280]{1,0:T(4,128)S(1)}, f32[4,1280]{1,0:T(4,128)S(1)}, u32[]{:S(2)}, u32[]{:S(2)}) collective-permute-start(f32[4,1280]{1,0:T(4,128)S(1)} %fusion), channel_id=1, source_target_pairs={{0,8},{8,0},{16,24},{24,16},{1,9},{9,1},{17,25},{25,17},{2,10},{10... | collective-permute-start | bytes 61448 | tf_op jit(solution)/shard_map/ppermute | solution.py:60
  53.8 6.1 %collective-permute-start.7 = (f32[4,1280]{1,0:T(4,128)S(1)}, f32[4,1280]{1,0:T(4,128)S(1)}, u32[]{:S(2)}, u32[]{:S(2)}) collective-permute-start(f32[4,1280]{1,0:T(4,128)S(1)} %add.10), channel_id=1, source_target_pairs={{0,16},{8,24},{16,0},{24,8},{1,17},{9,25},{17,1},{25,9},{2,18},{10... | collective-permute-start | bytes 61448 | tf_op jit(solution)/shard_map/ppermute | solution.py:60
